TPU v7x, 32 devices: a whole 2x2x4 slice. The times are simulated.
32 devices in a mesh: gx: 4 (over y, core), gy: 8 (over z, x).
Axes of the slice: x: 2, y: 2, z: 4, core: 2. Of those that a mesh axis runs over, the one named last changes fastest.
Arguments:
- air_forcing_quantities: float32 [8, 65536], P(None, ('gx', 'gy')), may hold values from -6 to 6
- segment_sea_subdomain: int32 [8192, 1], P(('gx', 'gy')), may hold values from 0 to 31; in each aligned block of 256 rows (0 to 255, 256 to 511, ...) at most 16 rows name the same one
- overlay_air_element: int32 [8192, 128], P(('gx', 'gy')), may hold values from 0 to 2047
- overlay_sea_profile: int32 [8192, 128], P(('gx', 'gy')), may hold values from 0 to 16383
- overlay_fraction_share: float32 [8192, 128], P(('gx', 'gy')), may hold values from 0.02 to 0.5
- thermal_deviation: float32 [20, 256, 2048], P(None, 'gy', 'gx'), may hold values from -6 to 6
- saltiness_deviation: float32 [20, 256, 2048], P(None, 'gy', 'gx'), may hold values from -6 to 6
- zonal_interface_speed: float32 [20, 256, 2048], P(None, 'gy', 'gx'), may hold values from -0.3 to 0.3
- poleward_interface_speed: float32 [20, 256, 2048], P(None, 'gy', 'gx'), may hold values from -0.3 to 0.3
- sea_profile_indicator: int32 [256, 2048], P('gy', 'gx'), may hold values 0 or 1
Outputs:
- temperature_out: float32 [20, 256, 2048], P(None, 'gy', 'gx')
- salinity_out: float32 [20, 256, 2048], P(None, 'gy', 'gx')
- back_fields: float32 [4, 65536], P(None, ('gx', 'gy'))
Inputs may be any that keep to these rules, and one draw needn't show every extreme that they name: segment_sea_subdomain names a tile as longitude tile times the number of latitude tiles plus latitude tile. Among the rows of one device at most 16 blocks name the same tile, and some device sends exactly 16 to one tile. overlay_air_element index the atmosphere cells of the tile that holds the block. overlay_sea_profile index the destination tile's columns as latitude row times 512 plus longitude column.
All inputs are finite; a program needn't handle non-finite values. No bound on the sum of `sea_profile_indicator` on one device may be relied on, other than what follows from the above.
Results may differ from a plain program's by a relative error of at most 0.00002.
Values sent between devices are 32-bit elements; how exact they have to be, the bound alone decides.
A program may use at most 192 MiB of HBM per device.

v0:
```python
import jax
import jax.numpy as jnp
from jax import lax
from jax.sharding import PartitionSpec as P

diffuse_rate = 0.12
mixing_base = 0.02
mixing_extra = 0.2
heat_factor = 0.5
fresh_factor = 0.5
stress_factor = 0.3


def extended(cells, sides, width):
    for axis, dim in sides:
        count = lax.axis_size(axis)
        head = lax.slice_in_dim(cells, 0, width, axis=dim)
        tail = lax.slice_in_dim(cells, cells.shape[dim] - width, cells.shape[dim], axis=dim)
        cells = jnp.concatenate(
            [
                lax.ppermute(tail, axis, [(i, (i + 1) % count) for i in range(count)]),
                cells,
                lax.ppermute(head, axis, [((i + 1) % count, i) for i in range(count)]),
            ],
            axis=dim,
        )
    return cells


def from_partner(array, axis, distance):
    return lax.ppermute(array, axis, [(i, i ^ 1 << distance) for i in range(lax.axis_size(axis))])


def density(temper_field, saline_field):
    return (
        -0.2 * temper_field
        - 0.05 * temper_field * temper_field
        + 0.8 * saline_field
        + 0.03 * temper_field * saline_field
    )


def face_flux(near_cells, far_cells, velocity, open_faces):
    return open_faces * (
        velocity * 0.5 * (near_cells + far_cells) - diffuse_rate * (far_cells - near_cells)
    )


def vertical_change(scalar_quantities, ocean_mask):
    heavy = density(scalar_quantities[0], scalar_quantities[1])
    mixing = (
        mixing_base + mixing_extra * jax.nn.sigmoid(4.0 * (heavy[:-1] - heavy[1:]))
    ) * ocean_mask
    gradients = mixing[None] * (scalar_quantities[:, 1:] - scalar_quantities[:, :-1])
    nothing = jnp.zeros_like(gradients[:, :1])
    return jnp.concatenate([gradients, nothing], axis=1) - jnp.concatenate(
        [nothing, gradients], axis=1
    )


def static_bundle(east_eff, north_eff, ocean_mask):
    return jnp.concatenate([east_eff, north_eff, ocean_mask[None]], axis=0)


def ocean_step(scalar_quantities, east_eff, north_eff, ocean_mask, forcing):
    depth_levels = scalar_quantities.shape[1]
    parallel_lines = scalar_quantities.shape[2]
    meridian_lines = scalar_quantities.shape[3]
    flat_tracers = scalar_quantities.reshape(2 * depth_levels, parallel_lines, meridian_lines)
    bundle = jnp.concatenate([flat_tracers, static_bundle(east_eff, north_eff, ocean_mask)], axis=0)
    padded = extended(bundle, (("gx", 2), ("gy", 1)), 1)
    fold_part = jnp.concatenate([flat_tracers[:, -1, :], ocean_mask[-1:]], axis=0)
    for bit_number in range(lax.axis_size("gx").bit_length() - 1):
        fold_part = from_partner(fold_part, "gx", bit_number)
    fold_here = fold_part[:, ::-1]
    is_top = lax.axis_index("gy") == lax.axis_size("gy") - 1
    is_bottom = lax.axis_index("gy") == 0
    north_row = padded[:, -1, 1:-1]
    replacement = jnp.concatenate(
        [
            fold_here[: 2 * depth_levels],
            north_row[2 * depth_levels : 4 * depth_levels],
            fold_here[2 * depth_levels :],
        ],
        axis=0,
    )
    padded = padded.at[:, -1, 1:-1].set(jnp.where(is_top, replacement, north_row))
    padded = padded.at[-1, 0, :].set(jnp.where(is_bottom, 0.0, padded[-1, 0, :]))
    tracer_pad = padded[: 2 * depth_levels].reshape(
        2, depth_levels, parallel_lines + 2, meridian_lines + 2
    )
    east_pad = padded[2 * depth_levels : 3 * depth_levels]
    north_pad = padded[3 * depth_levels : 4 * depth_levels]
    mask_pad = padded[4 * depth_levels]
    east_open = mask_pad[1:-1, :-1] * mask_pad[1:-1, 1:]
    east_all = face_flux(
        tracer_pad[:, :, 1:-1, :-1], tracer_pad[:, :, 1:-1, 1:], east_pad[:, 1:-1, :-1], east_open
    )
    global_rows = (
        lax.axis_index("gy") * parallel_lines
        + lax.broadcasted_iota(jnp.int32, (parallel_lines + 1, 1), 0)
        - 1
    )
    active = (global_rows < lax.axis_size("gy") * parallel_lines - 1).astype(jnp.float32)
    north_open = mask_pad[:-1, 1:-1] * mask_pad[1:, 1:-1]
    north_all = face_flux(
        tracer_pad[:, :, :-1, 1:-1],
        tracer_pad[:, :, 1:, 1:-1],
        north_pad[:, :-1, 1:-1] * active,
        north_open,
    )
    change = -(east_all[..., 1:] - east_all[..., :-1]) - (
        north_all[:, :, 1:] - north_all[:, :, :-1]
    )
    change = change + vertical_change(scalar_quantities, ocean_mask)
    change = change.at[:, 0].add(forcing)
    return scalar_quantities + ocean_mask * change


def body(
    air_forcing_quantities,
    segment_sea_subdomain,
    overlay_air_element,
    overlay_sea_profile,
    overlay_fraction_share,
    thermal_deviation,
    saltiness_deviation,
    zonal_interface_speed,
    poleward_interface_speed,
    sea_profile_indicator,
):
    count_gx = lax.axis_size("gx")
    count_gy = lax.axis_size("gy")
    devices = count_gx * count_gy
    blocks = segment_sea_subdomain.shape[0]
    entries = overlay_air_element.shape[1]
    atm_cells = air_forcing_quantities.shape[1]
    parallel_lines = thermal_deviation.shape[1]
    meridian_lines = thermal_deviation.shape[2]
    capacity = max(2, 2 * blocks // devices)
    one_hot = (segment_sea_subdomain == jnp.arange(devices, dtype=jnp.int32)[None, :]).astype(
        jnp.int32
    )
    earlier = jnp.sum((jnp.cumsum(one_hot, axis=0) - one_hot) * one_hot, axis=1)
    position = segment_sea_subdomain[:, 0] * capacity + earlier
    field_count = air_forcing_quantities.shape[0]
    weighted = (
        jnp.take(air_forcing_quantities, overlay_air_element, axis=1) * overlay_fraction_share[None]
    )
    outgoing = (
        jnp.zeros((field_count, devices * capacity, entries), jnp.float32)
        .at[:, position]
        .set(weighted)
    )
    addresses = (
        jnp.zeros((1, devices * capacity, entries), jnp.int32)
        .at[:, position]
        .set(overlay_sea_profile[None])
    )
    arrived, places = (
        lax.all_to_all(outgoing, ("gx", "gy"), split_axis=1, concat_axis=1, tiled=True),
        lax.all_to_all(addresses, ("gx", "gy"), split_axis=1, concat_axis=1, tiled=True),
    )
    remapped = (
        jnp.zeros((field_count, parallel_lines * meridian_lines), jnp.float32)
        .at[:, places.reshape(-1)]
        .add(arrived.reshape(field_count, -1))
    )
    remapped = remapped.reshape(field_count, parallel_lines, meridian_lines)
    heat_flux = remapped[0] + remapped[1] + remapped[2] + remapped[3]
    fresh_flux = remapped[5] - remapped[4]
    zonal_stress = remapped[6]
    meridional = remapped[7]
    east_eff = zonal_interface_speed.at[0].add(stress_factor * zonal_stress)
    north_eff = poleward_interface_speed.at[0].add(stress_factor * meridional)
    ocean_mask = sea_profile_indicator.astype(jnp.float32)
    forcing = jnp.stack([heat_factor * heat_flux, fresh_factor * fresh_flux])
    scalar_quantities = jnp.stack([thermal_deviation, saltiness_deviation])
    for step_number in range(2):
        scalar_quantities = ocean_step(scalar_quantities, east_eff, north_eff, ocean_mask, forcing)
    surface = (
        jnp.stack(
            [
                scalar_quantities[0, 0],
                scalar_quantities[1, 0],
                density(scalar_quantities[0, 0], scalar_quantities[1, 0]),
                east_eff[0],
            ]
        )
        * ocean_mask
    )
    picked = jnp.take(surface.reshape(4, -1), places[0], axis=1)
    returned = lax.all_to_all(picked, ("gx", "gy"), split_axis=1, concat_axis=1, tiled=True)
    own_blocks = returned[:, position] * overlay_fraction_share[None]
    back_fields = (
        jnp.zeros((4, atm_cells), jnp.float32)
        .at[:, overlay_air_element.reshape(-1)]
        .add(own_blocks.reshape(4, -1))
    )
    return (scalar_quantities[0], scalar_quantities[1], back_fields)


def solution(mesh):
    return jax.shard_map(
        body,
        mesh=mesh,
        in_specs=(
            P(None, ("gx", "gy")),
            P(("gx", "gy"), None),
            P(("gx", "gy"), None),
            P(("gx", "gy"), None),
            P(("gx", "gy"), None),
            P(None, "gy", "gx"),
            P(None, "gy", "gx"),
            P(None, "gy", "gx"),
            P(None, "gy", "gx"),
            P("gy", "gx"),
        ),
        out_specs=(P(None, "gy", "gx"), P(None, "gy", "gx"), P(None, ("gx", "gy"))),
        check_vma=False,
    )
```

profile of v0, /device:TPU:0, one launch (start us, length us, event | category | flops | bytes accessed | tf_op | source)
XLA Modules:
  0.0 1354.5 jit_solution(13132587423246561825)
XLA Ops:
  4.4 7.3 all-to-all-start
  17.3 108.2 %gather_fusion = f32[32768,8]{1,0:T(8,128)} fusion(f32[8,2048]{0,1:T(8,128)S(1)} %copy.169, s32[32768]{0:T(1024)S(1)} %bitcast_clamp_fusion), kind=kCustom, calls=%fused_computation | custom fusion | bytes 2228224 | tf_op jit(solution)/shard_map/jit(_take)/gather | solution.py:148
  125.5 9.2 copy.170
  137.1 23.9 %scatter_fusion = f32[8,512,128]{2,0,1:T(8,128)} fusion(f32[8,512,128]{2,0,1:T(8,128)} %broadcast_in_dim.39, s32[256]{0:T(256)S(1)} %bitcast.147, f32[256,8,128]{2,1,0:T(8,128)S(1)} %multiply_bitcast_fusion), kind=kCustom, calls=%fused_computation.4 | custom fusion | bytes 3146752 | tf_op jit(solution)/shard_map/scatter | solution.py:153
  162.6 3.6 collective-permute-done.5
  167.6 5.8 all-to-all-start.1
  173.7 49.8 %all-to-all-done.1 = f32[8,512,128]{2,0,1:T(8,128)S(1)} async-done(((f32[8,512,128]{2,0,1:T(8,128)}), f32[8,512,128]{2,0,1:T(8,128)S(1)}, u32[]{:S(2)}, u32[]{:S(2)}) %all-to-all-start.1) | async-done | bytes 2097184 | tf_op jit(solution)/shard_map/all_to_all | solution.py:161
  223.5 16.6 %copy.171 = f32[65536,8]{1,0:T(8,128)} copy(f32[65536,8]{0,1:T(8,128)S(1)} %bitcast.131) | data formatting | bytes 4194304 | tf_op jit(solution)/shard_map/reshape | solution.py:167
  240.1 412.7 %scatter_custom_fusion.2 = f32[8,16384]{0,1:T(8,128)} fusion(s32[65536]{0:T(1024)S(1)} %bitcast.144, f32[65536,8]{1,0:T(8,128)} %copy.171, f32[]{:T(128)} %constant.263.clone.1), kind=kCustom, calls=%fused_computation.49 | custom fusion | flops 524288 | bytes 524800 | tf_op jit(solution)/shard_map/scatter-add | solution.py:167
  652.8 41.8 %fusion.3 = (f32[16384]{0:T(1024)S(1)}, f32[16384]{0:T(1024)}, f32[16384]{0:T(1024)S(1)}, f32[16384]{0:T(1024)S(1)}) fusion(f32[8,16384]{0,1:T(8,128)} %scatter_custom_fusion.2), kind=kLoop, calls=%fused_computation.24 | loop fusion | flops 131072 | bytes 786432 | tf_op jit(solution)/shard_map/mul | solution.py:177
  704.5 10.0 collective-permute-start.1
  719.0 6.5 fusion.15
  738.0 17.0 %fusion.9 = f32[81,34,514]{2,1,0:T(8,128)} fusion(f32[1,32,512]{2,1,0:T(8,128)S(1)} %get-tuple-element.136, f32[20,32,512]{2,1,0:T(8,128)S(1)} %get-tuple-element.138, f32[20,32,512]{2,1,0:T(8,128)S(1)} %get-tuple-element.134, f32[81,1,514]{2,1,0:T(1,128)} %collective-permute-done.3, f32[81,32,1]{2,1,0:T(8,128)} %copy.175, f32[40,32,512]{2,1,0:T(8,128)} %bitcast.120, ...), kind=kLoop, calls=%fused_computation.34 | loop fusion | flops 9908892 | bytes 11324448 | tf_op jit(solution)/shard_map/concatenate | solution.py:19
  756.4 18.5 %scatter.36 = f32[81,34,514]{2,1,0:T(8,128)} dynamic-update-slice(f32[81,34,514]{2,1,0:T(8,128)} %fusion.9, f32[81,1,512]{2,1,0:T(1,128)S(1)} %broadcast_select_fusion.1, s32[]{:T(128)} %constant.264.clone.1, s32[]{:T(128)} %constant.274.clone.1, s32[]{:T(128)} %constant.275.clone.1) | dynamic-update-slice | bytes 331780 | tf_op jit(solution)/shard_map/scatter | solution.py:87
  809.3 6.9 fusion.17
  832.5 16.8 %fusion.13 = f32[81,34,514]{2,1,0:T(8,128)} fusion(f32[1,32,512]{2,1,0:T(8,128)S(1)} %get-tuple-element.136, f32[20,32,512]{2,1,0:T(8,128)} %copy-done.3, f32[20,32,512]{2,1,0:T(8,128)} %copy-done, f32[81,1,514]{2,1,0:T(1,128)S(1)} %collective-permute-done.9, f32[81,32,1]{2,1,0:T(8,128)} %copy.185, f32[40,32,512]{2,1,0:T(8,128)S(1)} %bitcast.112, ...), kind=kLoop, calls=%fused_computation.38 | loop fusion | flops 9908892 | bytes 11324448 | tf_op jit(solution)/shard_map/concatenate | solution.py:19
  849.8 18.6 %scatter.38 = f32[81,34,514]{2,1,0:T(8,128)} dynamic-update-slice(f32[81,34,514]{2,1,0:T(8,128)} %fusion.13, f32[81,1,512]{2,1,0:T(1,128)S(1)} %broadcast_select_fusion, s32[]{:T(128)} %constant.264.clone.1, s32[]{:T(128)} %constant.274.clone.1, s32[]{:T(128)} %constant.275.clone.1) | dynamic-update-slice | bytes 331780 | tf_op jit(solution)/shard_map/scatter | solution.py:87
  889.6 5.1 copy.192
  894.6 218.9 %gather_fusion.1 = f32[65536,4]{1,0:T(8,128)} fusion(f32[4,16384]{0,1:T(8,128)} %copy.192, s32[65536]{0:T(1024)S(1)} %fusion.55), kind=kCustom, calls=%fused_computation.1 | custom fusion | bytes 2359296 | tf_op jit(solution)/shard_map/jit(_take)/gather | solution.py:192
  1113.5 18.3 %copy.193 = f32[512,128,4]{1,2,0:T(4,128)} copy(f32[512,128,4]{2,1,0:T(8,128)} %bitcast.121) | data formatting | bytes 2097152 | tf_op jit(solution)/shard_map/jit(_take)/gather | solution.py:192
  1134.4 5.9 all-to-all-start.2
  1142.3 25.6 %all-to-all-done.2 = f32[4,512,128]{2,0,1:T(4,128)} async-done(((f32[4,512,128]{2,0,1:T(4,128)}), f32[4,512,128]{2,0,1:T(4,128)}, u32[]{:S(2)}, u32[]{:S(2)}) %all-to-all-start.2) | async-done | bytes 1048608 | tf_op jit(solution)/shard_map/all_to_all | solution.py:193
  1170.3 8.6 copy.194
  1178.8 174.5 %scatter_custom_fusion.3 = f32[4,2048]{0,1:T(8,128)S(1)} fusion(s32[32768]{0:T(1024)S(1)} %bitcast.145, f32[32768,4]{1,0:T(8,128)} %copy.194, f32[]{:T(128)} %constant.263.clone.1), kind=kCustom, calls=%fused_computation.120 | custom fusion | flops 131072 | bytes 33280 | tf_op jit(solution)/shard_map/scatter-add | solution.py:198
  (188 shorter events, 122.9 us)
Async XLA Ops:
  4.4 163.2 %all-to-all-start = ((s32[1,512,128]{2,0,1:T(1,128)}), s32[1,512,128]{2,0,1:T(1,128)S(1)}, u32[]{:S(2)}, u32[]{:S(2)}) async-start(s32[1,512,128]{2,0,1:T(1,128)} %bitcast.9), calls=%async_computation | async-start | bytes 524288 | tf_op jit(solution)/shard_map/all_to_all | solution.py:162
  13.7 147.3 %collective-permute-start.4 = (f32[41,512]{1,0:T(8,128)S(1)}, f32[41,512]{1,0:T(8,128)}, u32[]{:S(2)}, u32[]{:S(2)}) collective-permute-start(f32[41,512]{1,0:T(8,128)S(1)} %pad_maximum_fusion.20), channel_id=1, source_target_pairs={{0,8},{8,0},{16,24},{24,16},{1,9},{9,1},{17,25},{25,17},{2,10},{10... | collective-permute-start | bytes 251912 | tf_op jit(solution)/shard_map/ppermute | solution.py:31
  161.0 5.3 collective-permute-start.5
  167.6 55.8 %all-to-all-start.1 = ((f32[8,512,128]{2,0,1:T(8,128)}), f32[8,512,128]{2,0,1:T(8,128)S(1)}, u32[]{:S(2)}, u32[]{:S(2)}) async-start(f32[8,512,128]{2,0,1:T(8,128)} %scatter_fusion), calls=%async_computation.1 | async-start | bytes 4194304 | tf_op jit(solution)/shard_map/all_to_all | solution.py:161
  652.8 41.9 %copy-start.2 = (f32[20,32,512]{2,1,0:T(8,128)S(1)}, f32[20,32,512]{2,1,0:T(8,128)}, u32[]{:S(2)}) copy-start(f32[20,32,512]{2,1,0:T(8,128)} %param.33) | copy-start | bytes 3932164
  652.8 41.9 %copy-start.5 = (f32[20,32,512]{2,1,0:T(8,128)S(1)}, f32[20,32,512]{2,1,0:T(8,128)}, u32[]{:S(2)}) copy-start(f32[20,32,512]{2,1,0:T(8,128)} %param.34) | copy-start | bytes 3932164
  695.3 42.7 %copy-start = (f32[20,32,512]{2,1,0:T(8,128)}, f32[20,32,512]{2,1,0:T(8,128)S(1)}, u32[]{:S(2)}) copy-start(f32[20,32,512]{2,1,0:T(8,128)S(1)} %get-tuple-element.134) | copy-start | bytes 3932164
  695.3 42.7 %copy-start.3 = (f32[20,32,512]{2,1,0:T(8,128)}, f32[20,32,512]{2,1,0:T(8,128)S(1)}, u32[]{:S(2)}) copy-start(f32[20,32,512]{2,1,0:T(8,128)S(1)} %get-tuple-element.138) | copy-start | bytes 3932164
  702.5 12.1 collective-permute-start
  704.5 12.2 collective-permute-start.1
  726.5 7.1 collective-permute-start.3
  728.2 9.9 collective-permute-start.2
  734.7 20.3 %copy-start.21 = (f32[40,1,512]{2,1,0:T(1,128)S(1)}, f32[40,1,512]{2,1,0:T(1,128)}, u32[]{:S(2)}) copy-start(f32[40,1,512]{2,1,0:T(1,128)} %concatenate.75) | copy-start | bytes 245764
  799.4 5.5 collective-permute-start.6
  801.5 5.6 collective-permute-start.7
  804.5 15.9 %collective-permute-start.10 = (f32[41,512]{1,0:T(8,128)}, f32[41,512]{1,0:T(8,128)}, u32[]{:S(2)}, u32[]{:S(2)}) collective-permute-start(f32[41,512]{1,0:T(8,128)} %pad_maximum_fusion.19), channel_id=1, source_target_pairs={{0,8},{8,0},{16,24},{24,16},{1,9},{9,1},{17,25},{25,17},{2,10},{10... | collective-permute-start | bytes 251912 | tf_op jit(solution)/shard_map/ppermute | solution.py:31
  809.3 12.5 copy-start.17
  817.2 15.1 %collective-permute-start.9 = (f32[81,1,514]{2,1,0:T(1,128)}, f32[81,1,514]{2,1,0:T(1,128)S(1)}, u32[]{:S(2)}, u32[]{:S(2)}) collective-permute-start(f32[81,1,514]{2,1,0:T(1,128)} %get-tuple-element.122), channel_id=1, source_target_pairs={{1,0},{2,1},{3,2},{4,3},{5,4},{6,5},{7,6},{0,7},{9,8},{10,9},{11,1... | collective-permute-start | bytes 499616 | tf_op jit(solution)/shard_map/ppermute | solution.py:23
  820.4 12.1 collective-permute-start.8
  820.4 5.1 collective-permute-start.11
  832.5 16.9 %copy-start.22 = (f32[40,1,512]{2,1,0:T(1,128)S(1)}, f32[40,1,512]{2,1,0:T(1,128)}, u32[]{:S(2)}) copy-start(f32[40,1,512]{2,1,0:T(1,128)} %concatenate.84) | copy-start | bytes 245764
  1113.5 18.3 %copy-start.23 = (pred[512,128]{1,0:T(8,128)(4,1)S(1)}, pred[512,128]{1,0:T(8,128)(4,1)}, u32[]{:S(2)}) copy-start(pred[512,128]{1,0:T(8,128)(4,1)} %compare_and_fusion) | copy-start | bytes 196612
  1134.4 33.5 %all-to-all-start.2 = ((f32[4,512,128]{2,0,1:T(4,128)}), f32[4,512,128]{2,0,1:T(4,128)}, u32[]{:S(2)}, u32[]{:S(2)}) async-start(f32[4,512,128]{2,0,1:T(4,128)} %select_bitcast_fusion), calls=%async_computation.2 | async-start | bytes 2097152 | tf_op jit(solution)/shard_map/all_to_all | solution.py:193
  1140.5 29.6 %copy-start.20 = (f32[256,128]{1,0:T(8,128)S(1)}, f32[256,128]{1,0:T(8,128)}, u32[]{:S(2)}) copy-start(f32[256,128]{1,0:T(8,128)} %param.30) | copy-start | bytes 393220
  (21 other events, 81.7 us)
where the time goes:
time: 1360 us; the launch traced here: 1350 us
  other arithmetic  722 us (53%)
  local copies, waits for them, and re-layouts  505 us (37%)
  waiting for transfers between devices  85.8 us (6%)
  starting transfers between devices  40.5 us (3%)
    scatter-add x1, other arithmetic, body(): remapped = jnp.zeros((field_count, parallel_lines * meridian_lines), jnp....  413 us
    gather x2, local copies, waits for them, and re-layouts, body(): picked = jnp.take(surface.reshape(4, -1), places[0], axis=1)  237 us
    scatter-add x1, other arithmetic, body(): back_fields = jnp.zeros((4, atm_cells), jnp.float32).at[:, overlay_air_el...  174 us
    gather x2, local copies, waits for them, and re-layouts, body(): jnp.take(air_forcing_quantities, overlay_air_element, axis=1)  117 us
    all_to_all x1, waiting for transfers between devices, body(): lax.all_to_all(outgoing, ('gx', 'gy'), split_axis=1, concat_axis=1, tiled...  49.8 us
    concatenate x4, other arithmetic, extended(): jnp.concatenate([lax.ppermute(tail, axis, [(i, (i + 1) % count) for i in...  47.2 us
    mul x1, other arithmetic, body(): forcing = jnp.stack([heat_factor * heat_flux, fresh_factor * fresh_flux])  41.8 us
    scatter x2, local copies, waits for them, and re-layouts, ocean_step(): padded.at[:, -1, 1:-1].set(jnp.where(is_top, replacement, north_row))  37.1 us
  transfers between devices with their start and end apart: 15, of which 6 were waited for; matrix products, arithmetic and copies ran while one was open for 13% of the time, Pallas kernels for 0%

commit v1 on v0

v1 whole, which is shorter than its diff:
```python
import functools

import jax
import jax.numpy as jnp
from jax import lax
from jax.experimental import pallas as pl
from jax.experimental.pallas import tpu as pltpu
from jax.sharding import PartitionSpec as P

diffuse_rate = 0.12
mixing_base = 0.02
mixing_extra = 0.2
heat_factor = 0.5
fresh_factor = 0.5
stress_factor = 0.3

LANES = 128
GROUP = 8
PAIR = 2
VMEM_BYTES = 48 * 1024 * 1024
CONTRACT_LAST = (((1,), (1,)), ((), ()))

SMEM = pl.BlockSpec(memory_space=pltpu.SMEM)
VMEM = pl.BlockSpec(memory_space=pltpu.VMEM)


def density(temper_field, saline_field):
    return (
        -0.2 * temper_field
        - 0.05 * temper_field * temper_field
        + 0.8 * saline_field
        + 0.03 * temper_field * saline_field
    )


def face_flux(near_cells, far_cells, velocity, open_faces):
    return open_faces * (
        velocity * 0.5 * (near_cells + far_cells) - diffuse_rate * (far_cells - near_cells)
    )


def two_terms(values):
    high = values.astype(jnp.bfloat16).astype(jnp.float32)
    return high, values - high


def one_hot(places, count):
    rows = lax.broadcasted_iota(jnp.int32, (count, places.shape[1]), 0)
    return jnp.where(rows == places, 1.0, 0.0).astype(jnp.bfloat16)


def spread(rows_of, terms, count):
    rows = lax.broadcasted_iota(jnp.int32, (count, rows_of.shape[1]), 0)
    hit = rows == rows_of
    return jnp.concatenate([jnp.where(hit, term, 0.0) for term in terms], axis=0).astype(
        jnp.bfloat16
    )


def picked_rows(rows_of, table, fields, count):
    rows = lax.broadcasted_iota(jnp.int32, (count, rows_of.shape[1]), 0)
    hit = rows == rows_of
    return [
        jnp.sum(
            jnp.where(hit, table[field * count : (field + 1) * count], 0.0), axis=0, keepdims=True
        )
        for field in range(fields)
    ]


def send_kernel(
    capacity, subdomain, table, element, profile, share, out, home, tally, split_table
):
    devices = tally.shape[0]
    blocks = element.shape[0]
    high_rows = table.shape[0] // 4

    def clear(i, carry):
        tally[i] = 0
        return carry

    lax.fori_loop(0, devices, clear, 0)
    out[...] = jnp.full(out.shape, -1.0, jnp.float32)
    high, low = two_terms(table[...])
    split_table[:, :LANES] = high.astype(jnp.bfloat16)
    split_table[:, LANES:] = low.astype(jnp.bfloat16)

    def group(g, carry):
        base = pl.multiple_of(g * GROUP, GROUP)
        cells = element[pl.ds(base, GROUP), :]
        near = cells & (LANES - 1)
        far = cells >> 7
        address = profile[pl.ds(base, GROUP), :].astype(jnp.float32)
        weight = share[pl.ds(base, GROUP), :]
        for first in range(0, GROUP, PAIR):
            names = range(first, first + PAIR)
            hot = jnp.concatenate([one_hot(near[b : b + 1], LANES) for b in names], axis=1)
            found = jnp.dot(
                split_table[...],
                jnp.concatenate([hot, hot], axis=0),
                preferred_element_type=jnp.float32,
            )
            far_row = jnp.concatenate([far[b : b + 1] for b in names], axis=1)
            values = picked_rows(far_row, found, 4, high_rows)
            for turn, b in enumerate(names):
                tile = subdomain[base + b]
                place = tally[tile]
                tally[tile] = place + 1
                home[base + b] = tile * (4 * capacity) + place
                row = tile * (5 * capacity) + place
                for field in range(4):
                    out[pl.ds(row + field * capacity, 1), :] = (
                        values[field][:, turn * LANES : (turn + 1) * LANES] * weight[b : b + 1]
                    )
                out[pl.ds(row + 4 * capacity, 1), :] = address[b : b + 1]
        return carry

    lax.fori_loop(0, blocks // GROUP, group, 0)


def gather_kernel_params(flops):
    return dict(
        compiler_params=pltpu.CompilerParams(vmem_limit_bytes=VMEM_BYTES),
        cost_estimate=pl.CostEstimate(flops=flops, bytes_accessed=4_000_000, transcendentals=0),
    )


def land_kernel(capacity, parallels, meridians, counts, arrived, remapped, places, slots, values, total):
    sources = counts.shape[0]
    last = slots.shape[0] - 1
    shift = meridians.bit_length() - 1
    places[...] = jnp.full(places.shape, -1.0, jnp.float32)
    total[...] = jnp.zeros(total.shape, jnp.float32)

    def from_source(source, count):
        def slot(place, count):
            row = source * (5 * capacity) + place
            for field in range(4):
                values[field, pl.ds(count, 1), :] = arrived[pl.ds(row + field * capacity, 1), :]
            places[pl.ds(count, 1), :] = arrived[pl.ds(row + 4 * capacity, 1), :]
            slots[count] = source * (4 * capacity) + place
            return count + 1

        return lax.fori_loop(0, counts[source], slot, count)

    filled = lax.fori_loop(0, sources, from_source, 0)
    slots[last] = filled

    def group(g, carry):
        base = pl.multiple_of(g * GROUP, GROUP)
        address = places[pl.ds(base, GROUP), :].astype(jnp.int32)
        row = address >> shift
        column = address & (meridians - 1)
        split = [two_terms(values[field, pl.ds(base, GROUP), :]) for field in range(4)]
        terms = [split[field][term] for term in range(2) for field in range(4)]
        sums = None
        for first in range(0, GROUP, PAIR):
            names = range(first, first + PAIR)
            left = jnp.concatenate(
                [
                    spread(row[b : b + 1], [term[b : b + 1] for term in terms], parallels)
                    for b in names
                ],
                axis=1,
            )
            right = jnp.concatenate([one_hot(column[b : b + 1], meridians) for b in names], axis=1)
            part = lax.dot_general(
                left, right, CONTRACT_LAST, preferred_element_type=jnp.float32
            )
            sums = part if sums is None else sums + part
        total[...] += sums
        return carry

    lax.fori_loop(0, (filled + GROUP - 1) // GROUP, group, 0)
    half = 4 * parallels
    remapped[...] = total[:half] + total[half:]


def pick_kernel(capacity, parallels, meridians, slots, surface, places, out, split_table):
    last = slots.shape[0] - 1
    half = 4 * parallels
    shift = meridians.bit_length() - 1
    filled = slots[last]
    high, low = two_terms(surface[...])
    split_table[:half] = high.astype(jnp.bfloat16)
    split_table[half:] = low.astype(jnp.bfloat16)
    out[...] = jnp.zeros(out.shape, jnp.float32)

    def group(g, carry):
        base = pl.multiple_of(g * GROUP, GROUP)
        address = places[pl.ds(base, GROUP), :].astype(jnp.int32)
        row = address >> shift
        column = address & (meridians - 1)
        for first in range(0, GROUP, PAIR):
            names = range(first, first + PAIR)
            hot = jnp.concatenate([one_hot(column[b : b + 1], meridians) for b in names], axis=1)
            found = jnp.dot(split_table[...], hot, preferred_element_type=jnp.float32)
            found = found[:half] + found[half:]
            wide_row = jnp.concatenate([row[b : b + 1] for b in names], axis=1)
            values = picked_rows(wide_row, found, 4, parallels)
            for turn, b in enumerate(names):

                @pl.when(base + b < filled)
                def _():
                    target = slots[base + b]
                    for field in range(4):
                        out[pl.ds(target + field * capacity, 1), :] = values[field][
                            :, turn * LANES : (turn + 1) * LANES
                        ]

        return carry

    lax.fori_loop(0, (filled + GROUP - 1) // GROUP, group, 0)


def back_kernel(capacity, home, returned, element, share, out, total):
    blocks = element.shape[0]
    high_rows = out.shape[0] // 4
    total[...] = jnp.zeros(total.shape, jnp.float32)

    def group(g, carry):
        base = pl.multiple_of(g * GROUP, GROUP)
        cells = element[pl.ds(base, GROUP), :]
        near = cells & (LANES - 1)
        far = cells >> 7
        weight = share[pl.ds(base, GROUP), :]
        sums = None
        for first in range(0, GROUP, PAIR):
            names = range(first, first + PAIR)
            lefts = []
            for b in names:
                row = home[base + b]
                split = [
                    two_terms(returned[pl.ds(row + field * capacity, 1), :] * weight[b : b + 1])
                    for field in range(4)
                ]
                terms = [split[field][term] for term in range(2) for field in range(4)]
                lefts.append(spread(far[b : b + 1], terms, high_rows))
            left = jnp.concatenate(lefts, axis=1)
            right = jnp.concatenate([one_hot(near[b : b + 1], LANES) for b in names], axis=1)
            part = lax.dot_general(
                left, right, CONTRACT_LAST, preferred_element_type=jnp.float32
            )
            sums = part if sums is None else sums + part
        total[...] += sums
        return carry

    lax.fori_loop(0, blocks // GROUP, group, 0)
    half = 4 * high_rows
    out[...] = total[:half] + total[half:]


def ocean_kernel(
    top,
    temper,
    saline,
    east,
    north,
    ocean_mask,
    sides,
    ends,
    remapped,
    remap_sides,
    remap_ends,
    temper_out,
    saline_out,
    surface,
    first_t,
    first_s,
    second_t,
    second_s,
    east_all,
    north_all,
    remap_all,
    opens,
):
    depth, rows, columns = temper.shape
    all_rows, all_columns = first_t.shape[1:]

    def fill(target, source, side, end):
        target[:, :rows, :columns] = source[...]
        target[:, :rows, columns:] = side
        target[:, rows:, :] = end

    for turn, (target, source) in enumerate(
        ((first_t, temper), (first_s, saline), (east_all, east), (north_all, north))
    ):
        part = slice(turn * depth, (turn + 1) * depth)
        fill(target, source, sides[part], ends[part])
    fill(remap_all, remapped, remap_sides[...], remap_ends[...])
    opens[0, :rows, :columns] = ocean_mask[...].astype(jnp.float32)
    opens[0, :rows, columns:] = sides[4 * depth]
    opens[0, rows:, :] = ends[4 * depth]

    def next_column(x):
        return pltpu.roll(x, all_columns - 1, axis=1)

    def next_row(x):
        return pltpu.roll(x, all_rows - 1, axis=0)

    here = opens[0]
    opens[1] = here * next_column(here)
    opens[2] = here * next_row(here)
    row_ids = lax.broadcasted_iota(jnp.int32, (all_rows, all_columns), 0)
    opens[3] = jnp.where((row_ids == rows - 1) & (top[0] == 1), 0.0, 1.0)
    east_all[0] = east_all[0] + stress_factor * remap_all[2]
    north_all[0] = north_all[0] + stress_factor * remap_all[3]
    remap_all[0] = heat_factor * remap_all[0]
    remap_all[1] = fresh_factor * remap_all[1]

    def step(source_t, source_s, keep):
        def level(k, carry):
            gain_t, gain_s = carry
            below = jnp.minimum(k + 1, depth - 1)
            t, s = source_t[k], source_s[k]
            t_below, s_below = source_t[below], source_s[below]
            mask = opens[0]
            mixing = (
                mixing_base
                + mixing_extra
                * jax.nn.sigmoid(4.0 * (density(t, s) - density(t_below, s_below)))
            ) * mask
            east_speed = east_all[k]
            north_speed = north_all[k] * opens[3]
            new_gains = []
            for x, x_below, gain, target, forcing in (
                (t, t_below, gain_t, 0, 0),
                (s, s_below, gain_s, 1, 1),
            ):
                gradient = mixing * (x_below - x)
                east_flux = face_flux(x, next_column(x), east_speed, opens[1])
                north_flux = face_flux(x, next_row(x), north_speed, opens[2])
                change = (
                    -(east_flux - pltpu.roll(east_flux, 1, axis=1))
                    - (north_flux - pltpu.roll(north_flux, 1, axis=0))
                    + (gradient - gain)
                )
                change = change + jnp.where(k == 0, remap_all[forcing], 0.0)
                keep(target, k, x + mask * change)
                new_gains.append(gradient)
            return tuple(new_gains)

        nothing = jnp.zeros((all_rows, all_columns), jnp.float32)
        lax.fori_loop(0, depth, level, (nothing, nothing))

    def keep_first(target, k, value):
        (second_t, second_s)[target][k] = value

    def keep_last(target, k, value):
        (temper_out, saline_out)[target][k] = value[:rows, :columns]

    step(first_t, first_s, keep_first)
    step(second_t, second_s, keep_last)

    mask = opens[0, :rows, :columns]
    t, s = temper_out[0], saline_out[0]
    surface[0] = t * mask
    surface[1] = s * mask
    surface[2] = density(t, s) * mask
    surface[3] = east_all[0, :rows, :columns] * mask


def halo(parts, east_at, north_at):
    rows, columns = parts[0].shape[1:]
    count_gx, count_gy = lax.axis_size("gx"), lax.axis_size("gy")
    head = jnp.concatenate([x[:, :, :2] for x in parts], axis=0)
    tail = jnp.concatenate([x[:, :, -2:] for x in parts], axis=0)
    channels = head.shape[0]
    from_west = lax.ppermute(tail, "gx", [(i, (i + 1) % count_gx) for i in range(count_gx)])
    from_east = lax.ppermute(head, "gx", [((i + 1) % count_gx, i) for i in range(count_gx)])
    sides = jnp.concatenate(
        [from_east, jnp.zeros((channels, rows, LANES - 4), jnp.float32), from_west], axis=2
    )
    low = jnp.concatenate(
        [jnp.concatenate([x[:, :2] for x in parts], axis=0), sides[:, :2]], axis=2
    )
    high = jnp.concatenate(
        [jnp.concatenate([x[:, -2:] for x in parts], axis=0), sides[:, -2:]], axis=2
    )
    from_south = lax.ppermute(high, "gy", [(i, i + 1) for i in range(count_gy - 1)])
    from_north = lax.ppermute(low, "gy", [(i + 1, i) for i in range(count_gy - 1)])
    folded = lax.ppermute(high, "gx", [(i, count_gx - 1 - i) for i in range(count_gx)])
    folded = jnp.concatenate(
        [folded[:, ::-1, columns - 1 :: -1], folded[:, ::-1, : columns - 1 : -1]], axis=2
    )
    e0, e1 = east_at
    n0, n1 = north_at
    east_part = -jnp.concatenate([folded[e0:e1, :, 1:], folded[e0:e1, :, :1]], axis=2)
    north_part = -jnp.concatenate([folded[n0:n1, 1:], folded[n0:n1, :1]], axis=1)
    folded = jnp.concatenate([folded[:e0], east_part, north_part, folded[n1:]], axis=0)
    is_top = lax.axis_index("gy") == count_gy - 1
    above = jnp.where(is_top, folded, from_north)
    ends = jnp.concatenate(
        [above, jnp.zeros((channels, 4, columns + LANES), jnp.float32), from_south], axis=1
    )
    return sides, ends


def body(
    air_forcing_quantities,
    segment_sea_subdomain,
    overlay_air_element,
    overlay_sea_profile,
    overlay_fraction_share,
    thermal_deviation,
    saltiness_deviation,
    zonal_interface_speed,
    poleward_interface_speed,
    sea_profile_indicator,
):
    devices = lax.axis_size("gx") * lax.axis_size("gy")
    blocks = segment_sea_subdomain.shape[0]
    atm_cells = air_forcing_quantities.shape[1]
    depth, parallels, meridians = thermal_deviation.shape
    capacity = max(2, 2 * blocks // devices)
    slot_count = devices * capacity
    f32 = jnp.float32
    air = air_forcing_quantities
    table = jnp.stack([air[0] + air[1] + air[2] + air[3], air[5] - air[4], air[6], air[7]])
    table = table.reshape(4 * atm_cells // LANES, LANES)

    outgoing, home = pl.pallas_call(
        functools.partial(send_kernel, capacity),
        out_shape=(
            jax.ShapeDtypeStruct((slot_count * 5, LANES), f32),
            jax.ShapeDtypeStruct((blocks,), jnp.int32),
        ),
        in_specs=[SMEM, VMEM, VMEM, VMEM, VMEM],
        out_specs=(VMEM, SMEM),
        scratch_shapes=[
            pltpu.SMEM((devices,), jnp.int32),
            pltpu.VMEM((table.shape[0], 2 * LANES), jnp.bfloat16),
        ],
        **gather_kernel_params(10**9),
    )(
        segment_sea_subdomain.reshape(blocks),
        table,
        overlay_air_element,
        overlay_sea_profile,
        overlay_fraction_share,
    )
    arrived = lax.all_to_all(outgoing, ("gx", "gy"), split_axis=0, concat_axis=0, tiled=True)

    ocean_mask = sea_profile_indicator.astype(f32)
    sides, ends = halo(
        [
            thermal_deviation,
            saltiness_deviation,
            zonal_interface_speed,
            poleward_interface_speed,
            ocean_mask[None],
        ],
        (2 * depth, 3 * depth),
        (3 * depth, 4 * depth),
    )

    counts = jnp.sum(
        (arrived.reshape(devices, 5, capacity, LANES)[:, 4, :, 0] >= 0).astype(jnp.int32), axis=1
    )
    remapped, places, slots = pl.pallas_call(
        functools.partial(land_kernel, capacity, parallels, meridians),
        out_shape=(
            jax.ShapeDtypeStruct((4 * parallels, meridians), f32),
            jax.ShapeDtypeStruct((slot_count + GROUP, LANES), f32),
            jax.ShapeDtypeStruct((slot_count + 1,), jnp.int32),
        ),
        in_specs=[SMEM, VMEM],
        out_specs=(VMEM, VMEM, SMEM),
        scratch_shapes=[
            pltpu.VMEM((4, slot_count + GROUP, LANES), f32),
            pltpu.VMEM((8 * parallels, meridians), f32),
        ],
        **gather_kernel_params(2 * 10**10),
    )(counts, arrived)
    remapped = remapped.reshape(4, parallels, meridians)
    remap_sides, remap_ends = halo([remapped], (2, 3), (3, 4))

    top = (lax.axis_index("gy") == lax.axis_size("gy") - 1).astype(jnp.int32).reshape(1)
    wide = (parallels + 8, meridians + LANES)
    cube = jax.ShapeDtypeStruct((depth, parallels, meridians), f32)
    temper, saline, surface = pl.pallas_call(
        ocean_kernel,
        out_shape=(cube, cube, jax.ShapeDtypeStruct((4, parallels, meridians), f32)),
        in_specs=[SMEM] + [VMEM] * 10,
        out_specs=(VMEM, VMEM, VMEM),
        scratch_shapes=[pltpu.VMEM((depth,) + wide, f32)] * 6 + [pltpu.VMEM((4,) + wide, f32)] * 2,
        **gather_kernel_params(10**9),
    )(
        top,
        thermal_deviation,
        saltiness_deviation,
        zonal_interface_speed,
        poleward_interface_speed,
        sea_profile_indicator,
        sides,
        ends,
        remapped,
        remap_sides,
        remap_ends,
    )

    picked = pl.pallas_call(
        functools.partial(pick_kernel, capacity, parallels, meridians),
        out_shape=jax.ShapeDtypeStruct((slot_count * 4, LANES), f32),
        in_specs=[SMEM, VMEM, VMEM],
        out_specs=VMEM,
        scratch_shapes=[pltpu.VMEM((8 * parallels, meridians), jnp.bfloat16)],
        **gather_kernel_params(2 * 10**10),
    )(slots, surface.reshape(4 * parallels, meridians), places)
    returned = lax.all_to_all(picked, ("gx", "gy"), split_axis=0, concat_axis=0, tiled=True)
    back_fields = pl.pallas_call(
        functools.partial(back_kernel, capacity),
        out_shape=jax.ShapeDtypeStruct((4 * atm_cells // LANES, LANES), f32),
        in_specs=[SMEM, VMEM, VMEM, VMEM],
        out_specs=VMEM,
        scratch_shapes=[pltpu.VMEM((8 * atm_cells // LANES, LANES), f32)],
        **gather_kernel_params(2 * 10**9),
    )(home, returned, overlay_air_element, overlay_fraction_share)
    return temper, saline, back_fields.reshape(4, atm_cells)


def solution(mesh):
    return jax.shard_map(
        body,
        mesh=mesh,
        in_specs=(
            P(None, ("gx", "gy")),
            P(("gx", "gy"), None),
            P(("gx", "gy"), None),
            P(("gx", "gy"), None),
            P(("gx", "gy"), None),
            P(None, "gy", "gx"),
            P(None, "gy", "gx"),
            P(None, "gy", "gx"),
            P(None, "gy", "gx"),
            P("gy", "gx"),
        ),
        out_specs=(P(None, "gy", "gx"), P(None, "gy", "gx"), P(None, ("gx", "gy"))),
        check_vma=False,
    )
```

time: 1360 us -> 284 us (0.21)
  other arithmetic: 722 us -> 21.7 us
  local copies, waits for them, and re-layouts: 505 us -> 40 us
  Pallas kernels: 0 us -> 151 us
  waiting for transfers between devices: 85.8 us -> 13.4 us
  blocking collectives: 0 us -> 33 us
  starting transfers between devices: 40.5 us -> 20.5 us
    scatter-add x4 -> x0, other arithmetic: 589 us -> none  [the longest x1 413 us: body(): remapped = jnp.zeros((field_count, parallel_lines * meridian_lines), jnp....]
    gather x5 -> x0, local copies, waits for them, and re-layouts: 357 us -> none  [the longest x2 237 us: body(): picked = jnp.take(surface.reshape(4, -1), places[0], axis=1)]
    pallas_call x0 -> x5, Pallas kernels: none -> 151 us  [the longest x1 76.9 us: body(): pl.pallas_call(functools.partial(pick_kernel, capacity, parallels, meridi...]
    all_to_all x3 -> x1, waiting for transfers between devices: 75.4 us -> 0.01 us  [body(): lax.all_to_all(outgoing, ('gx', 'gy'), split_axis=0, concat_axis=0, tiled...]
    scatter x6 -> x0, local copies, waits for them, and re-layouts: 65.8 us -> none  [the longest x2 37.1 us: ocean_step(): padded.at[:, -1, 1:-1].set(jnp.where(is_top, replacement, north_row))]
    mul x20 -> x0, other arithmetic: 63.5 us -> none  [the longest x1 41.8 us: body(): forcing = jnp.stack([heat_factor * heat_flux, fresh_factor * fresh_flux])]
    concatenate x8 -> x14, other arithmetic: 51.9 us -> 15.2 us  [the longest x6 5.56 us: halo(): jnp.concatenate([folded[:, ::-1, columns - 1::-1], folded[:, ::-1, :colum...]
    all_to_all x0 -> x1, blocking collectives: none -> 33 us  [body(): lax.all_to_all(picked, ('gx', 'gy'), split_axis=0, concat_axis=0, tiled=T...]
  transfers between devices with their start and end apart: 15 -> 11, of which waited for: 6 -> 6; matrix products, arithmetic and copies ran while one was open for 13% -> 15% of each run, Pallas kernels for 0% -> 4%
where the time goes in v1:
time: 284 us; the launch traced here: 280 us
  Pallas kernels  151 us (53%)
  local copies, waits for them, and re-layouts  40 us (14%)
  blocking collectives  33 us (12%)
  other arithmetic  21.7 us (8%)
  starting transfers between devices  20.5 us (7%)
  waiting for transfers between devices  13.4 us (5%)
    pallas_call x1, Pallas kernels, body(): pl.pallas_call(functools.partial(pick_kernel, capacity, parallels, meridi...  76.9 us
    pallas_call x1, Pallas kernels, body(): pl.pallas_call(functools.partial(land_kernel, capacity, parallels, meridi...  37.4 us
    all_to_all x1, blocking collectives, body(): lax.all_to_all(picked, ('gx', 'gy'), split_axis=0, concat_axis=0, tiled=T...  33 us
    pallas_call x1, Pallas kernels, body(): pl.pallas_call(ocean_kernel, out_shape=(cube, cube, jax.ShapeDtypeStruct(...  17.7 us
    unnamed x50, local copies, waits for them, and re-layouts  12.7 us
    pallas_call x1, Pallas kernels, body(): pl.pallas_call(functools.partial(send_kernel, capacity), out_shape=(jax.S...  9.87 us
    pallas_call x1, Pallas kernels, body(): pl.pallas_call(functools.partial(back_kernel, capacity), out_shape=jax.Sh...  8.92 us
    all_to_all x1, starting transfers between devices, body(): lax.all_to_all(outgoing, ('gx', 'gy'), split_axis=0, concat_axis=0, tiled...  6.75 us
  transfers between devices with their start and end apart: 11, of which 6 were waited for; matrix products, arithmetic and copies ran while one was open for 15% of the time, Pallas kernels for 4%

profile of v1, /device:TPU:0, one launch (start us, length us, event | category | flops | bytes accessed | tf_op | source)
XLA Modules:
  0.0 280.3 jit_solution(14905882119230129315)
XLA Ops:
  13.4 2.0 collective-permute-start
  15.5 9.9 %shard_map.121 = (f32[2560,128]{1,0:T(8,128)S(1)}, s32[256]{0:T(256)S(1)}) custom-call(s32[256]{0:T(256)S(1)} %bitcast.18, f32[64,128]{1,0:T(8,128)S(1)} %reshape.96.table, s32[256,128]{1,0:T(8,128)S(1)} %copy-done.8, s32[256,128]{1,0:T(8,128)S(1)} %copy-done.7, f32[256,128]{1,0:T(8,128)S(1)} %copy-done.9), custom_call_target="tpu_custom_call" | custom-call | flops 1000000000 | bytes 4000000 | tf_op jit(solution)/shard_map/pallas_call | solution.py:422
  26.4 6.7 %all-to-all-start = ((f32[32,80,128]{2,1,0:T(8,128)}), f32[32,80,128]{2,1,0:T(8,128)}, u32[]{:S(2)}, u32[]{:S(2)}) async-start(f32[32,80,128]{2,1,0:T(8,128)} %bitcast.11), calls=%async_computation | async-start | bytes 2621440 | tf_op jit(solution)/shard_map/all_to_all | solution.py:442
  36.5 2.9 %copy.23 = f32[81,32,2]{2,1,0:T(8,128)} copy(f32[81,32,2]{0,1,2:T(8,128)} %collective-permute-done) | data formatting | bytes 41472 | tf_op jit(solution)/shard_map/ppermute | solution.py:370
  39.5 2.9 %copy.24 = f32[81,32,2]{2,1,0:T(8,128)} copy(f32[81,32,2]{0,1,2:T(8,128)} %collective-permute-done.1) | data formatting | bytes 41472 | tf_op jit(solution)/shard_map/ppermute | solution.py:369
  42.3 2.1 pad_maximum_fusion.1.sides
  47.2 1.5 collective-permute-start.2
  48.7 4.1 %collective-permute-start.4 = (f32[81,2,640]{2,1,0:T(2,128)}, f32[81,2,640]{2,1,0:T(2,128)}, u32[]{:S(2)}, u32[]{:S(2)}) collective-permute-start(f32[81,2,640]{2,1,0:T(2,128)} %pad_maximum_fusion.2), channel_id=1, source_target_pairs={{0,1},{1,2},{2,3},{3,4},{4,5},{5,6},{6,7},{8,9},{9,10},{10,11},{11... | collective-permute-start | bytes 1244168 | tf_op jit(solution)/shard_map/ppermute | solution.py:380
  52.9 1.8 pad_maximum_fusion.3
  56.0 5.3 %collective-permute-done.2 = f32[81,2,640]{2,1,0:T(2,128)} collective-permute-done((f32[81,2,640]{2,1,0:T(2,128)}, f32[81,2,640]{2,1,0:T(2,128)}, u32[]{:S(2)}, u32[]{:S(2)}) %collective-permute-start.2) | collective-permute-done | bytes 414752 | tf_op jit(solution)/shard_map/ppermute | solution.py:382
  62.3 1.5 rev.12
  70.6 3.5 %collective-permute-done.4 = f32[81,2,640]{2,1,0:T(2,128)} collective-permute-done((f32[81,2,640]{2,1,0:T(2,128)}, f32[81,2,640]{2,1,0:T(2,128)}, u32[]{:S(2)}, u32[]{:S(2)}) %collective-permute-start.4) | collective-permute-done | bytes 414752 | tf_op jit(solution)/shard_map/ppermute | solution.py:380
  74.1 2.6 pad_maximum_fusion.ends
  76.7 1.6 convert_reduce_fusion.counts
  78.4 37.4 %shard_map.122 = (f32[128,512]{1,0:T(8,128)S(1)}, f32[520,128]{1,0:T(8,128)S(1)}, s32[513]{0:T(1024)S(1)}) custom-call(s32[32]{0:T(128)S(1)} %convert_reduce_fusion.counts, f32[2560,128]{1,0:T(8,128)} %bitcast.5.arrived), custom_call_target="tpu_custom_call" | custom-call | flops 20000000000 | bytes 4000000 | tf_op jit(solution)/shard_map/pallas_call | solution.py:460
  116.4 1.8 collective-permute-done.5
  118.2 1.4 collective-permute-done.6
  120.3 1.9 collective-permute-start.9
  123.4 1.5 collective-permute-start.8
  126.8 2.7 rev.14
  143.1 17.7 %shard_map.123 = (f32[20,32,512]{2,1,0:T(8,128)}, f32[20,32,512]{2,1,0:T(8,128)}, f32[4,32,512]{2,1,0:T(8,128)S(1)}) custom-call(s32[1]{0:T(128)} %bitcast.top, f32[20,32,512]{2,1,0:T(8,128)S(1)} %copy-done, f32[20,32,512]{2,1,0:T(8,128)S(1)} %copy-done.1, f32[20,32,512]{2,1,0:T(8,128)S(1)} %copy-done.3, f32[20,32,512]{2,1,0:T(8,128)S(1)} %copy-done.4, ...), custom_call_target="tpu_custom_call" | custom-call | flops 1000000000 | bytes 4000000 | tf_op jit(solution)/shard_map/pallas_call | solution.py:481
  160.8 76.9 %shard_map.124 = f32[2048,128]{1,0:T(8,128)S(1)} custom-call(s32[513]{0:T(1024)S(1)} %get-tuple-element.16.slots, f32[128,512]{1,0:T(8,128)S(1)} %bitcast.17, f32[520,128]{1,0:T(8,128)S(1)} %get-tuple-element.18.places), custom_call_target="tpu_custom_call" | custom-call | flops 20000000000 | bytes 4000000 | tf_op jit(solution)/shard_map/pallas_call | solution.py:502
  237.8 33.0 %all_to_all.22 = f32[32,64,128]{2,1,0:T(8,128)S(1)} all-to-all(f32[32,64,128]{2,1,0:T(8,128)S(1)} %bitcast.12), channel_id=1, replica_groups=mesh['gx'=4,'gy'=8] {'gx','gy'}, dimensions={0} | all-to-all | bytes 2097152 | tf_op jit(solution)/shard_map/all_to_all | solution.py:510
  270.8 8.9 %shard_map.125 = f32[64,128]{1,0:T(8,128)S(1)} custom-call(s32[256]{0:T(256)S(1)} %get-tuple-element.15.home, f32[2048,128]{1,0:T(8,128)S(1)} %bitcast.13, s32[256,128]{1,0:T(8,128)S(1)} %copy-done.8, f32[256,128]{1,0:T(8,128)S(1)} %copy-done.9), custom_call_target="tpu_custom_call" | custom-call | flops 2000000000 | bytes 4000000 | tf_op jit(solution)/shard_map/pallas_call | solution.py:511
  (111 shorter events, 47.6 us)
Async XLA Ops:
  0.6 3.2 %copy-start.1 = (f32[20,32,512]{2,1,0:T(8,128)S(1)}, f32[20,32,512]{2,1,0:T(8,128)}, u32[]{:S(2)}) copy-start(f32[20,32,512]{2,1,0:T(8,128)} %saline.1) | copy-start | bytes 3932164
  3.4 2.5 copy-start.2
  8.2 3.8 %copy-start.12 = (f32[20,32,2]{2,1,0:T(8,128)S(1)}, f32[20,32,2]{2,1,0:T(8,128)}, u32[]{:S(2)}) copy-start(f32[20,32,2]{2,1,0:T(8,128)} %get-tuple-element.31) | copy-start | bytes 15364
  9.4 6.0 %copy-start.7 = (s32[256,128]{1,0:T(8,128)S(1)}, s32[256,128]{1,0:T(8,128)}, u32[]{:S(2)}) copy-start(s32[256,128]{1,0:T(8,128)} %profile.1) | copy-start | bytes 393220
  9.5 6.0 %copy-start.8 = (s32[256,128]{1,0:T(8,128)S(1)}, s32[256,128]{1,0:T(8,128)}, u32[]{:S(2)}) copy-start(s32[256,128]{1,0:T(8,128)} %element.3) | copy-start | bytes 393220
  9.5 6.0 %copy-start.9 = (f32[256,128]{1,0:T(8,128)S(1)}, f32[256,128]{1,0:T(8,128)}, u32[]{:S(2)}) copy-start(f32[256,128]{1,0:T(8,128)} %share.3) | copy-start | bytes 393220
  9.5 6.0 %copy-start.10 = (s32[256,1]{0,1:T(1,128)S(1)}, s32[256,1]{0,1:T(1,128)}, u32[]{:S(2)}) copy-start(s32[256,1]{0,1:T(1,128)} %param.11) | copy-start | bytes 3076
  9.8 5.5 %copy-start.14 = (f32[8,2048]{1,0:T(8,128)S(1)}, f32[8,2048]{1,0:T(8,128)}, u32[]{:S(2)}) copy-start(f32[8,2048]{1,0:T(8,128)} %param.10) | copy-start | bytes 196612
  10.5 28.9 %collective-permute-start.1 = (f32[81,32,2]{0,1,2:T(8,128)}, f32[81,32,2]{0,1,2:T(8,128)}, u32[]{:S(2)}, u32[]{:S(2)}) collective-permute-start(f32[81,32,2]{0,1,2:T(8,128)} %concatenate.77), channel_id=1, source_target_pairs={{0,8},{8,16},{16,24},{24,0},{1,9},{9,17},{17,25},{25,1},{2,10},{10... | collective-permute-start | bytes 62216 | tf_op jit(solution)/shard_map/ppermute | solution.py:369
  13.4 23.1 %collective-permute-start = (f32[81,32,2]{0,1,2:T(8,128)}, f32[81,32,2]{0,1,2:T(8,128)}, u32[]{:S(2)}, u32[]{:S(2)}) collective-permute-start(f32[81,32,2]{0,1,2:T(8,128)} %concatenate.76), channel_id=1, source_target_pairs={{8,0},{16,8},{24,16},{0,24},{9,1},{17,9},{25,17},{1,25},{10,2},{18... | collective-permute-start | bytes 62216 | tf_op jit(solution)/shard_map/ppermute | solution.py:370
  26.4 6.8 %copy-start = (f32[20,32,512]{2,1,0:T(8,128)S(1)}, f32[20,32,512]{2,1,0:T(8,128)}, u32[]{:S(2)}) copy-start(f32[20,32,512]{2,1,0:T(8,128)} %temper.1) | copy-start | bytes 3932164
  26.4 50.3 %all-to-all-start = ((f32[32,80,128]{2,1,0:T(8,128)}), f32[32,80,128]{2,1,0:T(8,128)}, u32[]{:S(2)}, u32[]{:S(2)}) async-start(f32[32,80,128]{2,1,0:T(8,128)} %bitcast.11), calls=%async_computation | async-start | bytes 2621440 | tf_op jit(solution)/shard_map/all_to_all | solution.py:442
  36.5 5.9 %copy-start.17 = (f32[128]{0:T(128)}, f32[128]{0:T(128)S(1)}, u32[]{:S(2)}) copy-start(f32[128]{0:T(128)S(1)} %pad.40.clone) | copy-start | bytes 1540
  47.2 14.1 %collective-permute-start.2 = (f32[81,2,640]{2,1,0:T(2,128)}, f32[81,2,640]{2,1,0:T(2,128)}, u32[]{:S(2)}, u32[]{:S(2)}) collective-permute-start(f32[81,2,640]{2,1,0:T(2,128)} %pad_maximum_fusion.2), channel_id=1, source_target_pairs={{0,24},{8,16},{16,8},{24,0},{1,25},{9,17},{17,9},{25,1},{2,26},{10... | collective-permute-start | bytes 1244168 | tf_op jit(solution)/shard_map/ppermute | solution.py:382
  48.7 25.4 %copy-start.16 = (f32[8]{0:T(128)}, f32[8]{0:T(128)S(1)}, u32[]{:S(2)}) copy-start(f32[8]{0:T(128)S(1)} %pad.23.clone) | copy-start | bytes 100
  48.7 25.4 %collective-permute-start.4 = (f32[81,2,640]{2,1,0:T(2,128)}, f32[81,2,640]{2,1,0:T(2,128)}, u32[]{:S(2)}, u32[]{:S(2)}) collective-permute-start(f32[81,2,640]{2,1,0:T(2,128)} %pad_maximum_fusion.2), channel_id=1, source_target_pairs={{0,1},{1,2},{2,3},{3,4},{4,5},{5,6},{6,7},{8,9},{9,10},{10,11},{11... | collective-permute-start | bytes 1244168 | tf_op jit(solution)/shard_map/ppermute | solution.py:380
  54.7 14.6 %collective-permute-start.3 = (f32[81,2,640]{2,1,0:T(2,128)}, f32[81,2,640]{2,1,0:T(2,128)}, u32[]{:S(2)}, u32[]{:S(2)}) collective-permute-start(f32[81,2,640]{2,1,0:T(2,128)} %pad_maximum_fusion.3), channel_id=1, source_target_pairs={{1,0},{2,1},{3,2},{4,3},{5,4},{6,5},{7,6},{9,8},{10,9},{11,10},{12... | collective-permute-start | bytes 1244168 | tf_op jit(solution)/shard_map/ppermute | solution.py:381
  78.3 41.3 %copy-start.18 = (f32[128]{0:T(128)S(1)}, f32[128]{0:T(128)}, u32[]{:S(2)}) copy-start(f32[128]{0:T(128)} %copy-done.17) | copy-start | bytes 1540
  78.4 62.1 %copy-start.6 = (s32[32,512]{1,0:T(8,128)S(1)}, s32[32,512]{1,0:T(8,128)}, u32[]{:S(2)}) copy-start(s32[32,512]{1,0:T(8,128)} %ocean_mask.1) | copy-start | bytes 196612
  115.8 2.3 collective-permute-start.5
  115.9 3.7 %collective-permute-start.6 = (f32[4,32,2]{2,1,0:T(8,128)S(1)}, f32[4,32,2]{2,1,0:T(8,128)S(1)}, u32[]{:S(2)}, u32[]{:S(2)}) collective-permute-start(f32[4,32,2]{2,1,0:T(8,128)S(1)} %get-tuple-element.42), channel_id=1, source_target_pairs={{0,8},{8,16},{16,24},{24,0},{1,9},{9,17},{17,25},{25,1},{2,10},{10... | collective-permute-start | bytes 3080 | tf_op jit(solution)/shard_map/ppermute | solution.py:369
  120.3 19.3 %collective-permute-start.9 = (f32[4,2,640]{2,1,0:T(2,128)}, f32[4,2,640]{2,1,0:T(2,128)}, u32[]{:S(2)}, u32[]{:S(2)}) collective-permute-start(f32[4,2,640]{2,1,0:T(2,128)} %pad_maximum_fusion.7), channel_id=1, source_target_pairs={{0,1},{1,2},{2,3},{3,4},{4,5},{5,6},{6,7},{8,9},{9,10},{10,11},{11... | collective-permute-start | bytes 61448 | tf_op jit(solution)/shard_map/ppermute | solution.py:380
  122.2 3.4 %collective-permute-start.7 = (f32[4,2,640]{2,1,0:T(2,128)}, f32[4,2,640]{2,1,0:T(2,128)S(1)}, u32[]{:S(2)}, u32[]{:S(2)}) collective-permute-start(f32[4,2,640]{2,1,0:T(2,128)} %pad_maximum_fusion.7), channel_id=1, source_target_pairs={{0,24},{8,16},{16,8},{24,0},{1,25},{9,17},{17,9},{25,1},{2,26},{10... | collective-permute-start | bytes 61448 | tf_op jit(solution)/shard_map/ppermute | solution.py:382
  123.4 15.5 %collective-permute-start.8 = (f32[4,2,640]{2,1,0:T(2,128)}, f32[4,2,640]{2,1,0:T(2,128)}, u32[]{:S(2)}, u32[]{:S(2)}) collective-permute-start(f32[4,2,640]{2,1,0:T(2,128)} %pad_maximum_fusion.8), channel_id=1, source_target_pairs={{1,0},{2,1},{3,2},{4,3},{5,4},{6,5},{7,6},{9,8},{10,9},{11,10},{12... | collective-permute-start | bytes 61448 | tf_op jit(solution)/shard_map/ppermute | solution.py:381
  (6 other events, 6.0 us)

commit v2 on v1

--- a/solution.py
+++ b/solution.py
@@ -16,6 +16,7 @@
 
 LANES = 128
 GROUP = 8
+HALF = 256
 PAIR = 2
 VMEM_BYTES = 48 * 1024 * 1024
 CONTRACT_LAST = (((1,), (1,)), ((), ()))
@@ -40,21 +41,36 @@
 
 
 def two_terms(values):
-    high = values.astype(jnp.bfloat16).astype(jnp.float32)
-    return high, values - high
-
-
-def one_hot(places, count):
-    rows = lax.broadcasted_iota(jnp.int32, (count, places.shape[1]), 0)
-    return jnp.where(rows == places, 1.0, 0.0).astype(jnp.bfloat16)
-
-
-def spread(rows_of, terms, count):
-    rows = lax.broadcasted_iota(jnp.int32, (count, rows_of.shape[1]), 0)
-    hit = rows == rows_of
-    return jnp.concatenate([jnp.where(hit, term, 0.0) for term in terms], axis=0).astype(
-        jnp.bfloat16
-    )
+    high = values.astype(jnp.bfloat16)
+    return high, (values - high.astype(jnp.float32)).astype(jnp.bfloat16)
+
+
+def narrow(places):
+    return places.astype(jnp.float32).astype(jnp.bfloat16)
+
+
+def number_rows(numbers):
+    numbers[...] = narrow(lax.broadcasted_iota(jnp.int32, numbers.shape, 0))
+
+
+def one_hot(places, numbers):
+    return jnp.where(numbers == places, jnp.bfloat16(1), jnp.bfloat16(0))
+
+
+def spread(rows_of, terms, numbers):
+    hit = numbers == rows_of
+    return jnp.concatenate([jnp.where(hit, term, jnp.bfloat16(0)) for term in terms], axis=0)
+
+
+def halves_of(column, meridians):
+    return [
+        narrow(jnp.where(column // HALF == part, column % HALF, -1))
+        for part in range(meridians // HALF)
+    ]
+
+
+def wide_one_hot(parts, b, numbers):
+    return jnp.concatenate([one_hot(part[b : b + 1], numbers) for part in parts], axis=0)
 
 
 def picked_rows(rows_of, table, fields, count):
@@ -69,7 +85,7 @@
 
 
 def send_kernel(
-    capacity, subdomain, table, element, profile, share, out, home, tally, split_table
+    capacity, subdomain, table, element, profile, share, out, home, tally, split_table, numbers
 ):
     devices = tally.shape[0]
     blocks = element.shape[0]
@@ -80,21 +96,22 @@
         return carry
 
     lax.fori_loop(0, devices, clear, 0)
+    number_rows(numbers)
     out[...] = jnp.full(out.shape, -1.0, jnp.float32)
     high, low = two_terms(table[...])
-    split_table[:, :LANES] = high.astype(jnp.bfloat16)
-    split_table[:, LANES:] = low.astype(jnp.bfloat16)
+    split_table[:, :LANES] = high
+    split_table[:, LANES:] = low
 
     def group(g, carry):
         base = pl.multiple_of(g * GROUP, GROUP)
         cells = element[pl.ds(base, GROUP), :]
-        near = cells & (LANES - 1)
+        near = narrow(cells & (LANES - 1))
         far = cells >> 7
         address = profile[pl.ds(base, GROUP), :].astype(jnp.float32)
         weight = share[pl.ds(base, GROUP), :]
         for first in range(0, GROUP, PAIR):
             names = range(first, first + PAIR)
-            hot = jnp.concatenate([one_hot(near[b : b + 1], LANES) for b in names], axis=1)
+            hot = jnp.concatenate([one_hot(near[b : b + 1], numbers[...]) for b in names], axis=1)
             found = jnp.dot(
                 split_table[...],
                 jnp.concatenate([hot, hot], axis=0),
@@ -125,7 +142,19 @@
     )
 
 
-def land_kernel(capacity, parallels, meridians, counts, arrived, remapped, places, slots, values, total):
+def land_kernel(
+    capacity,
+    parallels,
+    meridians,
+    counts,
+    arrived,
+    remapped,
+    places,
+    slots,
+    values,
+    total,
+    numbers,
+):
     sources = counts.shape[0]
     last = slots.shape[0] - 1
     shift = meridians.bit_length() - 1
@@ -145,12 +174,15 @@
 
     filled = lax.fori_loop(0, sources, from_source, 0)
     slots[last] = filled
+    for extra in range(GROUP):
+        slots[filled + extra] = sources * (4 * capacity)
+    number_rows(numbers)
 
     def group(g, carry):
         base = pl.multiple_of(g * GROUP, GROUP)
         address = places[pl.ds(base, GROUP), :].astype(jnp.int32)
-        row = address >> shift
-        column = address & (meridians - 1)
+        row = narrow(address >> shift)
+        column = halves_of(address & (meridians - 1), meridians)
         split = [two_terms(values[field, pl.ds(base, GROUP), :]) for field in range(4)]
         terms = [split[field][term] for term in range(2) for field in range(4)]
         sums = None
@@ -158,12 +190,12 @@
             names = range(first, first + PAIR)
             left = jnp.concatenate(
                 [
-                    spread(row[b : b + 1], [term[b : b + 1] for term in terms], parallels)
+                    spread(row[b : b + 1], [term[b : b + 1] for term in terms], numbers[:parallels])
                     for b in names
                 ],
                 axis=1,
             )
-            right = jnp.concatenate([one_hot(column[b : b + 1], meridians) for b in names], axis=1)
+            right = jnp.concatenate([wide_one_hot(column, b, numbers[...]) for b in names], axis=1)
             part = lax.dot_general(
                 left, right, CONTRACT_LAST, preferred_element_type=jnp.float32
             )
@@ -176,53 +208,52 @@
     remapped[...] = total[:half] + total[half:]
 
 
-def pick_kernel(capacity, parallels, meridians, slots, surface, places, out, split_table):
+def pick_kernel(capacity, parallels, meridians, slots, surface, places, out, split_table, numbers, found_rows):
     last = slots.shape[0] - 1
     half = 4 * parallels
     shift = meridians.bit_length() - 1
     filled = slots[last]
     high, low = two_terms(surface[...])
-    split_table[:half] = high.astype(jnp.bfloat16)
-    split_table[half:] = low.astype(jnp.bfloat16)
-    out[...] = jnp.zeros(out.shape, jnp.float32)
+    split_table[:half] = high
+    split_table[half:] = low
+    found_rows[...] = jnp.zeros(found_rows.shape, jnp.float32)
+    number_rows(numbers)
 
     def group(g, carry):
         base = pl.multiple_of(g * GROUP, GROUP)
         address = places[pl.ds(base, GROUP), :].astype(jnp.int32)
         row = address >> shift
-        column = address & (meridians - 1)
+        column = halves_of(address & (meridians - 1), meridians)
         for first in range(0, GROUP, PAIR):
             names = range(first, first + PAIR)
-            hot = jnp.concatenate([one_hot(column[b : b + 1], meridians) for b in names], axis=1)
+            hot = jnp.concatenate([wide_one_hot(column, b, numbers[...]) for b in names], axis=1)
             found = jnp.dot(split_table[...], hot, preferred_element_type=jnp.float32)
             found = found[:half] + found[half:]
             wide_row = jnp.concatenate([row[b : b + 1] for b in names], axis=1)
             values = picked_rows(wide_row, found, 4, parallels)
             for turn, b in enumerate(names):
-
-                @pl.when(base + b < filled)
-                def _():
-                    target = slots[base + b]
-                    for field in range(4):
-                        out[pl.ds(target + field * capacity, 1), :] = values[field][
-                            :, turn * LANES : (turn + 1) * LANES
-                        ]
-
+                target = slots[base + b]
+                for field in range(4):
+                    found_rows[pl.ds(target + field * capacity, 1), :] = values[field][
+                        :, turn * LANES : (turn + 1) * LANES
+                    ]
         return carry
 
     lax.fori_loop(0, (filled + GROUP - 1) // GROUP, group, 0)
-
-
-def back_kernel(capacity, home, returned, element, share, out, total):
+    out[...] = found_rows[: out.shape[0]]
+
+
+def back_kernel(capacity, home, returned, element, share, out, total, numbers):
     blocks = element.shape[0]
     high_rows = out.shape[0] // 4
     total[...] = jnp.zeros(total.shape, jnp.float32)
+    number_rows(numbers)
 
     def group(g, carry):
         base = pl.multiple_of(g * GROUP, GROUP)
         cells = element[pl.ds(base, GROUP), :]
-        near = cells & (LANES - 1)
-        far = cells >> 7
+        near = narrow(cells & (LANES - 1))
+        far = narrow(cells >> 7)
         weight = share[pl.ds(base, GROUP), :]
         sums = None
         for first in range(0, GROUP, PAIR):
@@ -235,9 +266,9 @@
                     for field in range(4)
                 ]
                 terms = [split[field][term] for term in range(2) for field in range(4)]
-                lefts.append(spread(far[b : b + 1], terms, high_rows))
+                lefts.append(spread(far[b : b + 1], terms, numbers[:high_rows]))
             left = jnp.concatenate(lefts, axis=1)
-            right = jnp.concatenate([one_hot(near[b : b + 1], LANES) for b in names], axis=1)
+            right = jnp.concatenate([one_hot(near[b : b + 1], numbers[...]) for b in names], axis=1)
             part = lax.dot_general(
                 left, right, CONTRACT_LAST, preferred_element_type=jnp.float32
             )
@@ -250,7 +281,89 @@
     out[...] = total[:half] + total[half:]
 
 
-def ocean_kernel(
+def next_column(x):
+    return pltpu.roll(x, x.shape[1] - 1, axis=1)
+
+
+def next_row(x):
+    return pltpu.roll(x, x.shape[0] - 1, axis=0)
+
+
+def fill_wide(target, source, side, end):
+    rows, columns = source.shape[1:]
+    target[:, :rows, :columns] = source[...]
+    target[:, :rows, columns:] = side
+    target[:, rows:, :] = end
+
+
+def fill_opens(opens, top, ocean_mask, side, end):
+    rows, columns = ocean_mask.shape
+    opens[0, :rows, :columns] = ocean_mask[...].astype(jnp.float32)
+    opens[0, :rows, columns:] = side
+    opens[0, rows:, :] = end
+    here = opens[0]
+    opens[1] = here * next_column(here)
+    opens[2] = here * next_row(here)
+    row_ids = lax.broadcasted_iota(jnp.int32, here.shape, 0)
+    opens[3] = jnp.where((row_ids == rows - 1) & (top[0] == 1), 0.0, 1.0)
+
+
+def mixing_at(t, s, t_below, s_below, mask):
+    return (
+        mixing_base
+        + mixing_extra * jax.nn.sigmoid(4.0 * (density(t, s) - density(t_below, s_below)))
+    ) * mask
+
+
+def step(source, speeds, opens, first, stop, floor, keep, forcing=None):
+    source_t, source_s = source
+    east_all, north_all = speeds
+
+    def level(k, carry):
+        below = jnp.minimum(k + 1, floor)
+        t, s = source_t[k], source_s[k]
+        t_below, s_below = source_t[below], source_s[below]
+        mask = opens[0]
+        mixing = mixing_at(t, s, t_below, s_below, mask)
+        east_speed = east_all[k]
+        north_speed = north_all[k] * opens[3]
+        new_gains = []
+        for turn, (x, x_below) in enumerate(((t, t_below), (s, s_below))):
+            gradient = mixing * (x_below - x)
+            east_flux = face_flux(x, next_column(x), east_speed, opens[1])
+            north_flux = face_flux(x, next_row(x), north_speed, opens[2])
+            change = (
+                -(east_flux - pltpu.roll(east_flux, 1, axis=1))
+                - (north_flux - pltpu.roll(north_flux, 1, axis=0))
+                + (gradient - carry[turn])
+            )
+            if forcing is not None:
+                change = change + jnp.where(k == 0, forcing[turn], 0.0)
+            keep(turn, k, x + mask * change)
+            new_gains.append(gradient)
+        return tuple(new_gains)
+
+    if first == 0:
+        nothing = jnp.zeros(source_t.shape[1:], jnp.float32)
+        gains = (nothing, nothing)
+    else:
+        t, s, t_below, s_below = (x[k] for k in (first - 1, first) for x in source)
+        mixing = mixing_at(t, s, t_below, s_below, opens[0])
+        gains = (mixing * (t_below - t), mixing * (s_below - s))
+    lax.fori_loop(first, stop, level, gains)
+
+
+def turned(x):
+    back = LANES - 1 - lax.broadcasted_iota(jnp.int32, (x.shape[0], LANES), 1)
+    pieces = [
+        jnp.take_along_axis(x[:, at : at + LANES], back, axis=1, mode="promise_in_bounds")
+        for at in range(0, x.shape[1], LANES)
+    ]
+    return jnp.concatenate(pieces[-2::-1] + pieces[-1:], axis=1)
+
+
+def near_kernel(
+    depth,
     top,
     temper,
     saline,
@@ -261,7 +374,9 @@
     ends,
     remapped,
     remap_sides,
-    remap_ends,
+    from_north,
+    from_south,
+    folded,
     temper_out,
     saline_out,
     surface,
@@ -274,74 +389,31 @@
     remap_all,
     opens,
 ):
-    depth, rows, columns = temper.shape
-    all_rows, all_columns = first_t.shape[1:]
-
-    def fill(target, source, side, end):
-        target[:, :rows, :columns] = source[...]
-        target[:, :rows, columns:] = side
-        target[:, rows:, :] = end
-
+    levels, rows, columns = temper.shape
     for turn, (target, source) in enumerate(
         ((first_t, temper), (first_s, saline), (east_all, east), (north_all, north))
     ):
-        part = slice(turn * depth, (turn + 1) * depth)
-        fill(target, source, sides[part], ends[part])
-    fill(remap_all, remapped, remap_sides[...], remap_ends[...])
-    opens[0, :rows, :columns] = ocean_mask[...].astype(jnp.float32)
-    opens[0, :rows, columns:] = sides[4 * depth]
-    opens[0, rows:, :] = ends[4 * depth]
-
-    def next_column(x):
-        return pltpu.roll(x, all_columns - 1, axis=1)
-
-    def next_row(x):
-        return pltpu.roll(x, all_rows - 1, axis=0)
-
-    here = opens[0]
-    opens[1] = here * next_column(here)
-    opens[2] = here * next_row(here)
-    row_ids = lax.broadcasted_iota(jnp.int32, (all_rows, all_columns), 0)
-    opens[3] = jnp.where((row_ids == rows - 1) & (top[0] == 1), 0.0, 1.0)
+        part = slice(turn * depth, turn * depth + levels)
+        fill_wide(target, source, sides[part], ends[part])
+    fill_opens(opens, top, ocean_mask, sides[4 * depth], ends[4 * depth])
+    upper = lax.broadcasted_iota(jnp.int32, (8, columns + LANES), 0)
+    remap_all[:, :rows, :columns] = remapped[...]
+    remap_all[:, :rows, columns:] = remap_sides[...]
+    for field in range(4):
+        across = turned(folded[field])
+        if field == 2:
+            across = -next_column(across)
+        last_row, row_before = across[7:8], across[6:7]
+        if field == 3:
+            last_row, row_before = -row_before, -row_before
+        across = jnp.where(upper == 0, last_row, row_before)
+        above = jnp.where(top[0] == 1, across, from_north[field])
+        remap_all[field, rows:, :] = jnp.where(upper < 4, above, from_south[field])
     east_all[0] = east_all[0] + stress_factor * remap_all[2]
     north_all[0] = north_all[0] + stress_factor * remap_all[3]
     remap_all[0] = heat_factor * remap_all[0]
     remap_all[1] = fresh_factor * remap_all[1]
-
-    def step(source_t, source_s, keep):
-        def level(k, carry):
-            gain_t, gain_s = carry
-            below = jnp.minimum(k + 1, depth - 1)
-            t, s = source_t[k], source_s[k]
-            t_below, s_below = source_t[below], source_s[below]
-            mask = opens[0]
-            mixing = (
-                mixing_base
-                + mixing_extra
-                * jax.nn.sigmoid(4.0 * (density(t, s) - density(t_below, s_below)))
-            ) * mask
-            east_speed = east_all[k]
-            north_speed = north_all[k] * opens[3]
-            new_gains = []
-            for x, x_below, gain, target, forcing in (
-                (t, t_below, gain_t, 0, 0),
-                (s, s_below, gain_s, 1, 1),
-            ):
-                gradient = mixing * (x_below - x)
-                east_flux = face_flux(x, next_column(x), east_speed, opens[1])
-                north_flux = face_flux(x, next_row(x), north_speed, opens[2])
-                change = (
-                    -(east_flux - pltpu.roll(east_flux, 1, axis=1))
-                    - (north_flux - pltpu.roll(north_flux, 1, axis=0))
-                    + (gradient - gain)
-                )
-                change = change + jnp.where(k == 0, remap_all[forcing], 0.0)
-                keep(target, k, x + mask * change)
-                new_gains.append(gradient)
-            return tuple(new_gains)
-
-        nothing = jnp.zeros((all_rows, all_columns), jnp.float32)
-        lax.fori_loop(0, depth, level, (nothing, nothing))
+    forcing = (remap_all[0], remap_all[1])
 
     def keep_first(target, k, value):
         (second_t, second_s)[target][k] = value
@@ -349,15 +421,58 @@
     def keep_last(target, k, value):
         (temper_out, saline_out)[target][k] = value[:rows, :columns]
 
-    step(first_t, first_s, keep_first)
-    step(second_t, second_s, keep_last)
-
+    speeds = (east_all, north_all)
+    step((first_t, first_s), speeds, opens, 0, levels - 1, levels - 1, keep_first, forcing)
+    step((second_t, second_s), speeds, opens, 0, levels - 2, levels - 1, keep_last, forcing)
     mask = opens[0, :rows, :columns]
     t, s = temper_out[0], saline_out[0]
     surface[0] = t * mask
     surface[1] = s * mask
     surface[2] = density(t, s) * mask
     surface[3] = east_all[0, :rows, :columns] * mask
+
+
+def deep_kernel(
+    top,
+    temper,
+    saline,
+    east,
+    north,
+    ocean_mask,
+    sides,
+    ends,
+    temper_near,
+    saline_near,
+    temper_out,
+    saline_out,
+    first_t,
+    first_s,
+    second_t,
+    second_s,
+    east_all,
+    north_all,
+    opens,
+):
+    depth, rows, columns = temper.shape
+    near = temper_near.shape[0]
+    for turn, (target, source) in enumerate(
+        ((first_t, temper), (first_s, saline), (east_all, east), (north_all, north))
+    ):
+        part = slice(turn * depth, (turn + 1) * depth)
+        fill_wide(target, source, sides[part], ends[part])
+    fill_opens(opens, top, ocean_mask, sides[4 * depth], ends[4 * depth])
+    temper_out[:near] = temper_near[...]
+    saline_out[:near] = saline_near[...]
+
+    def keep_first(target, k, value):
+        (second_t, second_s)[target][k] = value
+
+    def keep_last(target, k, value):
+        (temper_out, saline_out)[target][k] = value[:rows, :columns]
+
+    speeds = (east_all, north_all)
+    step((first_t, first_s), speeds, opens, near - 1, depth, depth - 1, keep_first)
+    step((second_t, second_s), speeds, opens, near, depth, depth - 1, keep_last)
 
 
 def halo(parts, east_at, north_at):
@@ -394,6 +509,25 @@
         [above, jnp.zeros((channels, 4, columns + LANES), jnp.float32), from_south], axis=1
     )
     return sides, ends
+
+
+def tile_halo(x):
+    rows, columns = x.shape[1:]
+    count_gx, count_gy = lax.axis_size("gx"), lax.axis_size("gy")
+    from_west = lax.ppermute(
+        x[:, :, -LANES:], "gx", [(i, (i + 1) % count_gx) for i in range(count_gx)]
+    )
+    from_east = lax.ppermute(
+        x[:, :, :LANES], "gx", [((i + 1) % count_gx, i) for i in range(count_gx)]
+    )
+    lane = lax.broadcasted_iota(jnp.int32, from_west.shape, 2)
+    sides = jnp.where(lane < LANES // 2, from_east, from_west)
+    low = jnp.concatenate([x[:, :8], sides[:, :8]], axis=2)
+    high = jnp.concatenate([x[:, -8:], sides[:, -8:]], axis=2)
+    from_south = lax.ppermute(high, "gy", [(i, i + 1) for i in range(count_gy - 1)])
+    from_north = lax.ppermute(low, "gy", [(i + 1, i) for i in range(count_gy - 1)])
+    folded = lax.ppermute(high, "gx", [(i, count_gx - 1 - i) for i in range(count_gx)])
+    return sides, from_north, from_south, folded
 
 
 def body(
@@ -430,6 +564,7 @@
         scratch_shapes=[
             pltpu.SMEM((devices,), jnp.int32),
             pltpu.VMEM((table.shape[0], 2 * LANES), jnp.bfloat16),
+            pltpu.VMEM((LANES, LANES), jnp.bfloat16),
         ],
         **gather_kernel_params(10**9),
     )(
@@ -439,8 +574,25 @@
         overlay_sea_profile,
         overlay_fraction_share,
     )
+
+    (
+        outgoing,
+        thermal_deviation,
+        saltiness_deviation,
+        zonal_interface_speed,
+        poleward_interface_speed,
+        sea_profile_indicator,
+    ) = lax.optimization_barrier(
+        (
+            outgoing,
+            thermal_deviation,
+            saltiness_deviation,
+            zonal_interface_speed,
+            poleward_interface_speed,
+            sea_profile_indicator,
+        )
+    )
     arrived = lax.all_to_all(outgoing, ("gx", "gy"), split_axis=0, concat_axis=0, tiled=True)
-
     ocean_mask = sea_profile_indicator.astype(f32)
     sides, ends = halo(
         [
@@ -462,28 +614,68 @@
         out_shape=(
             jax.ShapeDtypeStruct((4 * parallels, meridians), f32),
             jax.ShapeDtypeStruct((slot_count + GROUP, LANES), f32),
-            jax.ShapeDtypeStruct((slot_count + 1,), jnp.int32),
+            jax.ShapeDtypeStruct((slot_count + GROUP + 1,), jnp.int32),
         ),
         in_specs=[SMEM, VMEM],
         out_specs=(VMEM, VMEM, SMEM),
         scratch_shapes=[
             pltpu.VMEM((4, slot_count + GROUP, LANES), f32),
             pltpu.VMEM((8 * parallels, meridians), f32),
+            pltpu.VMEM((HALF, LANES), jnp.bfloat16),
         ],
         **gather_kernel_params(2 * 10**10),
     )(counts, arrived)
     remapped = remapped.reshape(4, parallels, meridians)
-    remap_sides, remap_ends = halo([remapped], (2, 3), (3, 4))
+    around = tile_halo(remapped)
 
     top = (lax.axis_index("gy") == lax.axis_size("gy") - 1).astype(jnp.int32).reshape(1)
     wide = (parallels + 8, meridians + LANES)
+    near, levels = 2, 4
+    first_levels = pl.BlockSpec((levels, parallels, meridians), lambda i: (0, 0, 0))
     cube = jax.ShapeDtypeStruct((depth, parallels, meridians), f32)
-    temper, saline, surface = pl.pallas_call(
-        ocean_kernel,
-        out_shape=(cube, cube, jax.ShapeDtypeStruct((4, parallels, meridians), f32)),
-        in_specs=[SMEM] + [VMEM] * 10,
+    slab = jax.ShapeDtypeStruct((near, parallels, meridians), f32)
+    temper_near, saline_near, surface = pl.pallas_call(
+        functools.partial(near_kernel, depth),
+        grid=(1,),
+        out_shape=(slab, slab, jax.ShapeDtypeStruct((4, parallels, meridians), f32)),
+        in_specs=[SMEM] + [first_levels] * 4 + [VMEM] * 8,
         out_specs=(VMEM, VMEM, VMEM),
-        scratch_shapes=[pltpu.VMEM((depth,) + wide, f32)] * 6 + [pltpu.VMEM((4,) + wide, f32)] * 2,
+        scratch_shapes=[pltpu.VMEM((levels,) + wide, f32)] * 6
+        + [pltpu.VMEM((4,) + wide, f32)] * 2,
+        **gather_kernel_params(10**8),
+    )(
+        top,
+        thermal_deviation,
+        saltiness_deviation,
+        zonal_interface_speed,
+        poleward_interface_speed,
+        sea_profile_indicator,
+        sides,
+        ends,
+        remapped,
+        *around,
+    )
+
+    picked = pl.pallas_call(
+        functools.partial(pick_kernel, capacity, parallels, meridians),
+        out_shape=jax.ShapeDtypeStruct((slot_count * 4, LANES), f32),
+        in_specs=[SMEM, VMEM, VMEM],
+        out_specs=VMEM,
+        scratch_shapes=[
+            pltpu.VMEM((8 * parallels, meridians), jnp.bfloat16),
+            pltpu.VMEM((HALF, LANES), jnp.bfloat16),
+            pltpu.VMEM(((slot_count + capacity) * 4, LANES), f32),
+        ],
+        **gather_kernel_params(2 * 10**10),
+    )(slots, surface.reshape(4 * parallels, meridians), places)
+    picked, top = lax.optimization_barrier((picked, top))
+    returned = lax.all_to_all(picked, ("gx", "gy"), split_axis=0, concat_axis=0, tiled=True)
+    temper, saline = pl.pallas_call(
+        deep_kernel,
+        out_shape=(cube, cube),
+        in_specs=[SMEM] + [VMEM] * 9,
+        out_specs=(VMEM, VMEM),
+        scratch_shapes=[pltpu.VMEM((depth,) + wide, f32)] * 6 + [pltpu.VMEM((4,) + wide, f32)],
         **gather_kernel_params(10**9),
     )(
         top,
@@ -494,26 +686,18 @@
         sea_profile_indicator,
         sides,
         ends,
-        remapped,
-        remap_sides,
-        remap_ends,
-    )
-
-    picked = pl.pallas_call(
-        functools.partial(pick_kernel, capacity, parallels, meridians),
-        out_shape=jax.ShapeDtypeStruct((slot_count * 4, LANES), f32),
-        in_specs=[SMEM, VMEM, VMEM],
-        out_specs=VMEM,
-        scratch_shapes=[pltpu.VMEM((8 * parallels, meridians), jnp.bfloat16)],
-        **gather_kernel_params(2 * 10**10),
-    )(slots, surface.reshape(4 * parallels, meridians), places)
-    returned = lax.all_to_all(picked, ("gx", "gy"), split_axis=0, concat_axis=0, tiled=True)
+        temper_near,
+        saline_near,
+    )
     back_fields = pl.pallas_call(
         functools.partial(back_kernel, capacity),
         out_shape=jax.ShapeDtypeStruct((4 * atm_cells // LANES, LANES), f32),
         in_specs=[SMEM, VMEM, VMEM, VMEM],
         out_specs=VMEM,
-        scratch_shapes=[pltpu.VMEM((8 * atm_cells // LANES, LANES), f32)],
+        scratch_shapes=[
+            pltpu.VMEM((8 * atm_cells // LANES, LANES), f32),
+            pltpu.VMEM((LANES, LANES), jnp.bfloat16),
+        ],
         **gather_kernel_params(2 * 10**9),
     )(home, returned, overlay_air_element, overlay_fraction_share)
     return temper, saline, back_fields.reshape(4, atm_cells)

time: 284 us -> 232 us (0.82)
  Pallas kernels: 151 us -> 74.1 us
  blocking collectives: 33 us -> 0 us
  starting transfers between devices: 20.5 us -> 51.5 us
  local copies, waits for them, and re-layouts: 40 us -> 59.4 us
  waiting for transfers between devices: 13.4 us -> 32.5 us
  other arithmetic: 21.7 us -> 12 us
    pallas_call x1, Pallas kernels: 76.9 us -> 15.2 us  [body(): pl.pallas_call(functools.partial(pick_kernel, capacity, parallels, meridi...]
    all_to_all x1 -> x0, blocking collectives: 33 us -> none  [body(): lax.all_to_all(picked, ('gx', 'gy'), split_axis=0, concat_axis=0, tiled=T...]
    optimization_barrier x0 -> x4, local copies, waits for them, and re-layouts: none -> 32.4 us  [body(): lax.optimization_barrier((outgoing, thermal_deviation, saltiness_deviatio...]
    all_to_all x0 -> x1, starting transfers between devices: none -> 20.8 us  [body(): lax.all_to_all(picked, ('gx', 'gy'), split_axis=0, concat_axis=0, tiled=T...]
    pallas_call x1, Pallas kernels: 37.4 us -> 19.5 us  [body(): pl.pallas_call(functools.partial(land_kernel, capacity, parallels, meridi...]
    ppermute x0 -> x5, waiting for transfers between devices: none -> 16.5 us  [the longest x1 10.9 us: tile_halo(): lax.ppermute(x[:, :, -LANES:], 'gx', [(i, (i + 1) % count_gx) for i in ra...]
    ppermute x0 -> x5, starting transfers between devices: none -> 15.9 us  [the longest x1 13.9 us: tile_halo(): lax.ppermute(high, 'gy', [(i, i + 1) for i in range(count_gy - 1)])]
    all_to_all x0 -> x1, waiting for transfers between devices: none -> 8.3 us  [body(): lax.all_to_all(picked, ('gx', 'gy'), split_axis=0, concat_axis=0, tiled=T...]
  transfers between devices with their start and end apart: 11 -> 12, of which waited for: 6 -> 6; matrix products, arithmetic and copies ran while one was open for 15% -> 26% of each run, Pallas kernels for 4% -> 16%
where the time goes in v2:
time: 232 us; the launch traced here: 231 us
  Pallas kernels  74.1 us (32%)
  local copies, waits for them, and re-layouts  59.4 us (26%)
  starting transfers between devices  51.5 us (22%)
  waiting for transfers between devices  32.5 us (14%)
  other arithmetic  12 us (5%)
    optimization_barrier x4, local copies, waits for them, and re-layouts, body(): lax.optimization_barrier((outgoing, thermal_deviation, saltiness_deviatio...  32.4 us
    all_to_all x1, starting transfers between devices, body(): lax.all_to_all(picked, ('gx', 'gy'), split_axis=0, concat_axis=0, tiled=T...  20.8 us
    pallas_call x1, Pallas kernels, body(): pl.pallas_call(functools.partial(land_kernel, capacity, parallels, meridi...  19.5 us
    pallas_call x1, Pallas kernels, body(): pl.pallas_call(deep_kernel, out_shape=(cube, cube), in_specs=[SMEM] + [VM...  16.6 us
    pallas_call x1, Pallas kernels, body(): pl.pallas_call(functools.partial(pick_kernel, capacity, parallels, meridi...  15.2 us
    ppermute x1, starting transfers between devices, tile_halo(): lax.ppermute(high, 'gy', [(i, i + 1) for i in range(count_gy - 1)])  13.9 us
    unnamed x36, local copies, waits for them, and re-layouts  11.6 us
    ppermute x1, waiting for transfers between devices, tile_halo(): lax.ppermute(x[:, :, -LANES:], 'gx', [(i, (i + 1) % count_gx) for i in ra...  10.9 us
  transfers between devices with their start and end apart: 12, of which 6 were waited for; matrix products, arithmetic and copies ran while one was open for 26% of the time, Pallas kernels for 16%

profile of v2, /device:TPU:0, one launch (start us, length us, event | category | flops | bytes accessed | tf_op | source)
XLA Modules:
  0.0 230.5 jit_solution(198910657826998901)
XLA Ops:
  6.1 8.9 %shard_map.121 = (f32[2560,128]{1,0:T(8,128)S(1)}, s32[256]{0:T(256)S(1)}) custom-call(s32[256]{0:T(256)S(1)} %bitcast.17, f32[64,128]{1,0:T(8,128)S(1)} %reshape.38.table, s32[256,128]{1,0:T(8,128)S(1)} %copy-done.9, s32[256,128]{1,0:T(8,128)S(1)} %copy-done.8, f32[256,128]{1,0:T(8,128)S(1)} %copy-done.11), custom_call_target="tpu_custom_call" | custom-call | flops 1000000000 | bytes 4000000 | tf_op jit(solution)/shard_map/pallas_call | solution.py:556
  16.0 7.4 %all-to-all-start = ((f32[32,80,128]{2,1,0:T(8,128)}), f32[32,80,128]{2,1,0:T(8,128)}, u32[]{:S(2)}, u32[]{:S(2)}) async-start(f32[32,80,128]{2,1,0:T(8,128)} %bitcast.11), calls=%async_computation | async-start | bytes 2621440 | tf_op jit(solution)/shard_map/all_to_all | solution.py:595
  23.4 7.8 %copy.14 = f32[20,32,512]{0,1,2:T(8,128)} copy(f32[20,32,512]{2,1,0:T(8,128)S(1)} %copy-done.1) | data formatting | bytes 2621440 | tf_op jit(solution)/shard_map/optimization_barrier | solution.py:585
  31.2 7.6 %copy.13 = f32[20,32,512]{0,1,2:T(8,128)} copy(f32[20,32,512]{2,1,0:T(8,128)S(1)} %copy-done) | data formatting | bytes 2621440 | tf_op jit(solution)/shard_map/optimization_barrier | solution.py:585
  38.8 8.5 %copy.16 = f32[20,32,512]{0,1,2:T(8,128)} copy(f32[20,32,512]{2,1,0:T(8,128)} %north.1) | data formatting | bytes 2621440 | tf_op jit(solution)/shard_map/optimization_barrier | solution.py:585
  47.4 8.5 %copy.15 = f32[20,32,512]{0,1,2:T(8,128)} copy(f32[20,32,512]{2,1,0:T(8,128)} %east.1) | data formatting | bytes 2621440 | tf_op jit(solution)/shard_map/optimization_barrier | solution.py:585
  64.0 3.0 %copy.24 = f32[81,32,2]{2,1,0:T(8,128)} copy(f32[81,32,2]{0,1,2:T(8,128)} %collective-permute-done.1) | data formatting | bytes 41472 | tf_op jit(solution)/shard_map/ppermute | solution.py:484
  67.0 2.1 copy.23
  69.1 2.1 pad_maximum_fusion.1.sides
  73.6 4.2 %collective-permute-start.4 = (f32[81,2,640]{2,1,0:T(2,128)}, f32[81,2,640]{2,1,0:T(2,128)}, u32[]{:S(2)}, u32[]{:S(2)}) collective-permute-start(f32[81,2,640]{2,1,0:T(2,128)} %pad_maximum_fusion.2), channel_id=1, source_target_pairs={{0,1},{1,2},{2,3},{3,4},{4,5},{5,6},{6,7},{8,9},{9,10},{10,11},{11... | collective-permute-start | bytes 1244168 | tf_op jit(solution)/shard_map/ppermute | solution.py:495
  80.0 5.2 %collective-permute-done.2 = f32[81,2,640]{2,1,0:T(2,128)} collective-permute-done((f32[81,2,640]{2,1,0:T(2,128)}, f32[81,2,640]{2,1,0:T(2,128)}, u32[]{:S(2)}, u32[]{:S(2)}) %collective-permute-start.2) | collective-permute-done | bytes 414752 | tf_op jit(solution)/shard_map/ppermute | solution.py:497
  90.6 2.5 %collective-permute-done.3 = f32[81,2,640]{2,1,0:T(2,128)} collective-permute-done((f32[81,2,640]{2,1,0:T(2,128)}, f32[81,2,640]{2,1,0:T(2,128)}, u32[]{:S(2)}, u32[]{:S(2)}) %collective-permute-start.3) | collective-permute-done | bytes 414752 | tf_op jit(solution)/shard_map/ppermute | solution.py:496
  93.0 2.0 fusion.2
  96.7 19.5 %shard_map.122 = (f32[128,512]{1,0:T(8,128)S(1)}, f32[520,128]{1,0:T(8,128)S(1)}, s32[521]{0:T(1024)S(1)}) custom-call(s32[32]{0:T(128)S(1)} %convert_reduce_fusion.counts, f32[2560,128]{1,0:T(8,128)} %bitcast.3.arrived), custom_call_target="tpu_custom_call" | custom-call | flops 20000000000 | bytes 4000000 | tf_op jit(solution)/shard_map/pallas_call | solution.py:612
  118.2 10.9 %collective-permute-done.6 = f32[4,32,128]{2,1,0:T(8,128)S(1)} collective-permute-done((f32[4,32,128]{2,1,0:T(8,128)S(1)}, f32[4,32,128]{2,1,0:T(8,128)S(1)}, u32[]{:S(2)}, u32[]{:S(2)}) %collective-permute-start.6) | collective-permute-done | bytes 65568 | tf_op jit(solution)/shard_map/ppermute | solution.py:517
  129.2 13.9 %collective-permute-start.8 = (f32[4,8,640]{2,1,0:T(8,128)S(1)}, f32[4,8,640]{2,1,0:T(8,128)S(1)}, u32[]{:S(2)}, u32[]{:S(2)}) collective-permute-start(f32[4,8,640]{2,1,0:T(8,128)S(1)} %pad_maximum_fusion.5), channel_id=1, source_target_pairs={{0,1},{1,2},{2,3},{3,4},{4,5},{5,6},{6,7},{8,9},{9,10},{10,11},{11... | collective-permute-start | bytes 245768 | tf_op jit(solution)/shard_map/ppermute | solution.py:527
  144.7 2.6 %pad_maximum_fusion.ends = f32[81,8,640]{2,1,0:T(8,128)} fusion(f32[81,2,640]{2,1,0:T(2,128)} %collective-permute-done.4, f32[81,2,640]{2,1,0:T(2,128)S(1)} %copy-done.15, f32[8]{0:T(128)S(1)} %pad.5.clone), kind=kLoop, calls=%fused_computation | loop fusion | flops 829440 | bytes 2488352 | tf_op jit(solution)/shard_map/concatenate | solution.py:508
  147.2 4.1 %collective-permute-done.7.from_north = f32[4,8,640]{2,1,0:T(8,128)S(1)} collective-permute-done((f32[4,8,640]{2,1,0:T(8,128)S(1)}, f32[4,8,640]{2,1,0:T(8,128)S(1)}, u32[]{:S(2)}, u32[]{:S(2)}) %collective-permute-start.7) | collective-permute-done | bytes 81952 | tf_op jit(solution)/shard_map/ppermute | solution.py:528
  151.4 4.0 %shard_map.123 = (f32[2,32,512]{2,1,0:T(8,128)S(1)}, f32[2,32,512]{2,1,0:T(8,128)S(1)}, f32[4,32,512]{2,1,0:T(8,128)S(1)}) custom-call(s32[1]{0:T(128)} %bitcast.4.top, f32[20,32,512]{2,1,0:T(8,128)S(1)} %copy-done, f32[20,32,512]{2,1,0:T(8,128)S(1)} %copy-done.1, f32[20,32,512]{2,1,0:T(8,128)S(1)} %copy-done.2, f32[20,32,512]{2,1,0:T(8,128)} %north.1, ...), custom_call_target="tpu_custom_call" | custom-call | flops 100000000 | bytes 4000000 | tf_op jit(solution)/shard_map/pallas_call | solution.py:637
  155.4 15.2 %shard_map.124 = f32[2048,128]{1,0:T(8,128)S(1)} custom-call(s32[521]{0:T(1024)S(1)} %get-tuple-element.23.slots, f32[128,512]{1,0:T(8,128)S(1)} %bitcast.16, f32[520,128]{1,0:T(8,128)S(1)} %get-tuple-element.31.places), custom_call_target="tpu_custom_call" | custom-call | flops 20000000000 | bytes 4000000 | tf_op jit(solution)/shard_map/pallas_call | solution.py:659
  171.6 20.8 %all-to-all-start.1 = ((f32[32,64,128]{2,1,0:T(8,128)}), f32[32,64,128]{2,1,0:T(8,128)}, u32[]{:S(2)}, u32[]{:S(2)}) async-start(f32[32,64,128]{2,1,0:T(8,128)} %bitcast.15), calls=%async_computation.1 | async-start | bytes 2097152 | tf_op jit(solution)/shard_map/all_to_all | solution.py:672
  195.1 16.6 %shard_map.125 = (f32[20,32,512]{2,1,0:T(8,128)}, f32[20,32,512]{2,1,0:T(8,128)}) custom-call(s32[1]{0:T(128)} %bitcast.4.top, f32[20,32,512]{2,1,0:T(8,128)S(1)} %copy-done, f32[20,32,512]{2,1,0:T(8,128)S(1)} %copy-done.1, f32[20,32,512]{2,1,0:T(8,128)S(1)} %copy-done.3, f32[20,32,512]{2,1,0:T(8,128)S(1)} %copy-done.4, s32[32,512]{1,0:T(8,128)S(1)} %copy-done.7, ...), custom_call_target="tpu_custom_call" | custom-call | flops 1000000000 | bytes 4000000 | tf_op jit(solution)/shard_map/pallas_call | solution.py:673
  211.7 8.3 %all-to-all-done.1 = f32[32,64,128]{2,1,0:T(8,128)} async-done(((f32[32,64,128]{2,1,0:T(8,128)}), f32[32,64,128]{2,1,0:T(8,128)}, u32[]{:S(2)}, u32[]{:S(2)}) %all-to-all-start.1) | async-done | bytes 1048608 | tf_op jit(solution)/shard_map/all_to_all | solution.py:672
  220.0 9.9 %shard_map.126 = f32[64,128]{1,0:T(8,128)S(1)} custom-call(s32[256]{0:T(256)S(1)} %get-tuple-element.37.home, f32[2048,128]{1,0:T(8,128)} %bitcast.9.returned, s32[256,128]{1,0:T(8,128)S(1)} %copy-done.10, f32[256,128]{1,0:T(8,128)S(1)} %copy-done.12), custom_call_target="tpu_custom_call" | custom-call | flops 2000000000 | bytes 4000000 | tf_op jit(solution)/shard_map/pallas_call | solution.py:692
  (91 shorter events, 33.8 us)
Async XLA Ops:
  14.9 1.1 copy-start.5
  16.0 7.4 %copy-start.1 = (f32[20,32,512]{2,1,0:T(8,128)S(1)}, f32[20,32,512]{2,1,0:T(8,128)}, u32[]{:S(2)}) copy-start(f32[20,32,512]{2,1,0:T(8,128)} %saline.1) | copy-start | bytes 3932164
  16.0 79.1 %all-to-all-start = ((f32[32,80,128]{2,1,0:T(8,128)}), f32[32,80,128]{2,1,0:T(8,128)}, u32[]{:S(2)}, u32[]{:S(2)}) async-start(f32[32,80,128]{2,1,0:T(8,128)} %bitcast.11), calls=%async_computation | async-start | bytes 2621440 | tf_op jit(solution)/shard_map/all_to_all | solution.py:595
  23.4 7.8 %copy-start = (f32[20,32,512]{2,1,0:T(8,128)S(1)}, f32[20,32,512]{2,1,0:T(8,128)}, u32[]{:S(2)}) copy-start(f32[20,32,512]{2,1,0:T(8,128)} %temper.1) | copy-start | bytes 3932164
  47.4 8.5 %copy-start.7 = (s32[32,512]{1,0:T(8,128)S(1)}, s32[32,512]{1,0:T(8,128)}, u32[]{:S(2)}) copy-start(s32[32,512]{1,0:T(8,128)} %ocean_mask.1) | copy-start | bytes 196612
  58.6 5.3 %collective-permute-start.1 = (f32[81,32,2]{0,1,2:T(8,128)}, f32[81,32,2]{0,1,2:T(8,128)}, u32[]{:S(2)}, u32[]{:S(2)}) collective-permute-start(f32[81,32,2]{0,1,2:T(8,128)} %concatenate.43), channel_id=1, source_target_pairs={{0,8},{8,16},{16,24},{24,0},{1,9},{9,17},{17,25},{25,1},{2,10},{10... | collective-permute-start | bytes 62216 | tf_op jit(solution)/shard_map/ppermute | solution.py:484
  59.9 7.1 %collective-permute-start = (f32[81,32,2]{0,1,2:T(8,128)}, f32[81,32,2]{0,1,2:T(8,128)S(1)}, u32[]{:S(2)}, u32[]{:S(2)}) collective-permute-start(f32[81,32,2]{0,1,2:T(8,128)} %concatenate.42), channel_id=1, source_target_pairs={{8,0},{16,8},{24,16},{0,24},{9,1},{17,9},{25,17},{1,25},{10,2},{18... | collective-permute-start | bytes 62216 | tf_op jit(solution)/shard_map/ppermute | solution.py:485
  71.2 1.1 copy-start.14
  73.3 11.9 %collective-permute-start.2 = (f32[81,2,640]{2,1,0:T(2,128)}, f32[81,2,640]{2,1,0:T(2,128)}, u32[]{:S(2)}, u32[]{:S(2)}) collective-permute-start(f32[81,2,640]{2,1,0:T(2,128)} %pad_maximum_fusion.2), channel_id=1, source_target_pairs={{0,24},{8,16},{16,8},{24,0},{1,25},{9,17},{17,9},{25,1},{2,26},{10... | collective-permute-start | bytes 1244168 | tf_op jit(solution)/shard_map/ppermute | solution.py:497
  73.6 71.0 %collective-permute-start.4 = (f32[81,2,640]{2,1,0:T(2,128)}, f32[81,2,640]{2,1,0:T(2,128)}, u32[]{:S(2)}, u32[]{:S(2)}) collective-permute-start(f32[81,2,640]{2,1,0:T(2,128)} %pad_maximum_fusion.2), channel_id=1, source_target_pairs={{0,1},{1,2},{2,3},{3,4},{4,5},{5,6},{6,7},{8,9},{9,10},{10,11},{11... | collective-permute-start | bytes 1244168 | tf_op jit(solution)/shard_map/ppermute | solution.py:495
  78.7 14.3 %collective-permute-start.3 = (f32[81,2,640]{2,1,0:T(2,128)}, f32[81,2,640]{2,1,0:T(2,128)}, u32[]{:S(2)}, u32[]{:S(2)}) collective-permute-start(f32[81,2,640]{2,1,0:T(2,128)} %pad_maximum_fusion.3), channel_id=1, source_target_pairs={{1,0},{2,1},{3,2},{4,3},{5,4},{6,5},{7,6},{9,8},{10,9},{11,10},{12... | collective-permute-start | bytes 1244168 | tf_op jit(solution)/shard_map/ppermute | solution.py:496
  116.2 28.4 %copy-start.15 = (f32[81,2,640]{2,1,0:T(2,128)S(1)}, f32[81,2,640]{2,1,0:T(2,128)}, u32[]{:S(2)}) copy-start(f32[81,2,640]{2,1,0:T(2,128)} %fusion.2) | copy-start | bytes 1244164
  116.3 2.0 collective-permute-start.5
  116.3 12.8 %collective-permute-start.6 = (f32[4,32,128]{2,1,0:T(8,128)S(1)}, f32[4,32,128]{2,1,0:T(8,128)S(1)}, u32[]{:S(2)}, u32[]{:S(2)}) collective-permute-start(f32[4,32,128]{2,1,0:T(8,128)S(1)} %get-tuple-element.61), channel_id=1, source_target_pairs={{0,8},{8,16},{16,24},{24,0},{1,9},{9,17},{17,25},{25,1},{2,10},{10... | collective-permute-start | bytes 196616 | tf_op jit(solution)/shard_map/ppermute | solution.py:517
  129.2 22.2 %collective-permute-start.8 = (f32[4,8,640]{2,1,0:T(8,128)S(1)}, f32[4,8,640]{2,1,0:T(8,128)S(1)}, u32[]{:S(2)}, u32[]{:S(2)}) collective-permute-start(f32[4,8,640]{2,1,0:T(8,128)S(1)} %pad_maximum_fusion.5), channel_id=1, source_target_pairs={{0,1},{1,2},{2,3},{3,4},{4,5},{5,6},{6,7},{8,9},{9,10},{10,11},{11... | collective-permute-start | bytes 245768 | tf_op jit(solution)/shard_map/ppermute | solution.py:527
  143.1 8.3 %collective-permute-start.9 = (f32[4,8,640]{2,1,0:T(8,128)S(1)}, f32[4,8,640]{2,1,0:T(8,128)S(1)}, u32[]{:S(2)}, u32[]{:S(2)}) collective-permute-start(f32[4,8,640]{2,1,0:T(8,128)S(1)} %pad_maximum_fusion.5), channel_id=1, source_target_pairs={{0,24},{8,16},{16,8},{24,0},{1,25},{9,17},{17,9},{25,1},{2,26},{10... | collective-permute-start | bytes 245768 | tf_op jit(solution)/shard_map/ppermute | solution.py:529
  143.2 8.2 %copy-start.2 = (f32[20,32,512]{2,1,0:T(8,128)S(1)}, f32[20,32,512]{2,1,0:T(8,128)}, u32[]{:S(2)}) copy-start(f32[20,32,512]{2,1,0:T(8,128)} %east.1) | copy-start | bytes 3932164
  143.2 8.2 %collective-permute-start.7 = (f32[4,8,640]{2,1,0:T(8,128)S(1)}, f32[4,8,640]{2,1,0:T(8,128)S(1)}, u32[]{:S(2)}, u32[]{:S(2)}) collective-permute-start(f32[4,8,640]{2,1,0:T(8,128)S(1)} %pad_maximum_fusion.4), channel_id=1, source_target_pairs={{1,0},{2,1},{3,2},{4,3},{5,4},{6,5},{7,6},{9,8},{10,9},{11,10},{12... | collective-permute-start | bytes 245768 | tf_op jit(solution)/shard_map/ppermute | solution.py:528
  170.6 1.0 copy-start.6
  171.6 48.4 %all-to-all-start.1 = ((f32[32,64,128]{2,1,0:T(8,128)}), f32[32,64,128]{2,1,0:T(8,128)}, u32[]{:S(2)}, u32[]{:S(2)}) async-start(f32[32,64,128]{2,1,0:T(8,128)} %bitcast.15), calls=%async_computation.1 | async-start | bytes 2097152 | tf_op jit(solution)/shard_map/all_to_all | solution.py:672
  192.5 1.3 copy-start.3
  193.8 1.3 copy-start.4
  195.1 24.9 %copy-start.10 = (s32[256,128]{1,0:T(8,128)S(1)}, s32[256,128]{1,0:T(8,128)}, u32[]{:S(2)}) copy-start(s32[256,128]{1,0:T(8,128)} %element.3) | copy-start | bytes 393220
  195.1 24.9 %copy-start.12 = (f32[256,128]{1,0:T(8,128)S(1)}, f32[256,128]{1,0:T(8,128)}, u32[]{:S(2)}) copy-start(f32[256,128]{1,0:T(8,128)} %share.3) | copy-start | bytes 393220
  (4 other events, 3.4 us)

commit v3 on v2

--- a/solution.py
+++ b/solution.py
@@ -185,22 +185,18 @@
         column = halves_of(address & (meridians - 1), meridians)
         split = [two_terms(values[field, pl.ds(base, GROUP), :]) for field in range(4)]
         terms = [split[field][term] for term in range(2) for field in range(4)]
-        sums = None
-        for first in range(0, GROUP, PAIR):
-            names = range(first, first + PAIR)
-            left = jnp.concatenate(
-                [
-                    spread(row[b : b + 1], [term[b : b + 1] for term in terms], numbers[:parallels])
-                    for b in names
-                ],
-                axis=1,
-            )
-            right = jnp.concatenate([wide_one_hot(column, b, numbers[...]) for b in names], axis=1)
-            part = lax.dot_general(
-                left, right, CONTRACT_LAST, preferred_element_type=jnp.float32
-            )
-            sums = part if sums is None else sums + part
-        total[...] += sums
+        names = range(GROUP)
+        left = jnp.concatenate(
+            [
+                spread(row[b : b + 1], [term[b : b + 1] for term in terms], numbers[:parallels])
+                for b in names
+            ],
+            axis=1,
+        )
+        right = jnp.concatenate([wide_one_hot(column, b, numbers[...]) for b in names], axis=1)
+        total[...] += lax.dot_general(
+            left, right, CONTRACT_LAST, preferred_element_type=jnp.float32
+        )
         return carry
 
     lax.fori_loop(0, (filled + GROUP - 1) // GROUP, group, 0)
@@ -255,25 +251,21 @@
         near = narrow(cells & (LANES - 1))
         far = narrow(cells >> 7)
         weight = share[pl.ds(base, GROUP), :]
-        sums = None
-        for first in range(0, GROUP, PAIR):
-            names = range(first, first + PAIR)
-            lefts = []
-            for b in names:
-                row = home[base + b]
-                split = [
-                    two_terms(returned[pl.ds(row + field * capacity, 1), :] * weight[b : b + 1])
-                    for field in range(4)
-                ]
-                terms = [split[field][term] for term in range(2) for field in range(4)]
-                lefts.append(spread(far[b : b + 1], terms, numbers[:high_rows]))
-            left = jnp.concatenate(lefts, axis=1)
-            right = jnp.concatenate([one_hot(near[b : b + 1], numbers[...]) for b in names], axis=1)
-            part = lax.dot_general(
-                left, right, CONTRACT_LAST, preferred_element_type=jnp.float32
-            )
-            sums = part if sums is None else sums + part
-        total[...] += sums
+        names = range(GROUP)
+        lefts = []
+        for b in names:
+            row = home[base + b]
+            split = [
+                two_terms(returned[pl.ds(row + field * capacity, 1), :] * weight[b : b + 1])
+                for field in range(4)
+            ]
+            terms = [split[field][term] for term in range(2) for field in range(4)]
+            lefts.append(spread(far[b : b + 1], terms, numbers[:high_rows]))
+        left = jnp.concatenate(lefts, axis=1)
+        right = jnp.concatenate([one_hot(near[b : b + 1], numbers[...]) for b in names], axis=1)
+        total[...] += lax.dot_general(
+            left, right, CONTRACT_LAST, preferred_element_type=jnp.float32
+        )
         return carry
 
     lax.fori_loop(0, blocks // GROUP, group, 0)
@@ -289,18 +281,104 @@
     return pltpu.roll(x, x.shape[0] - 1, axis=0)
 
 
-def fill_wide(target, source, side, end):
-    rows, columns = source.shape[1:]
-    target[:, :rows, :columns] = source[...]
-    target[:, :rows, columns:] = side
-    target[:, rows:, :] = end
-
-
-def fill_opens(opens, top, ocean_mask, side, end):
+EDGE = 2
+SIDE_CHANNELS = LANES // EDGE
+END_CHANNELS = 8 // EDGE
+
+
+def edge_kernel(home, temper, saline, east, north, ocean_mask, first, last, low, high):
+    depth, rows, columns = temper.shape
+    lane = lax.broadcasted_iota(jnp.int32, (rows, LANES), 1)
+    heads, tails = [None] * first.shape[0], [None] * first.shape[0]
+    mask = ocean_mask[...].astype(jnp.float32)
+    for c in range(4 * depth + 1):
+        if c < 4 * depth:
+            source, k = (temper, saline, east, north)[c // depth], c % depth
+            left, right = source[k, :, :LANES], source[k, :, columns - LANES :]
+            top_rows, end_rows = source[k, :EDGE, :], source[k, rows - EDGE :, :]
+        else:
+            left, right = mask[:, :LANES], mask[:, columns - LANES :]
+            top_rows, end_rows = mask[:EDGE], mask[rows - EDGE :]
+        tile, at = c // SIDE_CHANNELS, EDGE * (c % SIDE_CHANNELS)
+        here = (lane >= at) & (lane < at + EDGE)
+        head = left if at == 0 else pltpu.roll(left, at, axis=1)
+        tail = pltpu.roll(right, (at + EDGE) % LANES, axis=1) if at + EDGE < LANES else right
+        heads[tile] = head if at == 0 else jnp.where(here, head, heads[tile])
+        tails[tile] = tail if at == 0 else jnp.where(here, tail, tails[tile])
+        spot = EDGE * (c % END_CHANNELS)
+        low[c // END_CHANNELS, spot : spot + EDGE, :] = top_rows
+        high[c // END_CHANNELS, spot : spot + EDGE, :] = end_rows
+    for c in range(4 * depth + 1, END_CHANNELS * low.shape[0]):
+        spot = EDGE * (c % END_CHANNELS)
+        low[c // END_CHANNELS, spot : spot + EDGE, :] = jnp.zeros((EDGE, columns), jnp.float32)
+        high[c // END_CHANNELS, spot : spot + EDGE, :] = jnp.zeros((EDGE, columns), jnp.float32)
+    for tile in range(first.shape[0]):
+        first[tile] = heads[tile]
+        last[tile] = tails[tile]
+
+
+def rolled(x, shift, axis):
+    shift = shift % x.shape[axis]
+    return x if shift == 0 else pltpu.roll(x, shift, axis=axis)
+
+
+def side_of(channel, from_east, from_west):
+    at = EDGE * (channel % SIDE_CHANNELS)
+    lane = lax.broadcasted_iota(jnp.int32, from_east.shape, 1)
+    return jnp.where(
+        lane < LANES // 2, rolled(from_east, -at, 1), rolled(from_west, LANES - EDGE - at, 1)
+    )
+
+
+def mirrored(across, kind):
+    across = turned(across)
+    if kind == 2:
+        across = -next_column(across)
+    last_row, row_before = across[7:8], across[6:7]
+    if kind == 3:
+        last_row, row_before = -row_before, -row_before
+    upper = lax.broadcasted_iota(jnp.int32, across.shape, 0)
+    return jnp.where(upper == 0, last_row, row_before)
+
+
+def fill_channel(target, k, channel, kind, halo, top):
+    from_east, from_west, from_north, from_south, folded, corner_n, corner_s, corner_f = halo
+    rows = from_east.shape[1]
+    columns = from_north.shape[2]
+    tile, group = channel // SIDE_CHANNELS, channel // END_CHANNELS
+    spot = EDGE * (channel % END_CHANNELS)
+    tiles = from_east.shape[0]
+    target[k, :rows, columns:] = side_of(channel, from_east[tile], from_west[tile])
+
+    def end_of(part, corner, shift):
+        return jnp.concatenate(
+            [
+                rolled(part[group], shift, 0),
+                side_of(channel, corner[tile], corner[tiles + tile]),
+            ],
+            axis=1,
+        )
+
+    upper = lax.broadcasted_iota(jnp.int32, (8, columns + LANES), 0)
+    above = end_of(from_north, corner_n, -spot)
+    across = mirrored(end_of(folded, corner_f, 8 - EDGE - spot), kind)
+    above = jnp.where(top[0] == 1, across, above)
+    below = end_of(from_south, corner_s, 8 - EDGE - spot)
+    target[k, rows:, :] = jnp.where(upper < 4, above, below)
+
+
+def fill_wide(targets, sources, depth, halo, top):
+    for kind, (target, source) in enumerate(zip(targets, sources)):
+        levels, rows, columns = source.shape
+        target[:, :rows, :columns] = source[...]
+        for k in range(levels):
+            fill_channel(target, k, kind * depth + k, kind, halo, top)
+
+
+def fill_opens(opens, top, ocean_mask, channel, halo):
     rows, columns = ocean_mask.shape
     opens[0, :rows, :columns] = ocean_mask[...].astype(jnp.float32)
-    opens[0, :rows, columns:] = side
-    opens[0, rows:, :] = end
+    fill_channel(opens, 0, channel, 0, halo, top)
     here = opens[0]
     opens[1] = here * next_column(here)
     opens[2] = here * next_row(here)
@@ -370,8 +448,14 @@
     east,
     north,
     ocean_mask,
-    sides,
-    ends,
+    from_east,
+    from_west,
+    from_north_all,
+    from_south_all,
+    folded_all,
+    corner_n,
+    corner_s,
+    corner_f,
     remapped,
     remap_sides,
     from_north,
@@ -390,23 +474,24 @@
     opens,
 ):
     levels, rows, columns = temper.shape
-    for turn, (target, source) in enumerate(
-        ((first_t, temper), (first_s, saline), (east_all, east), (north_all, north))
-    ):
-        part = slice(turn * depth, turn * depth + levels)
-        fill_wide(target, source, sides[part], ends[part])
-    fill_opens(opens, top, ocean_mask, sides[4 * depth], ends[4 * depth])
+    halo = (
+        from_east,
+        from_west,
+        from_north_all,
+        from_south_all,
+        folded_all,
+        corner_n,
+        corner_s,
+        corner_f,
+    )
+    targets, sources = (first_t, first_s, east_all, north_all), (temper, saline, east, north)
+    fill_wide(targets, sources, depth, halo, top)
+    fill_opens(opens, top, ocean_mask, 4 * depth, halo)
     upper = lax.broadcasted_iota(jnp.int32, (8, columns + LANES), 0)
     remap_all[:, :rows, :columns] = remapped[...]
     remap_all[:, :rows, columns:] = remap_sides[...]
     for field in range(4):
-        across = turned(folded[field])
-        if field == 2:
-            across = -next_column(across)
-        last_row, row_before = across[7:8], across[6:7]
-        if field == 3:
-            last_row, row_before = -row_before, -row_before
-        across = jnp.where(upper == 0, last_row, row_before)
+        across = mirrored(folded[field], field)
         above = jnp.where(top[0] == 1, across, from_north[field])
         remap_all[field, rows:, :] = jnp.where(upper < 4, above, from_south[field])
     east_all[0] = east_all[0] + stress_factor * remap_all[2]
@@ -439,8 +524,14 @@
     east,
     north,
     ocean_mask,
-    sides,
-    ends,
+    from_east,
+    from_west,
+    from_north,
+    from_south,
+    folded,
+    corner_n,
+    corner_s,
+    corner_f,
     temper_near,
     saline_near,
     temper_out,
@@ -455,12 +546,10 @@
 ):
     depth, rows, columns = temper.shape
     near = temper_near.shape[0]
-    for turn, (target, source) in enumerate(
-        ((first_t, temper), (first_s, saline), (east_all, east), (north_all, north))
-    ):
-        part = slice(turn * depth, (turn + 1) * depth)
-        fill_wide(target, source, sides[part], ends[part])
-    fill_opens(opens, top, ocean_mask, sides[4 * depth], ends[4 * depth])
+    halo = (from_east, from_west, from_north, from_south, folded, corner_n, corner_s, corner_f)
+    targets, sources = (first_t, first_s, east_all, north_all), (temper, saline, east, north)
+    fill_wide(targets, sources, depth, halo, top)
+    fill_opens(opens, top, ocean_mask, 4 * depth, halo)
     temper_out[:near] = temper_near[...]
     saline_out[:near] = saline_near[...]
 
@@ -475,40 +564,28 @@
     step((second_t, second_s), speeds, opens, near, depth, depth - 1, keep_last)
 
 
-def halo(parts, east_at, north_at):
-    rows, columns = parts[0].shape[1:]
+def edge_halo(first, last, low, high):
     count_gx, count_gy = lax.axis_size("gx"), lax.axis_size("gy")
-    head = jnp.concatenate([x[:, :, :2] for x in parts], axis=0)
-    tail = jnp.concatenate([x[:, :, -2:] for x in parts], axis=0)
-    channels = head.shape[0]
-    from_west = lax.ppermute(tail, "gx", [(i, (i + 1) % count_gx) for i in range(count_gx)])
-    from_east = lax.ppermute(head, "gx", [((i + 1) % count_gx, i) for i in range(count_gx)])
-    sides = jnp.concatenate(
-        [from_east, jnp.zeros((channels, rows, LANES - 4), jnp.float32), from_west], axis=2
-    )
-    low = jnp.concatenate(
-        [jnp.concatenate([x[:, :2] for x in parts], axis=0), sides[:, :2]], axis=2
-    )
-    high = jnp.concatenate(
-        [jnp.concatenate([x[:, -2:] for x in parts], axis=0), sides[:, -2:]], axis=2
-    )
-    from_south = lax.ppermute(high, "gy", [(i, i + 1) for i in range(count_gy - 1)])
-    from_north = lax.ppermute(low, "gy", [(i + 1, i) for i in range(count_gy - 1)])
-    folded = lax.ppermute(high, "gx", [(i, count_gx - 1 - i) for i in range(count_gx)])
-    folded = jnp.concatenate(
-        [folded[:, ::-1, columns - 1 :: -1], folded[:, ::-1, : columns - 1 : -1]], axis=2
-    )
-    e0, e1 = east_at
-    n0, n1 = north_at
-    east_part = -jnp.concatenate([folded[e0:e1, :, 1:], folded[e0:e1, :, :1]], axis=2)
-    north_part = -jnp.concatenate([folded[n0:n1, 1:], folded[n0:n1, :1]], axis=1)
-    folded = jnp.concatenate([folded[:e0], east_part, north_part, folded[n1:]], axis=0)
-    is_top = lax.axis_index("gy") == count_gy - 1
-    above = jnp.where(is_top, folded, from_north)
-    ends = jnp.concatenate(
-        [above, jnp.zeros((channels, 4, columns + LANES), jnp.float32), from_south], axis=1
-    )
-    return sides, ends
+    north_of = [(i + 1, i) for i in range(count_gy - 1)]
+    south_of = [(i, i + 1) for i in range(count_gy - 1)]
+    across = [(i, count_gx - 1 - i) for i in range(count_gx)]
+    from_west = lax.ppermute(last, "gx", [(i, (i + 1) % count_gx) for i in range(count_gx)])
+    from_east = lax.ppermute(first, "gx", [((i + 1) % count_gx, i) for i in range(count_gx)])
+    from_south = lax.ppermute(high, "gy", south_of)
+    from_north = lax.ppermute(low, "gy", north_of)
+    folded = lax.ppermute(high, "gx", across)
+    corner_low = jnp.concatenate([from_east[:, :8], from_west[:, :8]], axis=0)
+    corner_high = jnp.concatenate([from_east[:, -8:], from_west[:, -8:]], axis=0)
+    return (
+        from_east,
+        from_west,
+        from_north,
+        from_south,
+        folded,
+        lax.ppermute(corner_low, "gy", north_of),
+        lax.ppermute(corner_high, "gy", south_of),
+        lax.ppermute(corner_high, "gx", across),
+    )
 
 
 def tile_halo(x):
@@ -575,36 +652,25 @@
         overlay_fraction_share,
     )
 
-    (
-        outgoing,
+    arrived = lax.all_to_all(outgoing, ("gx", "gy"), split_axis=0, concat_axis=0, tiled=True)
+    channels = 4 * depth + 1
+    packed = jax.ShapeDtypeStruct((-(-channels // SIDE_CHANNELS), parallels, LANES), f32)
+    stacked = jax.ShapeDtypeStruct((-(-channels // END_CHANNELS), 8, meridians), f32)
+    edges = pl.pallas_call(
+        edge_kernel,
+        out_shape=(packed, packed, stacked, stacked),
+        in_specs=[SMEM] + [VMEM] * 5,
+        out_specs=(VMEM,) * 4,
+        **gather_kernel_params(10**7),
+    )(
+        home,
         thermal_deviation,
         saltiness_deviation,
         zonal_interface_speed,
         poleward_interface_speed,
         sea_profile_indicator,
-    ) = lax.optimization_barrier(
-        (
-            outgoing,
-            thermal_deviation,
-            saltiness_deviation,
-            zonal_interface_speed,
-            poleward_interface_speed,
-            sea_profile_indicator,
-        )
-    )
-    arrived = lax.all_to_all(outgoing, ("gx", "gy"), split_axis=0, concat_axis=0, tiled=True)
-    ocean_mask = sea_profile_indicator.astype(f32)
-    sides, ends = halo(
-        [
-            thermal_deviation,
-            saltiness_deviation,
-            zonal_interface_speed,
-            poleward_interface_speed,
-            ocean_mask[None],
-        ],
-        (2 * depth, 3 * depth),
-        (3 * depth, 4 * depth),
-    )
+    )
+    halo = edge_halo(*edges)
 
     counts = jnp.sum(
         (arrived.reshape(devices, 5, capacity, LANES)[:, 4, :, 0] >= 0).astype(jnp.int32), axis=1
@@ -638,7 +704,7 @@
         functools.partial(near_kernel, depth),
         grid=(1,),
         out_shape=(slab, slab, jax.ShapeDtypeStruct((4, parallels, meridians), f32)),
-        in_specs=[SMEM] + [first_levels] * 4 + [VMEM] * 8,
+        in_specs=[SMEM] + [first_levels] * 4 + [VMEM] * 14,
         out_specs=(VMEM, VMEM, VMEM),
         scratch_shapes=[pltpu.VMEM((levels,) + wide, f32)] * 6
         + [pltpu.VMEM((4,) + wide, f32)] * 2,
@@ -650,8 +716,7 @@
         zonal_interface_speed,
         poleward_interface_speed,
         sea_profile_indicator,
-        sides,
-        ends,
+        *halo,
         remapped,
         *around,
     )
@@ -673,7 +738,7 @@
     temper, saline = pl.pallas_call(
         deep_kernel,
         out_shape=(cube, cube),
-        in_specs=[SMEM] + [VMEM] * 9,
+        in_specs=[SMEM] + [VMEM] * 15,
         out_specs=(VMEM, VMEM),
         scratch_shapes=[pltpu.VMEM((depth,) + wide, f32)] * 6 + [pltpu.VMEM((4,) + wide, f32)],
         **gather_kernel_params(10**9),
@@ -684,8 +749,7 @@
         zonal_interface_speed,
         poleward_interface_speed,
         sea_profile_indicator,
-        sides,
-        ends,
+        *halo,
         temper_near,
         saline_near,
     )

time: 232 us -> 200 us (0.86)
  local copies, waits for them, and re-layouts: 59.4 us -> 17.4 us
  starting transfers between devices: 51.5 us -> 68.1 us
  other arithmetic: 12 us -> 5.2 us
  waiting for transfers between devices: 32.5 us -> 27.3 us
  Pallas kernels: 74.1 us -> 78.5 us
    optimization_barrier x4 -> x0, local copies, waits for them, and re-layouts: 32.4 us -> none  [body(): lax.optimization_barrier((outgoing, thermal_deviation, saltiness_deviatio...]
    ppermute x1, starting transfers between devices: 0.5 us -> 21.9 us  [tile_halo(): lax.ppermute(x[:, :, -LANES:], 'gx', [(i, (i + 1) % count_gx) for i in ra...]
    ppermute x1, waiting for transfers between devices: 10.9 us -> 0.88 us  [tile_halo(): lax.ppermute(x[:, :, -LANES:], 'gx', [(i, (i + 1) % count_gx) for i in ra...]
    all_to_all x1, waiting for transfers between devices: 0.01 us -> 9.75 us  [body(): lax.all_to_all(outgoing, ('gx', 'gy'), split_axis=0, concat_axis=0, tiled...]
    ppermute x1, starting transfers between devices: 13.9 us -> 4.89 us  [tile_halo(): lax.ppermute(high, 'gy', [(i, i + 1) for i in range(count_gy - 1)])]
    all_to_all x1, waiting for transfers between devices: 8.3 us -> 0.88 us  [body(): lax.all_to_all(picked, ('gx', 'gy'), split_axis=0, concat_axis=0, tiled=T...]
    pallas_call x1, Pallas kernels: 16.6 us -> 23.5 us  [body(): pl.pallas_call(deep_kernel, out_shape=(cube, cube), in_specs=[SMEM] + [VM...]
    concatenate x7 -> x2, other arithmetic: 6.96 us -> 0.61 us  [the longest x1 0.61 us: edge_halo(): jnp.concatenate([from_east[:, -8:], from_west[:, -8:]], axis=0)]
  transfers between devices with their start and end apart: 12 -> 15, of which waited for: 6 -> 7; matrix products, arithmetic and copies ran while one was open for 26% -> 2% of each run, Pallas kernels for 16% -> 21%
where the time goes in v3:
time: 200 us; the launch traced here: 197 us
  Pallas kernels  78.5 us (39%)
  starting transfers between devices  68.1 us (34%)
  waiting for transfers between devices  27.3 us (14%)
  local copies, waits for them, and re-layouts  17.4 us (9%)
  other arithmetic  5.2 us (3%)
    pallas_call x1, Pallas kernels, body(): pl.pallas_call(deep_kernel, out_shape=(cube, cube), in_specs=[SMEM] + [VM...  23.5 us
    ppermute x1, starting transfers between devices, tile_halo(): lax.ppermute(x[:, :, -LANES:], 'gx', [(i, (i + 1) % count_gx) for i in ra...  21.9 us
    all_to_all x1, starting transfers between devices, body(): lax.all_to_all(picked, ('gx', 'gy'), split_axis=0, concat_axis=0, tiled=T...  20.7 us
    pallas_call x1, Pallas kernels, body(): pl.pallas_call(functools.partial(land_kernel, capacity, parallels, meridi...  16.5 us
    unnamed x54, local copies, waits for them, and re-layouts  15.8 us
    pallas_call x1, Pallas kernels, body(): pl.pallas_call(functools.partial(pick_kernel, capacity, parallels, meridi...  12.8 us
    ppermute x1, waiting for transfers between devices, edge_halo(): lax.ppermute(first, 'gx', [((i + 1) % count_gx, i) for i in range(count_g...  10.5 us
    pallas_call x1, Pallas kernels, body(): pl.pallas_call(functools.partial(back_kernel, capacity), out_shape=jax.Sh...  9.87 us
  transfers between devices with their start and end apart: 15, of which 7 were waited for; matrix products, arithmetic and copies ran while one was open for 2% of the time, Pallas kernels for 21%

profile of v3, /device:TPU:0, one launch (start us, length us, event | category | flops | bytes accessed | tf_op | source)
XLA Modules:
  0.0 197.4 jit_solution(8496743131462381147)
XLA Ops:
  6.1 8.9 %shard_map.121 = (f32[2560,128]{1,0:T(8,128)S(1)}, s32[256]{0:T(256)S(1)}) custom-call(s32[256]{0:T(256)S(1)} %bitcast.15, f32[64,128]{1,0:T(8,128)S(1)} %reshape.38.table, s32[256,128]{1,0:T(8,128)S(1)} %copy-done.17, s32[256,128]{1,0:T(8,128)S(1)} %copy-done.16, f32[256,128]{1,0:T(8,128)S(1)} %copy-done.19), custom_call_target="tpu_custom_call" | custom-call | flops 1000000000 | bytes 4000000 | tf_op jit(solution)/shard_map/pallas_call | solution.py:633
  16.0 7.4 %all-to-all-start = ((f32[32,80,128]{2,1,0:T(8,128)}), f32[32,80,128]{2,1,0:T(8,128)}, u32[]{:S(2)}, u32[]{:S(2)}) async-start(f32[32,80,128]{2,1,0:T(8,128)} %bitcast.9), calls=%async_computation | async-start | bytes 2621440 | tf_op jit(solution)/shard_map/all_to_all | solution.py:655
  23.5 1.3 copy-done.2
  24.8 1.3 copy-done.4
  26.1 2.2 %shard_map.123 = (f32[2,32,128]{2,1,0:T(8,128)S(1)}, f32[2,32,128]{2,1,0:T(8,128)S(1)}, f32[21,8,512]{2,1,0:T(8,128)}, f32[21,8,512]{2,1,0:T(8,128)}) custom-call(s32[256]{0:T(256)S(1)} %get-tuple-element.21.home, f32[20,32,512]{2,1,0:T(8,128)S(1)} %copy-done, f32[20,32,512]{2,1,0:T(8,128)S(1)} %copy-done.1, f32[20,32,512]{2,1,0:T(8,128)S(1)} %copy-done.2, ...), custom_call_target="tpu_custom_call" | custom-call | flops 10000000 | bytes 4000000 | tf_op jit(solution)/shard_map/pallas_call | solution.py:659
  28.3 1.5 collective-permute-start.4
  29.8 3.4 %collective-permute-start.3 = (f32[21,8,512]{2,1,0:T(8,128)}, f32[21,8,512]{2,1,0:T(8,128)S(1)}, u32[]{:S(2)}, u32[]{:S(2)}) collective-permute-start(f32[21,8,512]{2,1,0:T(8,128)} %get-tuple-element.25), channel_id=1, source_target_pairs={{0,1},{1,2},{2,3},{3,4},{4,5},{5,6},{6,7},{8,9},{9,10},{10,11},{11... | collective-permute-start | bytes 1032200 | tf_op jit(solution)/shard_map/ppermute | solution.py:574
  35.6 10.5 %collective-permute-done.from_east = f32[2,32,128]{2,1,0:T(8,128)S(1)} collective-permute-done((f32[2,32,128]{2,1,0:T(8,128)S(1)}, f32[2,32,128]{2,1,0:T(8,128)S(1)}, u32[]{:S(2)}, u32[]{:S(2)}) %collective-permute-start) | collective-permute-done | bytes 32800 | tf_op jit(solution)/shard_map/ppermute | solution.py:573
  46.1 1.4 collective-permute-done.1.from_west
  48.1 9.7 %all-to-all-done = f32[32,80,128]{2,1,0:T(8,128)} async-done(((f32[32,80,128]{2,1,0:T(8,128)}), f32[32,80,128]{2,1,0:T(8,128)}, u32[]{:S(2)}, u32[]{:S(2)}) %all-to-all-start) | async-done | bytes 1310752 | tf_op jit(solution)/shard_map/all_to_all | solution.py:655
  57.8 1.6 convert_reduce_fusion.counts
  59.4 16.5 %shard_map.122 = (f32[128,512]{1,0:T(8,128)S(1)}, f32[520,128]{1,0:T(8,128)S(1)}, s32[521]{0:T(1024)S(1)}) custom-call(s32[32]{0:T(128)S(1)} %convert_reduce_fusion.counts, f32[2560,128]{1,0:T(8,128)} %bitcast.3.arrived), custom_call_target="tpu_custom_call" | custom-call | flops 20000000000 | bytes 4000000 | tf_op jit(solution)/shard_map/pallas_call | solution.py:678
  76.5 21.9 %collective-permute-start.9 = (f32[4,32,128]{2,1,0:T(8,128)S(1)}, f32[4,32,128]{2,1,0:T(8,128)S(1)}, u32[]{:S(2)}, u32[]{:S(2)}) collective-permute-start(f32[4,32,128]{2,1,0:T(8,128)S(1)} %get-tuple-element.37), channel_id=1, source_target_pairs={{0,8},{8,16},{16,24},{24,0},{1,9},{9,17},{17,25},{25,1},{2,10},{10... | collective-permute-start | bytes 196616 | tf_op jit(solution)/shard_map/ppermute | solution.py:594
  100.6 1.5 collective-permute-start.7
  102.8 2.2 %collective-permute-done.5.corner_n = f32[4,8,128]{2,1,0:T(8,128)S(1)} collective-permute-done((f32[4,8,128]{2,1,0:T(8,128)S(1)}, f32[4,8,128]{2,1,0:T(8,128)S(1)}, u32[]{:S(2)}, u32[]{:S(2)}) %collective-permute-start.5) | collective-permute-done | bytes 16416 | tf_op jit(solution)/shard_map/ppermute | solution.py:585
  104.9 1.6 collective-permute-start.6
  109.4 4.9 %collective-permute-start.11 = (f32[4,8,640]{2,1,0:T(8,128)}, f32[4,8,640]{2,1,0:T(8,128)}, u32[]{:S(2)}, u32[]{:S(2)}) collective-permute-start(f32[4,8,640]{2,1,0:T(8,128)} %pad_maximum_fusion.1), channel_id=1, source_target_pairs={{0,1},{1,2},{2,3},{3,4},{4,5},{5,6},{6,7},{8,9},{9,10},{10,11},{11... | collective-permute-start | bytes 245768 | tf_op jit(solution)/shard_map/ppermute | solution.py:604
  114.3 1.7 collective-permute-done.11.from_south
  116.9 4.8 %shard_map.124 = (f32[2,32,512]{2,1,0:T(8,128)S(1)}, f32[2,32,512]{2,1,0:T(8,128)S(1)}, f32[4,32,512]{2,1,0:T(8,128)S(1)}) custom-call(s32[1]{0:T(128)} %bitcast.4.top, f32[20,32,512]{2,1,0:T(8,128)S(1)} %copy-done, f32[20,32,512]{2,1,0:T(8,128)S(1)} %copy-done.1, f32[20,32,512]{2,1,0:T(8,128)} %east.5, f32[20,32,512]{2,1,0:T(8,128)} %north.5, ...), custom_call_target="tpu_custom_call" | custom-call | flops 100000000 | bytes 4000000 | tf_op jit(solution)/shard_map/pallas_call | solution.py:703
  123.0 12.8 %shard_map.125 = f32[2048,128]{1,0:T(8,128)S(1)} custom-call(s32[521]{0:T(1024)S(1)} %copy-done.25, f32[128,512]{1,0:T(8,128)S(1)} %bitcast.14, f32[520,128]{1,0:T(8,128)S(1)} %copy-done.23), custom_call_target="tpu_custom_call" | custom-call | flops 20000000000 | bytes 4000000 | tf_op jit(solution)/shard_map/pallas_call | solution.py:724
  136.8 20.7 %all-to-all-start.1 = ((f32[32,64,128]{2,1,0:T(8,128)}), f32[32,64,128]{2,1,0:T(8,128)}, u32[]{:S(2)}, u32[]{:S(2)}) async-start(f32[32,64,128]{2,1,0:T(8,128)} %bitcast.13), calls=%async_computation.1 | async-start | bytes 2097152 | tf_op jit(solution)/shard_map/all_to_all | solution.py:737
  157.5 1.3 copy-done.3
  160.6 23.5 %shard_map.126 = (f32[20,32,512]{2,1,0:T(8,128)}, f32[20,32,512]{2,1,0:T(8,128)}) custom-call(s32[1]{0:T(128)} %bitcast.4.top, f32[20,32,512]{2,1,0:T(8,128)S(1)} %copy-done, f32[20,32,512]{2,1,0:T(8,128)S(1)} %copy-done.1, f32[20,32,512]{2,1,0:T(8,128)S(1)} %copy-done.3, f32[20,32,512]{2,1,0:T(8,128)} %north.5, s32[32,512]{1,0:T(8,128)S(1)} %copy-done.9, ...), custom_call_target="tpu_custom_call" | custom-call | flops 1000000000 | bytes 4000000 | tf_op jit(solution)/shard_map/pallas_call | solution.py:738
  186.9 9.9 %shard_map.127 = f32[64,128]{1,0:T(8,128)S(1)} custom-call(s32[256]{0:T(256)S(1)} %copy-done.15, f32[2048,128]{1,0:T(8,128)} %bitcast.8.returned, s32[256,128]{1,0:T(8,128)S(1)} %copy-done.18, f32[256,128]{1,0:T(8,128)S(1)} %copy-done.20), custom_call_target="tpu_custom_call" | custom-call | flops 2000000000 | bytes 4000000 | tf_op jit(solution)/shard_map/pallas_call | solution.py:756
  (84 shorter events, 24.1 us)
Async XLA Ops:
  6.1 17.4 %copy-start.9 = (s32[32,512]{1,0:T(8,128)S(1)}, s32[32,512]{1,0:T(8,128)}, u32[]{:S(2)}) copy-start(s32[32,512]{1,0:T(8,128)} %ocean_mask.5) | copy-start | bytes 196612
  16.0 7.4 %copy-start.14 = (s32[256]{0:T(256)}, s32[256]{0:T(256)S(1)}, u32[]{:S(2)}) copy-start(s32[256]{0:T(256)S(1)} %get-tuple-element.21.home) | copy-start | bytes 3076
  16.0 7.4 %copy-start = (f32[20,32,512]{2,1,0:T(8,128)S(1)}, f32[20,32,512]{2,1,0:T(8,128)}, u32[]{:S(2)}) copy-start(f32[20,32,512]{2,1,0:T(8,128)} %temper.5) | copy-start | bytes 3932164
  16.0 7.5 %copy-start.1 = (f32[20,32,512]{2,1,0:T(8,128)S(1)}, f32[20,32,512]{2,1,0:T(8,128)}, u32[]{:S(2)}) copy-start(f32[20,32,512]{2,1,0:T(8,128)} %saline.5) | copy-start | bytes 3932164
  16.0 41.8 %all-to-all-start = ((f32[32,80,128]{2,1,0:T(8,128)}), f32[32,80,128]{2,1,0:T(8,128)}, u32[]{:S(2)}, u32[]{:S(2)}) async-start(f32[32,80,128]{2,1,0:T(8,128)} %bitcast.9), calls=%async_computation | async-start | bytes 2621440 | tf_op jit(solution)/shard_map/all_to_all | solution.py:655
  28.3 85.9 %collective-permute-start.4 = (f32[21,8,512]{2,1,0:T(8,128)}, f32[21,8,512]{2,1,0:T(8,128)S(1)}, u32[]{:S(2)}, u32[]{:S(2)}) collective-permute-start(f32[21,8,512]{2,1,0:T(8,128)} %get-tuple-element.25), channel_id=1, source_target_pairs={{0,24},{8,16},{16,8},{24,0},{1,25},{9,17},{17,9},{25,1},{2,26},{10... | collective-permute-start | bytes 1032200 | tf_op jit(solution)/shard_map/ppermute | solution.py:576
  29.8 84.5 %collective-permute-start.3 = (f32[21,8,512]{2,1,0:T(8,128)}, f32[21,8,512]{2,1,0:T(8,128)S(1)}, u32[]{:S(2)}, u32[]{:S(2)}) collective-permute-start(f32[21,8,512]{2,1,0:T(8,128)} %get-tuple-element.25), channel_id=1, source_target_pairs={{0,1},{1,2},{2,3},{3,4},{4,5},{5,6},{6,7},{8,9},{9,10},{10,11},{11... | collective-permute-start | bytes 1032200 | tf_op jit(solution)/shard_map/ppermute | solution.py:574
  33.2 12.9 %collective-permute-start = (f32[2,32,128]{2,1,0:T(8,128)S(1)}, f32[2,32,128]{2,1,0:T(8,128)S(1)}, u32[]{:S(2)}, u32[]{:S(2)}) collective-permute-start(f32[2,32,128]{2,1,0:T(8,128)S(1)} %get-tuple-element.22), channel_id=1, source_target_pairs={{8,0},{16,8},{24,16},{0,24},{9,1},{17,9},{25,17},{1,25},{10,2},{18... | collective-permute-start | bytes 98312 | tf_op jit(solution)/shard_map/ppermute | solution.py:573
  33.5 14.0 %collective-permute-start.1 = (f32[2,32,128]{2,1,0:T(8,128)S(1)}, f32[2,32,128]{2,1,0:T(8,128)S(1)}, u32[]{:S(2)}, u32[]{:S(2)}) collective-permute-start(f32[2,32,128]{2,1,0:T(8,128)S(1)} %get-tuple-element.23), channel_id=1, source_target_pairs={{0,8},{8,16},{16,24},{24,0},{1,9},{9,17},{17,25},{25,1},{2,10},{10... | collective-permute-start | bytes 98312 | tf_op jit(solution)/shard_map/ppermute | solution.py:572
  33.7 75.6 %collective-permute-start.2 = (f32[21,8,512]{2,1,0:T(8,128)}, f32[21,8,512]{2,1,0:T(8,128)}, u32[]{:S(2)}, u32[]{:S(2)}) collective-permute-start(f32[21,8,512]{2,1,0:T(8,128)} %get-tuple-element.24), channel_id=1, source_target_pairs={{1,0},{2,1},{3,2},{4,3},{5,4},{6,5},{7,6},{9,8},{10,9},{11,10},{12... | collective-permute-start | bytes 1032200 | tf_op jit(solution)/shard_map/ppermute | solution.py:575
  59.4 42.7 %copy-start.26 = (pred[128]{0:T(512)(128)(4,1)S(1)}, pred[128]{0:T(512)(128)(4,1)}, u32[]{:S(2)}) copy-start(pred[128]{0:T(512)(128)(4,1)} %iota_compare_fusion) | copy-start | bytes 388
  76.5 21.9 %copy-start.6 = (f32[128,512]{1,0:T(8,128)}, f32[128,512]{1,0:T(8,128)S(1)}, u32[]{:S(2)}) copy-start(f32[128,512]{1,0:T(8,128)S(1)} %get-tuple-element.26) | copy-start | bytes 786436
  76.5 32.0 %copy-start.22 = (f32[520,128]{1,0:T(8,128)}, f32[520,128]{1,0:T(8,128)S(1)}, u32[]{:S(2)}) copy-start(f32[520,128]{1,0:T(8,128)S(1)} %get-tuple-element.28.places) | copy-start | bytes 798724
  76.5 22.8 %collective-permute-start.9 = (f32[4,32,128]{2,1,0:T(8,128)S(1)}, f32[4,32,128]{2,1,0:T(8,128)S(1)}, u32[]{:S(2)}, u32[]{:S(2)}) collective-permute-start(f32[4,32,128]{2,1,0:T(8,128)S(1)} %get-tuple-element.37), channel_id=1, source_target_pairs={{0,8},{8,16},{16,24},{24,0},{1,9},{9,17},{17,25},{25,1},{2,10},{10... | collective-permute-start | bytes 196616 | tf_op jit(solution)/shard_map/ppermute | solution.py:594
  98.4 2.2 %collective-permute-start.8 = (f32[4,32,128]{2,1,0:T(8,128)S(1)}, f32[4,32,128]{2,1,0:T(8,128)S(1)}, u32[]{:S(2)}, u32[]{:S(2)}) collective-permute-start(f32[4,32,128]{2,1,0:T(8,128)S(1)} %get-tuple-element.38), channel_id=1, source_target_pairs={{8,0},{16,8},{24,16},{0,24},{9,1},{17,9},{25,17},{1,25},{10,2},{18... | collective-permute-start | bytes 196616 | tf_op jit(solution)/shard_map/ppermute | solution.py:597
  99.3 5.6 %collective-permute-start.5 = (f32[4,8,128]{2,1,0:T(8,128)S(1)}, f32[4,8,128]{2,1,0:T(8,128)S(1)}, u32[]{:S(2)}, u32[]{:S(2)}) collective-permute-start(f32[4,8,128]{2,1,0:T(8,128)S(1)} %pad_maximum_fusion.3), channel_id=1, source_target_pairs={{1,0},{2,1},{3,2},{4,3},{5,4},{6,5},{7,6},{9,8},{10,9},{11,10},{12... | collective-permute-start | bytes 49160 | tf_op jit(solution)/shard_map/ppermute | solution.py:585
  100.6 6.6 %collective-permute-start.7 = (f32[4,8,128]{2,1,0:T(8,128)}, f32[4,8,128]{2,1,0:T(8,128)S(1)}, u32[]{:S(2)}, u32[]{:S(2)}) collective-permute-start(f32[4,8,128]{2,1,0:T(8,128)} %pad_maximum_fusion.4), channel_id=1, source_target_pairs={{0,24},{8,16},{16,8},{24,0},{1,25},{9,17},{17,9},{25,1},{2,26},{10... | collective-permute-start | bytes 49160 | tf_op jit(solution)/shard_map/ppermute | solution.py:587
  104.9 3.6 %collective-permute-start.6 = (f32[4,8,128]{2,1,0:T(8,128)}, f32[4,8,128]{2,1,0:T(8,128)S(1)}, u32[]{:S(2)}, u32[]{:S(2)}) collective-permute-start(f32[4,8,128]{2,1,0:T(8,128)} %pad_maximum_fusion.4), channel_id=1, source_target_pairs={{0,1},{1,2},{2,3},{3,4},{4,5},{5,6},{6,7},{8,9},{9,10},{10,11},{11... | collective-permute-start | bytes 49160 | tf_op jit(solution)/shard_map/ppermute | solution.py:586
  107.2 7.1 %collective-permute-start.10 = (f32[4,8,640]{2,1,0:T(8,128)}, f32[4,8,640]{2,1,0:T(8,128)}, u32[]{:S(2)}, u32[]{:S(2)}) collective-permute-start(f32[4,8,640]{2,1,0:T(8,128)} %pad_maximum_fusion), channel_id=1, source_target_pairs={{1,0},{2,1},{3,2},{4,3},{5,4},{6,5},{7,6},{9,8},{10,9},{11,10},{12... | collective-permute-start | bytes 245768 | tf_op jit(solution)/shard_map/ppermute | solution.py:605
  108.5 5.8 %collective-permute-start.12 = (f32[4,8,640]{2,1,0:T(8,128)}, f32[4,8,640]{2,1,0:T(8,128)}, u32[]{:S(2)}, u32[]{:S(2)}) collective-permute-start(f32[4,8,640]{2,1,0:T(8,128)} %pad_maximum_fusion.1), channel_id=1, source_target_pairs={{0,24},{8,16},{16,8},{24,0},{1,25},{9,17},{17,9},{25,1},{2,26},{10... | collective-permute-start | bytes 245768 | tf_op jit(solution)/shard_map/ppermute | solution.py:606
  109.4 6.6 %collective-permute-start.11 = (f32[4,8,640]{2,1,0:T(8,128)}, f32[4,8,640]{2,1,0:T(8,128)}, u32[]{:S(2)}, u32[]{:S(2)}) collective-permute-start(f32[4,8,640]{2,1,0:T(8,128)} %pad_maximum_fusion.1), channel_id=1, source_target_pairs={{0,1},{1,2},{2,3},{3,4},{4,5},{5,6},{6,7},{8,9},{9,10},{10,11},{11... | collective-permute-start | bytes 245768 | tf_op jit(solution)/shard_map/ppermute | solution.py:604
  116.9 6.1 %copy-start.25 = (s32[521]{0:T(1024)S(1)}, s32[521]{0:T(1024)}, u32[]{:S(2)}) copy-start(s32[521]{0:T(1024)} %copy-done.24) | copy-start | bytes 6256
  136.8 48.3 %all-to-all-start.1 = ((f32[32,64,128]{2,1,0:T(8,128)}), f32[32,64,128]{2,1,0:T(8,128)}, u32[]{:S(2)}, u32[]{:S(2)}) async-start(f32[32,64,128]{2,1,0:T(8,128)} %bitcast.13), calls=%async_computation.1 | async-start | bytes 2097152 | tf_op jit(solution)/shard_map/all_to_all | solution.py:737
  160.6 24.4 %copy-start.15 = (s32[256]{0:T(256)S(1)}, s32[256]{0:T(256)}, u32[]{:S(2)}) copy-start(s32[256]{0:T(256)} %copy-done.14) | copy-start | bytes 3076
  (18 other events, 21.9 us)

commit v4 on v3

--- a/solution.py
+++ b/solution.py
@@ -15,7 +15,10 @@
 stress_factor = 0.3
 
 LANES = 128
-GROUP = 8
+SEND_GROUP = 32
+LAND_GROUP = 16
+PICK_GROUP = 16
+BACK_GROUP = 32
 HALF = 256
 PAIR = 2
 VMEM_BYTES = 48 * 1024 * 1024
@@ -62,15 +65,11 @@
     return jnp.concatenate([jnp.where(hit, term, jnp.bfloat16(0)) for term in terms], axis=0)
 
 
-def halves_of(column, meridians):
-    return [
-        narrow(jnp.where(column // HALF == part, column % HALF, -1))
-        for part in range(meridians // HALF)
-    ]
-
-
-def wide_one_hot(parts, b, numbers):
-    return jnp.concatenate([one_hot(part[b : b + 1], numbers) for part in parts], axis=0)
+def halves_of(address, parallels, meridians):
+    shift = meridians.bit_length() - 1
+    column = address & (meridians - 1)
+    row = (address >> shift) + parallels * (column // HALF)
+    return jnp.where(address < 0, -1, row), column % HALF
 
 
 def picked_rows(rows_of, table, fields, count):
@@ -103,13 +102,13 @@
     split_table[:, LANES:] = low
 
     def group(g, carry):
-        base = pl.multiple_of(g * GROUP, GROUP)
-        cells = element[pl.ds(base, GROUP), :]
+        base = pl.multiple_of(g * SEND_GROUP, SEND_GROUP)
+        cells = element[pl.ds(base, SEND_GROUP), :]
         near = narrow(cells & (LANES - 1))
         far = cells >> 7
-        address = profile[pl.ds(base, GROUP), :].astype(jnp.float32)
-        weight = share[pl.ds(base, GROUP), :]
-        for first in range(0, GROUP, PAIR):
+        address = profile[pl.ds(base, SEND_GROUP), :].astype(jnp.float32)
+        weight = share[pl.ds(base, SEND_GROUP), :]
+        for first in range(0, SEND_GROUP, PAIR):
             names = range(first, first + PAIR)
             hot = jnp.concatenate([one_hot(near[b : b + 1], numbers[...]) for b in names], axis=1)
             found = jnp.dot(
@@ -132,7 +131,7 @@
                 out[pl.ds(row + 4 * capacity, 1), :] = address[b : b + 1]
         return carry
 
-    lax.fori_loop(0, blocks // GROUP, group, 0)
+    lax.fori_loop(0, blocks // SEND_GROUP, group, 0)
 
 
 def gather_kernel_params(flops):
@@ -157,76 +156,88 @@
 ):
     sources = counts.shape[0]
     last = slots.shape[0] - 1
-    shift = meridians.bit_length() - 1
+    long_rows = parallels * (meridians // HALF)
     places[...] = jnp.full(places.shape, -1.0, jnp.float32)
     total[...] = jnp.zeros(total.shape, jnp.float32)
 
     def from_source(source, count):
-        def slot(place, count):
-            row = source * (5 * capacity) + place
-            for field in range(4):
-                values[field, pl.ds(count, 1), :] = arrived[pl.ds(row + field * capacity, 1), :]
-            places[pl.ds(count, 1), :] = arrived[pl.ds(row + 4 * capacity, 1), :]
-            slots[count] = source * (4 * capacity) + place
-            return count + 1
-
-        return lax.fori_loop(0, counts[source], slot, count)
+        row = source * (5 * capacity)
+        for field in range(4):
+            values[field, pl.ds(count, capacity), :] = arrived[
+                pl.ds(row + field * capacity, capacity), :
+            ]
+        places[pl.ds(count, capacity), :] = arrived[pl.ds(row + 4 * capacity, capacity), :]
+        for place in range(capacity):
+            slots[count + place] = source * (4 * capacity) + place
+        return count + counts[source]
 
     filled = lax.fori_loop(0, sources, from_source, 0)
     slots[last] = filled
-    for extra in range(GROUP):
+    for extra in range(LAND_GROUP):
         slots[filled + extra] = sources * (4 * capacity)
     number_rows(numbers)
 
     def group(g, carry):
-        base = pl.multiple_of(g * GROUP, GROUP)
-        address = places[pl.ds(base, GROUP), :].astype(jnp.int32)
-        row = narrow(address >> shift)
-        column = halves_of(address & (meridians - 1), meridians)
-        split = [two_terms(values[field, pl.ds(base, GROUP), :]) for field in range(4)]
+        base = pl.multiple_of(g * LAND_GROUP, LAND_GROUP)
+        address = places[pl.ds(base, LAND_GROUP), :].astype(jnp.int32)
+        row, column = halves_of(address, parallels, meridians)
+        row, column = narrow(row), narrow(column)
+        split = [two_terms(values[field, pl.ds(base, LAND_GROUP), :]) for field in range(4)]
         terms = [split[field][term] for term in range(2) for field in range(4)]
-        names = range(GROUP)
+        names = range(LAND_GROUP)
         left = jnp.concatenate(
             [
-                spread(row[b : b + 1], [term[b : b + 1] for term in terms], numbers[:parallels])
+                spread(row[b : b + 1], [term[b : b + 1] for term in terms], numbers[:long_rows])
                 for b in names
             ],
             axis=1,
         )
-        right = jnp.concatenate([wide_one_hot(column, b, numbers[...]) for b in names], axis=1)
+        right = jnp.concatenate([one_hot(column[b : b + 1], numbers[...]) for b in names], axis=1)
         total[...] += lax.dot_general(
             left, right, CONTRACT_LAST, preferred_element_type=jnp.float32
         )
         return carry
 
-    lax.fori_loop(0, (filled + GROUP - 1) // GROUP, group, 0)
-    half = 4 * parallels
-    remapped[...] = total[:half] + total[half:]
+    lax.fori_loop(0, (filled + LAND_GROUP - 1) // LAND_GROUP, group, 0)
+    for field in range(4):
+        for part in range(meridians // HALF):
+            at = field * long_rows + part * parallels
+            remapped[field * parallels : (field + 1) * parallels, part * HALF : (part + 1) * HALF] = (
+                total[at : at + parallels]
+                + total[4 * long_rows + at : 4 * long_rows + at + parallels]
+            )
 
 
 def pick_kernel(capacity, parallels, meridians, slots, surface, places, out, split_table, numbers, found_rows):
     last = slots.shape[0] - 1
-    half = 4 * parallels
-    shift = meridians.bit_length() - 1
+    long_rows = parallels * (meridians // HALF)
+    half = 4 * long_rows
     filled = slots[last]
-    high, low = two_terms(surface[...])
-    split_table[:half] = high
-    split_table[half:] = low
+    for field in range(4):
+        for part in range(meridians // HALF):
+            high, low = two_terms(
+                surface[
+                    field * parallels : (field + 1) * parallels, part * HALF : (part + 1) * HALF
+                ]
+            )
+            at = field * long_rows + part * parallels
+            split_table[at : at + parallels] = high
+            split_table[half + at : half + at + parallels] = low
     found_rows[...] = jnp.zeros(found_rows.shape, jnp.float32)
     number_rows(numbers)
 
     def group(g, carry):
-        base = pl.multiple_of(g * GROUP, GROUP)
-        address = places[pl.ds(base, GROUP), :].astype(jnp.int32)
-        row = address >> shift
-        column = halves_of(address & (meridians - 1), meridians)
-        for first in range(0, GROUP, PAIR):
+        base = pl.multiple_of(g * PICK_GROUP, PICK_GROUP)
+        address = places[pl.ds(base, PICK_GROUP), :].astype(jnp.int32)
+        row, column = halves_of(address, parallels, meridians)
+        column = narrow(column)
+        for first in range(0, PICK_GROUP, PAIR):
             names = range(first, first + PAIR)
-            hot = jnp.concatenate([wide_one_hot(column, b, numbers[...]) for b in names], axis=1)
+            hot = jnp.concatenate([one_hot(column[b : b + 1], numbers[...]) for b in names], axis=1)
             found = jnp.dot(split_table[...], hot, preferred_element_type=jnp.float32)
             found = found[:half] + found[half:]
             wide_row = jnp.concatenate([row[b : b + 1] for b in names], axis=1)
-            values = picked_rows(wide_row, found, 4, parallels)
+            values = picked_rows(wide_row, found, 4, long_rows)
             for turn, b in enumerate(names):
                 target = slots[base + b]
                 for field in range(4):
@@ -235,7 +246,7 @@
                     ]
         return carry
 
-    lax.fori_loop(0, (filled + GROUP - 1) // GROUP, group, 0)
+    lax.fori_loop(0, (filled + PICK_GROUP - 1) // PICK_GROUP, group, 0)
     out[...] = found_rows[: out.shape[0]]
 
 
@@ -246,12 +257,12 @@
     number_rows(numbers)
 
     def group(g, carry):
-        base = pl.multiple_of(g * GROUP, GROUP)
-        cells = element[pl.ds(base, GROUP), :]
+        base = pl.multiple_of(g * BACK_GROUP, BACK_GROUP)
+        cells = element[pl.ds(base, BACK_GROUP), :]
         near = narrow(cells & (LANES - 1))
         far = narrow(cells >> 7)
-        weight = share[pl.ds(base, GROUP), :]
-        names = range(GROUP)
+        weight = share[pl.ds(base, BACK_GROUP), :]
+        names = range(BACK_GROUP)
         lefts = []
         for b in names:
             row = home[base + b]
@@ -268,7 +279,7 @@
         )
         return carry
 
-    lax.fori_loop(0, blocks // GROUP, group, 0)
+    lax.fori_loop(0, blocks // BACK_GROUP, group, 0)
     half = 4 * high_rows
     out[...] = total[:half] + total[half:]
 
@@ -625,6 +636,7 @@
     depth, parallels, meridians = thermal_deviation.shape
     capacity = max(2, 2 * blocks // devices)
     slot_count = devices * capacity
+    spare = max(LAND_GROUP, PICK_GROUP, capacity)
     f32 = jnp.float32
     air = air_forcing_quantities
     table = jnp.stack([air[0] + air[1] + air[2] + air[3], air[5] - air[4], air[6], air[7]])
@@ -679,14 +691,14 @@
         functools.partial(land_kernel, capacity, parallels, meridians),
         out_shape=(
             jax.ShapeDtypeStruct((4 * parallels, meridians), f32),
-            jax.ShapeDtypeStruct((slot_count + GROUP, LANES), f32),
-            jax.ShapeDtypeStruct((slot_count + GROUP + 1,), jnp.int32),
+            jax.ShapeDtypeStruct((slot_count + spare, LANES), f32),
+            jax.ShapeDtypeStruct((slot_count + spare + 1,), jnp.int32),
         ),
         in_specs=[SMEM, VMEM],
         out_specs=(VMEM, VMEM, SMEM),
         scratch_shapes=[
-            pltpu.VMEM((4, slot_count + GROUP, LANES), f32),
-            pltpu.VMEM((8 * parallels, meridians), f32),
+            pltpu.VMEM((4, slot_count + spare, LANES), f32),
+            pltpu.VMEM((8 * parallels * (meridians // HALF), HALF), f32),
             pltpu.VMEM((HALF, LANES), jnp.bfloat16),
         ],
         **gather_kernel_params(2 * 10**10),
@@ -727,7 +739,7 @@
         in_specs=[SMEM, VMEM, VMEM],
         out_specs=VMEM,
         scratch_shapes=[
-            pltpu.VMEM((8 * parallels, meridians), jnp.bfloat16),
+            pltpu.VMEM((8 * parallels * (meridians // HALF), HALF), jnp.bfloat16),
             pltpu.VMEM((HALF, LANES), jnp.bfloat16),
             pltpu.VMEM(((slot_count + capacity) * 4, LANES), f32),
         ],

time: 200 us -> 180 us (0.900)
  starting transfers between devices: 68.1 us -> 41.4 us
  Pallas kernels: 78.5 us -> 83.7 us
  waiting for transfers between devices: 27.3 us -> 29.9 us
    ppermute x1, starting transfers between devices: 21.9 us -> 0.06 us  [tile_halo(): lax.ppermute(x[:, :, -LANES:], 'gx', [(i, (i + 1) % count_gx) for i in ra...]
    pallas_call x1, Pallas kernels: 12.8 us -> 18.8 us  [body(): pl.pallas_call(functools.partial(pick_kernel, capacity, parallels, meridi...]
    all_to_all x1, starting transfers between devices: 20.7 us -> 14.9 us  [body(): lax.all_to_all(picked, ('gx', 'gy'), split_axis=0, concat_axis=0, tiled=T...]
    pallas_call x1, Pallas kernels: 16.5 us -> 22 us  [body(): pl.pallas_call(functools.partial(land_kernel, capacity, parallels, meridi...]
    pallas_call x1, Pallas kernels: 9.87 us -> 6.64 us  [body(): pl.pallas_call(functools.partial(back_kernel, capacity), out_shape=jax.Sh...]
    pallas_call x1, Pallas kernels: 8.86 us -> 5.7 us  [body(): pl.pallas_call(functools.partial(send_kernel, capacity), out_shape=(jax.S...]
  transfers between devices with their start and end apart: 15 -> 15, of which waited for: 7 -> 8; matrix products, arithmetic and copies ran while one was open for 2% -> 2% of each run, Pallas kernels for 21% -> 27%
where the time goes in v4:
time: 180 us; the launch traced here: 178 us
  Pallas kernels  83.7 us (46%)
  starting transfers between devices  41.4 us (23%)
  waiting for transfers between devices  29.9 us (17%)
  local copies, waits for them, and re-layouts  17.4 us (10%)
  other arithmetic  5.2 us (3%)
    pallas_call x1, Pallas kernels, body(): pl.pallas_call(deep_kernel, out_shape=(cube, cube), in_specs=[SMEM] + [VM...  23.5 us
    pallas_call x1, Pallas kernels, body(): pl.pallas_call(functools.partial(land_kernel, capacity, parallels, meridi...  22 us
    pallas_call x1, Pallas kernels, body(): pl.pallas_call(functools.partial(pick_kernel, capacity, parallels, meridi...  18.8 us
    unnamed x54, local copies, waits for them, and re-layouts  15.8 us
    all_to_all x1, starting transfers between devices, body(): lax.all_to_all(picked, ('gx', 'gy'), split_axis=0, concat_axis=0, tiled=T...  14.9 us
    ppermute x1, waiting for transfers between devices, edge_halo(): lax.ppermute(first, 'gx', [((i + 1) % count_gx, i) for i in range(count_g...  10.5 us
    all_to_all x1, waiting for transfers between devices, body(): lax.all_to_all(outgoing, ('gx', 'gy'), split_axis=0, concat_axis=0, tiled...  9.75 us
    all_to_all x1, starting transfers between devices, body(): lax.all_to_all(outgoing, ('gx', 'gy'), split_axis=0, concat_axis=0, tiled...  7.41 us
  transfers between devices with their start and end apart: 15, of which 8 were waited for; matrix products, arithmetic and copies ran while one was open for 2% of the time, Pallas kernels for 27%

profile of v4, /device:TPU:0, one launch (start us, length us, event | category | flops | bytes accessed | tf_op | source)
XLA Modules:
  0.0 178.4 jit_solution(4558864152759276420)
XLA Ops:
  6.1 5.7 %shard_map.121 = (f32[2560,128]{1,0:T(8,128)S(1)}, s32[256]{0:T(256)S(1)}) custom-call(s32[256]{0:T(256)S(1)} %bitcast.15, f32[64,128]{1,0:T(8,128)S(1)} %reshape.38.table, s32[256,128]{1,0:T(8,128)S(1)} %copy-done.17, s32[256,128]{1,0:T(8,128)S(1)} %copy-done.16, f32[256,128]{1,0:T(8,128)S(1)} %copy-done.19), custom_call_target="tpu_custom_call" | custom-call | flops 1000000000 | bytes 4000000 | tf_op jit(solution)/shard_map/pallas_call | solution.py:645
  12.8 7.4 %all-to-all-start = ((f32[32,80,128]{2,1,0:T(8,128)}), f32[32,80,128]{2,1,0:T(8,128)}, u32[]{:S(2)}, u32[]{:S(2)}) async-start(f32[32,80,128]{2,1,0:T(8,128)} %bitcast.9), calls=%async_computation | async-start | bytes 2621440 | tf_op jit(solution)/shard_map/all_to_all | solution.py:667
  20.3 1.3 copy-done.2
  21.6 1.3 copy-done.4
  22.9 2.2 %shard_map.123 = (f32[2,32,128]{2,1,0:T(8,128)S(1)}, f32[2,32,128]{2,1,0:T(8,128)S(1)}, f32[21,8,512]{2,1,0:T(8,128)}, f32[21,8,512]{2,1,0:T(8,128)}) custom-call(s32[256]{0:T(256)S(1)} %get-tuple-element.21.home, f32[20,32,512]{2,1,0:T(8,128)S(1)} %copy-done, f32[20,32,512]{2,1,0:T(8,128)S(1)} %copy-done.1, f32[20,32,512]{2,1,0:T(8,128)S(1)} %copy-done.2, ...), custom_call_target="tpu_custom_call" | custom-call | flops 10000000 | bytes 4000000 | tf_op jit(solution)/shard_map/pallas_call | solution.py:671
  25.2 1.5 collective-permute-start.4
  26.6 3.4 %collective-permute-start.3 = (f32[21,8,512]{2,1,0:T(8,128)}, f32[21,8,512]{2,1,0:T(8,128)S(1)}, u32[]{:S(2)}, u32[]{:S(2)}) collective-permute-start(f32[21,8,512]{2,1,0:T(8,128)} %get-tuple-element.25), channel_id=1, source_target_pairs={{0,1},{1,2},{2,3},{3,4},{4,5},{5,6},{6,7},{8,9},{9,10},{10,11},{11... | collective-permute-start | bytes 1032200 | tf_op jit(solution)/shard_map/ppermute | solution.py:585
  32.4 10.5 %collective-permute-done.from_east = f32[2,32,128]{2,1,0:T(8,128)S(1)} collective-permute-done((f32[2,32,128]{2,1,0:T(8,128)S(1)}, f32[2,32,128]{2,1,0:T(8,128)S(1)}, u32[]{:S(2)}, u32[]{:S(2)}) %collective-permute-start) | collective-permute-done | bytes 32800 | tf_op jit(solution)/shard_map/ppermute | solution.py:584
  42.9 1.4 collective-permute-done.1.from_west
  44.9 9.7 %all-to-all-done = f32[32,80,128]{2,1,0:T(8,128)} async-done(((f32[32,80,128]{2,1,0:T(8,128)}), f32[32,80,128]{2,1,0:T(8,128)}, u32[]{:S(2)}, u32[]{:S(2)}) %all-to-all-start) | async-done | bytes 1310752 | tf_op jit(solution)/shard_map/all_to_all | solution.py:667
  54.6 1.6 convert_reduce_fusion.counts
  56.3 22.0 %shard_map.122 = (f32[128,512]{1,0:T(8,128)S(1)}, f32[528,128]{1,0:T(8,128)S(1)}, s32[529]{0:T(1024)S(1)}) custom-call(s32[32]{0:T(128)S(1)} %convert_reduce_fusion.counts, f32[2560,128]{1,0:T(8,128)} %bitcast.3.arrived), custom_call_target="tpu_custom_call" | custom-call | flops 20000000000 | bytes 4000000 | tf_op jit(solution)/shard_map/pallas_call | solution.py:690
  78.9 1.7 collective-permute-start.8
  80.7 1.9 %collective-permute-done.9 = f32[4,32,128]{2,1,0:T(8,128)S(1)} collective-permute-done((f32[4,32,128]{2,1,0:T(8,128)S(1)}, f32[4,32,128]{2,1,0:T(8,128)S(1)}, u32[]{:S(2)}, u32[]{:S(2)}) %collective-permute-start.9) | collective-permute-done | bytes 65568 | tf_op jit(solution)/shard_map/ppermute | solution.py:605
  85.0 3.2 %collective-permute-done.5.corner_n = f32[4,8,128]{2,1,0:T(8,128)S(1)} collective-permute-done((f32[4,8,128]{2,1,0:T(8,128)S(1)}, f32[4,8,128]{2,1,0:T(8,128)S(1)}, u32[]{:S(2)}, u32[]{:S(2)}) %collective-permute-start.5) | collective-permute-done | bytes 16416 | tf_op jit(solution)/shard_map/ppermute | solution.py:596
  88.2 1.6 collective-permute-start.6
  92.7 5.1 %collective-permute-start.11 = (f32[4,8,640]{2,1,0:T(8,128)}, f32[4,8,640]{2,1,0:T(8,128)}, u32[]{:S(2)}, u32[]{:S(2)}) collective-permute-start(f32[4,8,640]{2,1,0:T(8,128)} %pad_maximum_fusion.1), channel_id=1, source_target_pairs={{0,1},{1,2},{2,3},{3,4},{4,5},{5,6},{6,7},{8,9},{9,10},{10,11},{11... | collective-permute-start | bytes 245768 | tf_op jit(solution)/shard_map/ppermute | solution.py:615
  97.9 2.2 %collective-permute-done.11.from_south = f32[4,8,640]{2,1,0:T(8,128)} collective-permute-done((f32[4,8,640]{2,1,0:T(8,128)}, f32[4,8,640]{2,1,0:T(8,128)}, u32[]{:S(2)}, u32[]{:S(2)}) %collective-permute-start.11) | collective-permute-done | bytes 81952 | tf_op jit(solution)/shard_map/ppermute | solution.py:615
  101.0 4.8 %shard_map.124 = (f32[2,32,512]{2,1,0:T(8,128)S(1)}, f32[2,32,512]{2,1,0:T(8,128)S(1)}, f32[4,32,512]{2,1,0:T(8,128)S(1)}) custom-call(s32[1]{0:T(128)} %bitcast.4.top, f32[20,32,512]{2,1,0:T(8,128)S(1)} %copy-done, f32[20,32,512]{2,1,0:T(8,128)S(1)} %copy-done.1, f32[20,32,512]{2,1,0:T(8,128)} %east.5, f32[20,32,512]{2,1,0:T(8,128)} %north.5, ...), custom_call_target="tpu_custom_call" | custom-call | flops 100000000 | bytes 4000000 | tf_op jit(solution)/shard_map/pallas_call | solution.py:715
  107.1 18.8 %shard_map.125 = f32[2048,128]{1,0:T(8,128)S(1)} custom-call(s32[529]{0:T(1024)S(1)} %copy-done.25, f32[128,512]{1,0:T(8,128)S(1)} %bitcast.14, f32[528,128]{1,0:T(8,128)S(1)} %copy-done.23), custom_call_target="tpu_custom_call" | custom-call | flops 20000000000 | bytes 4000000 | tf_op jit(solution)/shard_map/pallas_call | solution.py:736
  126.9 14.9 %all-to-all-start.1 = ((f32[32,64,128]{2,1,0:T(8,128)}), f32[32,64,128]{2,1,0:T(8,128)}, u32[]{:S(2)}, u32[]{:S(2)}) async-start(f32[32,64,128]{2,1,0:T(8,128)} %bitcast.13), calls=%async_computation.1 | async-start | bytes 2097152 | tf_op jit(solution)/shard_map/all_to_all | solution.py:749
  141.8 1.3 copy-done.3
  144.9 23.5 %shard_map.126 = (f32[20,32,512]{2,1,0:T(8,128)}, f32[20,32,512]{2,1,0:T(8,128)}) custom-call(s32[1]{0:T(128)} %bitcast.4.top, f32[20,32,512]{2,1,0:T(8,128)S(1)} %copy-done, f32[20,32,512]{2,1,0:T(8,128)S(1)} %copy-done.1, f32[20,32,512]{2,1,0:T(8,128)S(1)} %copy-done.3, f32[20,32,512]{2,1,0:T(8,128)} %north.5, s32[32,512]{1,0:T(8,128)S(1)} %copy-done.9, ...), custom_call_target="tpu_custom_call" | custom-call | flops 1000000000 | bytes 4000000 | tf_op jit(solution)/shard_map/pallas_call | solution.py:750
  171.2 6.6 %shard_map.127 = f32[64,128]{1,0:T(8,128)S(1)} custom-call(s32[256]{0:T(256)S(1)} %copy-done.15, f32[2048,128]{1,0:T(8,128)} %bitcast.8.returned, s32[256,128]{1,0:T(8,128)S(1)} %copy-done.18, f32[256,128]{1,0:T(8,128)S(1)} %copy-done.20), custom_call_target="tpu_custom_call" | custom-call | flops 2000000000 | bytes 4000000 | tf_op jit(solution)/shard_map/pallas_call | solution.py:768
  (84 shorter events, 23.7 us)
Async XLA Ops:
  6.1 14.2 %copy-start.9 = (s32[32,512]{1,0:T(8,128)S(1)}, s32[32,512]{1,0:T(8,128)}, u32[]{:S(2)}) copy-start(s32[32,512]{1,0:T(8,128)} %ocean_mask.5) | copy-start | bytes 196612
  12.8 7.4 %copy-start.14 = (s32[256]{0:T(256)}, s32[256]{0:T(256)S(1)}, u32[]{:S(2)}) copy-start(s32[256]{0:T(256)S(1)} %get-tuple-element.21.home) | copy-start | bytes 3076
  12.8 7.4 %copy-start = (f32[20,32,512]{2,1,0:T(8,128)S(1)}, f32[20,32,512]{2,1,0:T(8,128)}, u32[]{:S(2)}) copy-start(f32[20,32,512]{2,1,0:T(8,128)} %temper.5) | copy-start | bytes 3932164
  12.8 7.4 %copy-start.1 = (f32[20,32,512]{2,1,0:T(8,128)S(1)}, f32[20,32,512]{2,1,0:T(8,128)}, u32[]{:S(2)}) copy-start(f32[20,32,512]{2,1,0:T(8,128)} %saline.5) | copy-start | bytes 3932164
  12.8 41.8 %all-to-all-start = ((f32[32,80,128]{2,1,0:T(8,128)}), f32[32,80,128]{2,1,0:T(8,128)}, u32[]{:S(2)}, u32[]{:S(2)}) async-start(f32[32,80,128]{2,1,0:T(8,128)} %bitcast.9), calls=%async_computation | async-start | bytes 2621440 | tf_op jit(solution)/shard_map/all_to_all | solution.py:667
  25.2 72.7 %collective-permute-start.4 = (f32[21,8,512]{2,1,0:T(8,128)}, f32[21,8,512]{2,1,0:T(8,128)S(1)}, u32[]{:S(2)}, u32[]{:S(2)}) collective-permute-start(f32[21,8,512]{2,1,0:T(8,128)} %get-tuple-element.25), channel_id=1, source_target_pairs={{0,24},{8,16},{16,8},{24,0},{1,25},{9,17},{17,9},{25,1},{2,26},{10... | collective-permute-start | bytes 1032200 | tf_op jit(solution)/shard_map/ppermute | solution.py:587
  26.6 71.2 %collective-permute-start.3 = (f32[21,8,512]{2,1,0:T(8,128)}, f32[21,8,512]{2,1,0:T(8,128)S(1)}, u32[]{:S(2)}, u32[]{:S(2)}) collective-permute-start(f32[21,8,512]{2,1,0:T(8,128)} %get-tuple-element.25), channel_id=1, source_target_pairs={{0,1},{1,2},{2,3},{3,4},{4,5},{5,6},{6,7},{8,9},{9,10},{10,11},{11... | collective-permute-start | bytes 1032200 | tf_op jit(solution)/shard_map/ppermute | solution.py:585
  30.0 12.9 %collective-permute-start = (f32[2,32,128]{2,1,0:T(8,128)S(1)}, f32[2,32,128]{2,1,0:T(8,128)S(1)}, u32[]{:S(2)}, u32[]{:S(2)}) collective-permute-start(f32[2,32,128]{2,1,0:T(8,128)S(1)} %get-tuple-element.22), channel_id=1, source_target_pairs={{8,0},{16,8},{24,16},{0,24},{9,1},{17,9},{25,17},{1,25},{10,2},{18... | collective-permute-start | bytes 98312 | tf_op jit(solution)/shard_map/ppermute | solution.py:584
  30.3 14.0 %collective-permute-start.1 = (f32[2,32,128]{2,1,0:T(8,128)S(1)}, f32[2,32,128]{2,1,0:T(8,128)S(1)}, u32[]{:S(2)}, u32[]{:S(2)}) collective-permute-start(f32[2,32,128]{2,1,0:T(8,128)S(1)} %get-tuple-element.23), channel_id=1, source_target_pairs={{0,8},{8,16},{16,24},{24,0},{1,9},{9,17},{17,25},{25,1},{2,10},{10... | collective-permute-start | bytes 98312 | tf_op jit(solution)/shard_map/ppermute | solution.py:583
  30.6 62.1 %collective-permute-start.2 = (f32[21,8,512]{2,1,0:T(8,128)}, f32[21,8,512]{2,1,0:T(8,128)}, u32[]{:S(2)}, u32[]{:S(2)}) collective-permute-start(f32[21,8,512]{2,1,0:T(8,128)} %get-tuple-element.24), channel_id=1, source_target_pairs={{1,0},{2,1},{3,2},{4,3},{5,4},{6,5},{7,6},{9,8},{10,9},{11,10},{12... | collective-permute-start | bytes 1032200 | tf_op jit(solution)/shard_map/ppermute | solution.py:586
  56.3 28.1 %copy-start.26 = (pred[128]{0:T(512)(128)(4,1)S(1)}, pred[128]{0:T(512)(128)(4,1)}, u32[]{:S(2)}) copy-start(pred[128]{0:T(512)(128)(4,1)} %iota_compare_fusion) | copy-start | bytes 388
  78.9 12.9 %copy-start.22 = (f32[528,128]{1,0:T(8,128)}, f32[528,128]{1,0:T(8,128)S(1)}, u32[]{:S(2)}) copy-start(f32[528,128]{1,0:T(8,128)S(1)} %get-tuple-element.28.places) | copy-start | bytes 811012
  78.9 3.7 %collective-permute-start.9 = (f32[4,32,128]{2,1,0:T(8,128)S(1)}, f32[4,32,128]{2,1,0:T(8,128)S(1)}, u32[]{:S(2)}, u32[]{:S(2)}) collective-permute-start(f32[4,32,128]{2,1,0:T(8,128)S(1)} %get-tuple-element.37), channel_id=1, source_target_pairs={{0,8},{8,16},{16,24},{24,0},{1,9},{9,17},{17,25},{25,1},{2,10},{10... | collective-permute-start | bytes 196616 | tf_op jit(solution)/shard_map/ppermute | solution.py:605
  78.9 5.0 %collective-permute-start.8 = (f32[4,32,128]{2,1,0:T(8,128)S(1)}, f32[4,32,128]{2,1,0:T(8,128)S(1)}, u32[]{:S(2)}, u32[]{:S(2)}) collective-permute-start(f32[4,32,128]{2,1,0:T(8,128)S(1)} %get-tuple-element.38), channel_id=1, source_target_pairs={{8,0},{16,8},{24,16},{0,24},{9,1},{17,9},{25,17},{1,25},{10,2},{18... | collective-permute-start | bytes 196616 | tf_op jit(solution)/shard_map/ppermute | solution.py:608
  82.6 5.6 %collective-permute-start.5 = (f32[4,8,128]{2,1,0:T(8,128)S(1)}, f32[4,8,128]{2,1,0:T(8,128)S(1)}, u32[]{:S(2)}, u32[]{:S(2)}) collective-permute-start(f32[4,8,128]{2,1,0:T(8,128)S(1)} %pad_maximum_fusion.3), channel_id=1, source_target_pairs={{1,0},{2,1},{3,2},{4,3},{5,4},{6,5},{7,6},{9,8},{10,9},{11,10},{12... | collective-permute-start | bytes 49160 | tf_op jit(solution)/shard_map/ppermute | solution.py:596
  83.9 6.6 %collective-permute-start.7 = (f32[4,8,128]{2,1,0:T(8,128)}, f32[4,8,128]{2,1,0:T(8,128)S(1)}, u32[]{:S(2)}, u32[]{:S(2)}) collective-permute-start(f32[4,8,128]{2,1,0:T(8,128)} %pad_maximum_fusion.4), channel_id=1, source_target_pairs={{0,24},{8,16},{16,8},{24,0},{1,25},{9,17},{17,9},{25,1},{2,26},{10... | collective-permute-start | bytes 49160 | tf_op jit(solution)/shard_map/ppermute | solution.py:598
  88.2 3.6 %collective-permute-start.6 = (f32[4,8,128]{2,1,0:T(8,128)}, f32[4,8,128]{2,1,0:T(8,128)S(1)}, u32[]{:S(2)}, u32[]{:S(2)}) collective-permute-start(f32[4,8,128]{2,1,0:T(8,128)} %pad_maximum_fusion.4), channel_id=1, source_target_pairs={{0,1},{1,2},{2,3},{3,4},{4,5},{5,6},{6,7},{8,9},{9,10},{10,11},{11... | collective-permute-start | bytes 49160 | tf_op jit(solution)/shard_map/ppermute | solution.py:597
  90.5 7.4 %collective-permute-start.10 = (f32[4,8,640]{2,1,0:T(8,128)}, f32[4,8,640]{2,1,0:T(8,128)}, u32[]{:S(2)}, u32[]{:S(2)}) collective-permute-start(f32[4,8,640]{2,1,0:T(8,128)} %pad_maximum_fusion), channel_id=1, source_target_pairs={{1,0},{2,1},{3,2},{4,3},{5,4},{6,5},{7,6},{9,8},{10,9},{11,10},{12... | collective-permute-start | bytes 245768 | tf_op jit(solution)/shard_map/ppermute | solution.py:616
  91.8 6.1 %collective-permute-start.12 = (f32[4,8,640]{2,1,0:T(8,128)}, f32[4,8,640]{2,1,0:T(8,128)}, u32[]{:S(2)}, u32[]{:S(2)}) collective-permute-start(f32[4,8,640]{2,1,0:T(8,128)} %pad_maximum_fusion.1), channel_id=1, source_target_pairs={{0,24},{8,16},{16,8},{24,0},{1,25},{9,17},{17,9},{25,1},{2,26},{10... | collective-permute-start | bytes 245768 | tf_op jit(solution)/shard_map/ppermute | solution.py:617
  92.7 7.4 %collective-permute-start.11 = (f32[4,8,640]{2,1,0:T(8,128)}, f32[4,8,640]{2,1,0:T(8,128)}, u32[]{:S(2)}, u32[]{:S(2)}) collective-permute-start(f32[4,8,640]{2,1,0:T(8,128)} %pad_maximum_fusion.1), channel_id=1, source_target_pairs={{0,1},{1,2},{2,3},{3,4},{4,5},{5,6},{6,7},{8,9},{9,10},{10,11},{11... | collective-permute-start | bytes 245768 | tf_op jit(solution)/shard_map/ppermute | solution.py:615
  101.0 6.1 %copy-start.23 = (f32[528,128]{1,0:T(8,128)S(1)}, f32[528,128]{1,0:T(8,128)}, u32[]{:S(2)}) copy-start(f32[528,128]{1,0:T(8,128)} %copy-done.22) | copy-start | bytes 811012
  101.0 6.1 %copy-start.25 = (s32[529]{0:T(1024)S(1)}, s32[529]{0:T(1024)}, u32[]{:S(2)}) copy-start(s32[529]{0:T(1024)} %copy-done.24) | copy-start | bytes 6352
  126.9 42.5 %all-to-all-start.1 = ((f32[32,64,128]{2,1,0:T(8,128)}), f32[32,64,128]{2,1,0:T(8,128)}, u32[]{:S(2)}, u32[]{:S(2)}) async-start(f32[32,64,128]{2,1,0:T(8,128)} %bitcast.13), calls=%async_computation.1 | async-start | bytes 2097152 | tf_op jit(solution)/shard_map/all_to_all | solution.py:749
  144.9 24.4 %copy-start.15 = (s32[256]{0:T(256)S(1)}, s32[256]{0:T(256)}, u32[]{:S(2)}) copy-start(s32[256]{0:T(256)} %copy-done.14) | copy-start | bytes 3076
  (18 other events, 17.7 us)

commit v5 on v4

--- a/solution.py
+++ b/solution.py
@@ -34,12 +34,6 @@
         - 0.05 * temper_field * temper_field
         + 0.8 * saline_field
         + 0.03 * temper_field * saline_field
-    )
-
-
-def face_flux(near_cells, far_cells, velocity, open_faces):
-    return open_faces * (
-        velocity * 0.5 * (near_cells + far_cells) - diffuse_rate * (far_cells - near_cells)
     )
 
 
@@ -341,8 +335,16 @@
     )
 
 
+def reversed_tiles(x):
+    back = LANES - 1 - lax.broadcasted_iota(jnp.int32, (x.shape[0], LANES), 1)
+    pieces = [
+        jnp.take_along_axis(x[:, at : at + LANES], back, axis=1, mode="promise_in_bounds")
+        for at in range(0, x.shape[1], LANES)
+    ]
+    return jnp.concatenate(pieces[::-1], axis=1)
+
+
 def mirrored(across, kind):
-    across = turned(across)
     if kind == 2:
         across = -next_column(across)
     last_row, row_before = across[7:8], across[6:7]
@@ -352,12 +354,17 @@
     return jnp.where(upper == 0, last_row, row_before)
 
 
-def fill_channel(target, k, channel, kind, halo, top):
-    from_east, from_west, from_north, from_south, folded, corner_n, corner_s, corner_f = halo
+def turned_corners(corner_f):
+    return [reversed_tiles(corner_f[tile]) for tile in range(corner_f.shape[0])]
+
+
+def fill_channel(target, k, channel, kind, halo, top, turned_rows, turned_ends):
+    from_east, from_west, from_north, from_south, _, corner_n, corner_s, _ = halo
     rows = from_east.shape[1]
     columns = from_north.shape[2]
     tile, group = channel // SIDE_CHANNELS, channel // END_CHANNELS
     spot = EDGE * (channel % END_CHANNELS)
+    at = EDGE * (channel % SIDE_CHANNELS)
     tiles = from_east.shape[0]
     target[k, :rows, columns:] = side_of(channel, from_east[tile], from_west[tile])
 
@@ -371,25 +378,40 @@
         )
 
     upper = lax.broadcasted_iota(jnp.int32, (8, columns + LANES), 0)
+    lane = lax.broadcasted_iota(jnp.int32, (8, LANES), 1)
     above = end_of(from_north, corner_n, -spot)
-    across = mirrored(end_of(folded, corner_f, 8 - EDGE - spot), kind)
+    turned_side = jnp.where(
+        lane < LANES // 2,
+        rolled(turned_ends[tiles + tile], EDGE + at - LANES, 1),
+        rolled(turned_ends[tile], at, 1),
+    )
+    across = mirrored(
+        jnp.concatenate([rolled(turned_rows, 8 - EDGE - spot, 0), turned_side], axis=1), kind
+    )
     above = jnp.where(top[0] == 1, across, above)
     below = end_of(from_south, corner_s, 8 - EDGE - spot)
     target[k, rows:, :] = jnp.where(upper < 4, above, below)
 
 
 def fill_wide(targets, sources, depth, halo, top):
+    turned_ends = turned_corners(halo[7])
     for kind, (target, source) in enumerate(zip(targets, sources)):
         levels, rows, columns = source.shape
         target[:, :rows, :columns] = source[...]
+        turned_rows, group = None, None
         for k in range(levels):
-            fill_channel(target, k, kind * depth + k, kind, halo, top)
+            channel = kind * depth + k
+            if channel // END_CHANNELS != group:
+                group = channel // END_CHANNELS
+                turned_rows = reversed_tiles(halo[4][group])
+            fill_channel(target, k, channel, kind, halo, top, turned_rows, turned_ends)
 
 
 def fill_opens(opens, top, ocean_mask, channel, halo):
     rows, columns = ocean_mask.shape
     opens[0, :rows, :columns] = ocean_mask[...].astype(jnp.float32)
-    fill_channel(opens, 0, channel, 0, halo, top)
+    turned_rows = reversed_tiles(halo[4][channel // END_CHANNELS])
+    fill_channel(opens, 0, channel, 0, halo, top, turned_rows, turned_corners(halo[7]))
     here = opens[0]
     opens[1] = here * next_column(here)
     opens[2] = here * next_row(here)
@@ -404,51 +426,61 @@
     ) * mask
 
 
-def step(source, speeds, opens, first, stop, floor, keep, forcing=None):
+def step(source, speeds, opens, first, stop, floor, keep, forcing=None, shape=None):
     source_t, source_s = source
     east_all, north_all = speeds
+    rows, columns = shape or source_t.shape[1:]
+
+    def kept(x):
+        return x[:rows, :columns]
+
+    def weights(speed, open_faces):
+        return open_faces * (0.5 * speed + diffuse_rate), open_faces * (0.5 * speed - diffuse_rate)
 
     def level(k, carry):
         below = jnp.minimum(k + 1, floor)
-        t, s = source_t[k], source_s[k]
-        t_below, s_below = source_t[below], source_s[below]
-        mask = opens[0]
+        pair = (source_t[k], source_s[k])
+        mask = opens[0, :rows, :columns]
+        t, s = kept(pair[0]), kept(pair[1])
+        t_below, s_below = source_t[below, :rows, :columns], source_s[below, :rows, :columns]
         mixing = mixing_at(t, s, t_below, s_below, mask)
-        east_speed = east_all[k]
-        north_speed = north_all[k] * opens[3]
+        east_near, east_far = weights(east_all[k], opens[1])
+        north_near, north_far = weights(north_all[k] * opens[3], opens[2])
         new_gains = []
-        for turn, (x, x_below) in enumerate(((t, t_below), (s, s_below))):
-            gradient = mixing * (x_below - x)
-            east_flux = face_flux(x, next_column(x), east_speed, opens[1])
-            north_flux = face_flux(x, next_row(x), north_speed, opens[2])
+        for turn, (x, own, x_below) in enumerate(
+            ((pair[0], t, t_below), (pair[1], s, s_below))
+        ):
+            gradient = mixing * (x_below - own)
+            east_flux = east_near * x + east_far * next_column(x)
+            north_flux = north_near * x + north_far * next_row(x)
             change = (
-                -(east_flux - pltpu.roll(east_flux, 1, axis=1))
-                - (north_flux - pltpu.roll(north_flux, 1, axis=0))
+                kept(pltpu.roll(east_flux, 1, axis=1))
+                - kept(east_flux)
+                + kept(pltpu.roll(north_flux, 1, axis=0))
+                - kept(north_flux)
                 + (gradient - carry[turn])
             )
             if forcing is not None:
-                change = change + jnp.where(k == 0, forcing[turn], 0.0)
-            keep(turn, k, x + mask * change)
+                change = change + jnp.where(k == 0, kept(forcing[turn]), 0.0)
+            keep(turn, k, own + mask * change)
             new_gains.append(gradient)
         return tuple(new_gains)
 
     if first == 0:
-        nothing = jnp.zeros(source_t.shape[1:], jnp.float32)
+        nothing = jnp.zeros((rows, columns), jnp.float32)
         gains = (nothing, nothing)
     else:
-        t, s, t_below, s_below = (x[k] for k in (first - 1, first) for x in source)
-        mixing = mixing_at(t, s, t_below, s_below, opens[0])
+        t, s, t_below, s_below = (
+            x[k, :rows, :columns] for k in (first - 1, first) for x in source
+        )
+        mixing = mixing_at(t, s, t_below, s_below, opens[0, :rows, :columns])
         gains = (mixing * (t_below - t), mixing * (s_below - s))
     lax.fori_loop(first, stop, level, gains)
 
 
 def turned(x):
-    back = LANES - 1 - lax.broadcasted_iota(jnp.int32, (x.shape[0], LANES), 1)
-    pieces = [
-        jnp.take_along_axis(x[:, at : at + LANES], back, axis=1, mode="promise_in_bounds")
-        for at in range(0, x.shape[1], LANES)
-    ]
-    return jnp.concatenate(pieces[-2::-1] + pieces[-1:], axis=1)
+    columns = x.shape[1] - LANES
+    return jnp.concatenate([reversed_tiles(x[:, :columns]), reversed_tiles(x[:, columns:])], axis=1)
 
 
 def near_kernel(
@@ -502,7 +534,7 @@
     remap_all[:, :rows, :columns] = remapped[...]
     remap_all[:, :rows, columns:] = remap_sides[...]
     for field in range(4):
-        across = mirrored(folded[field], field)
+        across = mirrored(turned(folded[field]), field)
         above = jnp.where(top[0] == 1, across, from_north[field])
         remap_all[field, rows:, :] = jnp.where(upper < 4, above, from_south[field])
     east_all[0] = east_all[0] + stress_factor * remap_all[2]
@@ -515,11 +547,11 @@
         (second_t, second_s)[target][k] = value
 
     def keep_last(target, k, value):
-        (temper_out, saline_out)[target][k] = value[:rows, :columns]
+        (temper_out, saline_out)[target][k] = value
 
     speeds = (east_all, north_all)
     step((first_t, first_s), speeds, opens, 0, levels - 1, levels - 1, keep_first, forcing)
-    step((second_t, second_s), speeds, opens, 0, levels - 2, levels - 1, keep_last, forcing)
+    step((second_t, second_s), speeds, opens, 0, levels - 2, levels - 1, keep_last, forcing, (rows, columns))
     mask = opens[0, :rows, :columns]
     t, s = temper_out[0], saline_out[0]
     surface[0] = t * mask
@@ -568,23 +600,30 @@
         (second_t, second_s)[target][k] = value
 
     def keep_last(target, k, value):
-        (temper_out, saline_out)[target][k] = value[:rows, :columns]
+        (temper_out, saline_out)[target][k] = value
 
     speeds = (east_all, north_all)
     step((first_t, first_s), speeds, opens, near - 1, depth, depth - 1, keep_first)
-    step((second_t, second_s), speeds, opens, near, depth, depth - 1, keep_last)
+    step((second_t, second_s), speeds, opens, near, depth, depth - 1, keep_last, None, (rows, columns))
+
+
+def across_fold(count_gx, count_gy):
+    return [
+        (i * count_gy + count_gy - 1, (count_gx - 1 - i) * count_gy + count_gy - 1)
+        for i in range(count_gx)
+    ]
 
 
 def edge_halo(first, last, low, high):
     count_gx, count_gy = lax.axis_size("gx"), lax.axis_size("gy")
     north_of = [(i + 1, i) for i in range(count_gy - 1)]
     south_of = [(i, i + 1) for i in range(count_gy - 1)]
-    across = [(i, count_gx - 1 - i) for i in range(count_gx)]
+    across = across_fold(count_gx, count_gy)
     from_west = lax.ppermute(last, "gx", [(i, (i + 1) % count_gx) for i in range(count_gx)])
     from_east = lax.ppermute(first, "gx", [((i + 1) % count_gx, i) for i in range(count_gx)])
     from_south = lax.ppermute(high, "gy", south_of)
     from_north = lax.ppermute(low, "gy", north_of)
-    folded = lax.ppermute(high, "gx", across)
+    folded = lax.ppermute(high, ("gx", "gy"), across)
     corner_low = jnp.concatenate([from_east[:, :8], from_west[:, :8]], axis=0)
     corner_high = jnp.concatenate([from_east[:, -8:], from_west[:, -8:]], axis=0)
     return (
@@ -595,7 +634,7 @@
         folded,
         lax.ppermute(corner_low, "gy", north_of),
         lax.ppermute(corner_high, "gy", south_of),
-        lax.ppermute(corner_high, "gx", across),
+        lax.ppermute(corner_high, ("gx", "gy"), across),
     )
 
 
@@ -614,7 +653,7 @@
     high = jnp.concatenate([x[:, -8:], sides[:, -8:]], axis=2)
     from_south = lax.ppermute(high, "gy", [(i, i + 1) for i in range(count_gy - 1)])
     from_north = lax.ppermute(low, "gy", [(i + 1, i) for i in range(count_gy - 1)])
-    folded = lax.ppermute(high, "gx", [(i, count_gx - 1 - i) for i in range(count_gx)])
+    folded = lax.ppermute(high, ("gx", "gy"), across_fold(count_gx, count_gy))
     return sides, from_north, from_south, folded
 
 

time: 180 us -> 180 us (level)
  Pallas kernels: 83.7 us -> 77.6 us
  waiting for transfers between devices: 29.9 us -> 35.8 us
    ppermute x1, waiting for transfers between devices: 10.5 us -> 0.4 us  [edge_halo(): lax.ppermute(first, 'gx', [((i + 1) % count_gx, i) for i in range(count_g...]
    all_to_all x1, waiting for transfers between devices: 9.75 us -> 19 us  [body(): lax.all_to_all(outgoing, ('gx', 'gy'), split_axis=0, concat_axis=0, tiled...]
    all_to_all x1, waiting for transfers between devices: 0.88 us -> 7.4 us  [body(): lax.all_to_all(picked, ('gx', 'gy'), split_axis=0, concat_axis=0, tiled=T...]
    pallas_call x1, Pallas kernels: 23.5 us -> 17 us  [body(): pl.pallas_call(deep_kernel, out_shape=(cube, cube), in_specs=[SMEM] + [VM...]
    all_to_all x1, starting transfers between devices: 14.9 us -> 11.9 us  [body(): lax.all_to_all(picked, ('gx', 'gy'), split_axis=0, concat_axis=0, tiled=T...]
    ppermute x1, starting transfers between devices: 1.62 us -> 4.14 us  [edge_halo(): lax.ppermute(corner_high, 'gy', south_of)]
  transfers between devices with their start and end apart: 15 -> 15, of which waited for: 8 -> 7; matrix products, arithmetic and copies ran while one was open for 2% -> 2% of each run, Pallas kernels for 27% -> 24%
where the time goes in v5:
time: 180 us; the launch traced here: 178 us
  Pallas kernels  77.6 us (43%)
  starting transfers between devices  41.5 us (23%)
  waiting for transfers between devices  35.8 us (20%)
  local copies, waits for them, and re-layouts  17.4 us (10%)
  other arithmetic  5.21 us (3%)
    pallas_call x1, Pallas kernels, body(): pl.pallas_call(functools.partial(land_kernel, capacity, parallels, meridi...  22.8 us
    pallas_call x1, Pallas kernels, body(): pl.pallas_call(functools.partial(pick_kernel, capacity, parallels, meridi...  19.6 us
    all_to_all x1, waiting for transfers between devices, body(): lax.all_to_all(outgoing, ('gx', 'gy'), split_axis=0, concat_axis=0, tiled...  19 us
    pallas_call x1, Pallas kernels, body(): pl.pallas_call(deep_kernel, out_shape=(cube, cube), in_specs=[SMEM] + [VM...  17 us
    unnamed x54, local copies, waits for them, and re-layouts  15.8 us
    all_to_all x1, starting transfers between devices, body(): lax.all_to_all(picked, ('gx', 'gy'), split_axis=0, concat_axis=0, tiled=T...  11.9 us
    all_to_all x1, starting transfers between devices, body(): lax.all_to_all(outgoing, ('gx', 'gy'), split_axis=0, concat_axis=0, tiled...  7.41 us
    all_to_all x1, waiting for transfers between devices, body(): lax.all_to_all(picked, ('gx', 'gy'), split_axis=0, concat_axis=0, tiled=T...  7.4 us
  transfers between devices with their start and end apart: 15, of which 7 were waited for; matrix products, arithmetic and copies ran while one was open for 2% of the time, Pallas kernels for 24%

profile of v5, /device:TPU:0, one launch (start us, length us, event | category | flops | bytes accessed | tf_op | source)
XLA Modules:
  0.0 178.5 jit_solution(1314736573461825085)
XLA Ops:
  6.1 5.7 %shard_map.121 = (f32[2560,128]{1,0:T(8,128)S(1)}, s32[256]{0:T(256)S(1)}) custom-call(s32[256]{0:T(256)S(1)} %bitcast.15, f32[64,128]{1,0:T(8,128)S(1)} %reshape.38.table, s32[256,128]{1,0:T(8,128)S(1)} %copy-done.17, s32[256,128]{1,0:T(8,128)S(1)} %copy-done.16, f32[256,128]{1,0:T(8,128)S(1)} %copy-done.19), custom_call_target="tpu_custom_call" | custom-call | flops 1000000000 | bytes 4000000 | tf_op jit(solution)/shard_map/pallas_call | solution.py:684
  12.8 7.4 %all-to-all-start = ((f32[32,80,128]{2,1,0:T(8,128)}), f32[32,80,128]{2,1,0:T(8,128)}, u32[]{:S(2)}, u32[]{:S(2)}) async-start(f32[32,80,128]{2,1,0:T(8,128)} %bitcast.9), calls=%async_computation | async-start | bytes 2621440 | tf_op jit(solution)/shard_map/all_to_all | solution.py:706
  20.3 1.3 copy-done.2
  21.6 1.3 copy-done.4
  22.9 2.2 %shard_map.123 = (f32[2,32,128]{2,1,0:T(8,128)S(1)}, f32[2,32,128]{2,1,0:T(8,128)S(1)}, f32[21,8,512]{2,1,0:T(8,128)}, f32[21,8,512]{2,1,0:T(8,128)}) custom-call(s32[256]{0:T(256)S(1)} %get-tuple-element.21.home, f32[20,32,512]{2,1,0:T(8,128)S(1)} %copy-done, f32[20,32,512]{2,1,0:T(8,128)S(1)} %copy-done.1, f32[20,32,512]{2,1,0:T(8,128)S(1)} %copy-done.2, ...), custom_call_target="tpu_custom_call" | custom-call | flops 10000000 | bytes 4000000 | tf_op jit(solution)/shard_map/pallas_call | solution.py:710
  25.8 3.6 %collective-permute-start.3 = (f32[21,8,512]{2,1,0:T(8,128)}, f32[21,8,512]{2,1,0:T(8,128)S(1)}, u32[]{:S(2)}, u32[]{:S(2)}) collective-permute-start(f32[21,8,512]{2,1,0:T(8,128)} %get-tuple-element.25), channel_id=1, source_target_pairs={{0,1},{1,2},{2,3},{3,4},{4,5},{5,6},{6,7},{8,9},{9,10},{10,11},{11... | collective-permute-start | bytes 1032200 | tf_op jit(solution)/shard_map/ppermute | solution.py:624
  32.7 2.3 %collective-permute-done.1.from_west = f32[2,32,128]{2,1,0:T(8,128)S(1)} collective-permute-done((f32[2,32,128]{2,1,0:T(8,128)S(1)}, f32[2,32,128]{2,1,0:T(8,128)S(1)}, u32[]{:S(2)}, u32[]{:S(2)}) %collective-permute-start.1) | collective-permute-done | bytes 32800 | tf_op jit(solution)/shard_map/ppermute | solution.py:622
  35.6 19.0 %all-to-all-done = f32[32,80,128]{2,1,0:T(8,128)} async-done(((f32[32,80,128]{2,1,0:T(8,128)}), f32[32,80,128]{2,1,0:T(8,128)}, u32[]{:S(2)}, u32[]{:S(2)}) %all-to-all-start) | async-done | bytes 1310752 | tf_op jit(solution)/shard_map/all_to_all | solution.py:706
  54.6 1.6 convert_reduce_fusion.counts
  56.3 22.8 %shard_map.122 = (f32[128,512]{1,0:T(8,128)S(1)}, f32[528,128]{1,0:T(8,128)S(1)}, s32[529]{0:T(1024)S(1)}) custom-call(s32[32]{0:T(128)S(1)} %convert_reduce_fusion.counts, f32[2560,128]{1,0:T(8,128)} %bitcast.3.arrived), custom_call_target="tpu_custom_call" | custom-call | flops 20000000000 | bytes 4000000 | tf_op jit(solution)/shard_map/pallas_call | solution.py:729
  79.7 1.7 collective-permute-start.8
  81.5 1.9 %collective-permute-done.9 = f32[4,32,128]{2,1,0:T(8,128)S(1)} collective-permute-done((f32[4,32,128]{2,1,0:T(8,128)S(1)}, f32[4,32,128]{2,1,0:T(8,128)S(1)}, u32[]{:S(2)}, u32[]{:S(2)}) %collective-permute-start.9) | collective-permute-done | bytes 65568 | tf_op jit(solution)/shard_map/ppermute | solution.py:644
  86.1 3.0 %collective-permute-done.5.corner_n = f32[4,8,128]{2,1,0:T(8,128)S(1)} collective-permute-done((f32[4,8,128]{2,1,0:T(8,128)S(1)}, f32[4,8,128]{2,1,0:T(8,128)S(1)}, u32[]{:S(2)}, u32[]{:S(2)}) %collective-permute-start.5) | collective-permute-done | bytes 16416 | tf_op jit(solution)/shard_map/ppermute | solution.py:635
  89.0 4.1 %collective-permute-start.6 = (f32[4,8,128]{2,1,0:T(8,128)}, f32[4,8,128]{2,1,0:T(8,128)S(1)}, u32[]{:S(2)}, u32[]{:S(2)}) collective-permute-start(f32[4,8,128]{2,1,0:T(8,128)} %pad_maximum_fusion.4), channel_id=1, source_target_pairs={{0,1},{1,2},{2,3},{3,4},{4,5},{5,6},{6,7},{8,9},{9,10},{10,11},{11... | collective-permute-start | bytes 49160 | tf_op jit(solution)/shard_map/ppermute | solution.py:636
  95.1 1.3 collective-permute-start.12
  96.4 5.2 %collective-permute-start.11 = (f32[4,8,640]{2,1,0:T(8,128)}, f32[4,8,640]{2,1,0:T(8,128)}, u32[]{:S(2)}, u32[]{:S(2)}) collective-permute-start(f32[4,8,640]{2,1,0:T(8,128)} %pad_maximum_fusion.1), channel_id=1, source_target_pairs={{0,1},{1,2},{2,3},{3,4},{4,5},{5,6},{6,7},{8,9},{9,10},{10,11},{11... | collective-permute-start | bytes 245768 | tf_op jit(solution)/shard_map/ppermute | solution.py:654
  101.6 1.7 collective-permute-done.11.from_south
  104.3 3.7 %shard_map.124 = (f32[2,32,512]{2,1,0:T(8,128)S(1)}, f32[2,32,512]{2,1,0:T(8,128)S(1)}, f32[4,32,512]{2,1,0:T(8,128)S(1)}) custom-call(s32[1]{0:T(128)} %bitcast.4.top, f32[20,32,512]{2,1,0:T(8,128)S(1)} %copy-done, f32[20,32,512]{2,1,0:T(8,128)S(1)} %copy-done.1, f32[20,32,512]{2,1,0:T(8,128)} %east.5, f32[20,32,512]{2,1,0:T(8,128)} %north.5, ...), custom_call_target="tpu_custom_call" | custom-call | flops 100000000 | bytes 4000000 | tf_op jit(solution)/shard_map/pallas_call | solution.py:754
  109.3 19.6 %shard_map.125 = f32[2048,128]{1,0:T(8,128)S(1)} custom-call(s32[529]{0:T(1024)S(1)} %copy-done.25, f32[128,512]{1,0:T(8,128)S(1)} %bitcast.14, f32[528,128]{1,0:T(8,128)S(1)} %copy-done.23), custom_call_target="tpu_custom_call" | custom-call | flops 20000000000 | bytes 4000000 | tf_op jit(solution)/shard_map/pallas_call | solution.py:775
  129.9 11.9 %all-to-all-start.1 = ((f32[32,64,128]{2,1,0:T(8,128)}), f32[32,64,128]{2,1,0:T(8,128)}, u32[]{:S(2)}, u32[]{:S(2)}) async-start(f32[32,64,128]{2,1,0:T(8,128)} %bitcast.13), calls=%async_computation.1 | async-start | bytes 2097152 | tf_op jit(solution)/shard_map/all_to_all | solution.py:788
  141.8 1.3 copy-done.3
  145.0 17.0 %shard_map.126 = (f32[20,32,512]{2,1,0:T(8,128)}, f32[20,32,512]{2,1,0:T(8,128)}) custom-call(s32[1]{0:T(128)} %bitcast.4.top, f32[20,32,512]{2,1,0:T(8,128)S(1)} %copy-done, f32[20,32,512]{2,1,0:T(8,128)S(1)} %copy-done.1, f32[20,32,512]{2,1,0:T(8,128)S(1)} %copy-done.3, f32[20,32,512]{2,1,0:T(8,128)} %north.5, s32[32,512]{1,0:T(8,128)S(1)} %copy-done.9, ...), custom_call_target="tpu_custom_call" | custom-call | flops 1000000000 | bytes 4000000 | tf_op jit(solution)/shard_map/pallas_call | solution.py:789
  162.0 7.4 %all-to-all-done.1 = f32[32,64,128]{2,1,0:T(8,128)} async-done(((f32[32,64,128]{2,1,0:T(8,128)}), f32[32,64,128]{2,1,0:T(8,128)}, u32[]{:S(2)}, u32[]{:S(2)}) %all-to-all-start.1) | async-done | bytes 1048608 | tf_op jit(solution)/shard_map/all_to_all | solution.py:788
  171.2 6.6 %shard_map.127 = f32[64,128]{1,0:T(8,128)S(1)} custom-call(s32[256]{0:T(256)S(1)} %copy-done.15, f32[2048,128]{1,0:T(8,128)} %bitcast.8.returned, s32[256,128]{1,0:T(8,128)S(1)} %copy-done.18, f32[256,128]{1,0:T(8,128)S(1)} %copy-done.20), custom_call_target="tpu_custom_call" | custom-call | flops 2000000000 | bytes 4000000 | tf_op jit(solution)/shard_map/pallas_call | solution.py:807
  (84 shorter events, 23.7 us)
Async XLA Ops:
  6.1 14.2 %copy-start.9 = (s32[32,512]{1,0:T(8,128)S(1)}, s32[32,512]{1,0:T(8,128)}, u32[]{:S(2)}) copy-start(s32[32,512]{1,0:T(8,128)} %ocean_mask.5) | copy-start | bytes 196612
  12.8 7.4 %copy-start.14 = (s32[256]{0:T(256)}, s32[256]{0:T(256)S(1)}, u32[]{:S(2)}) copy-start(s32[256]{0:T(256)S(1)} %get-tuple-element.21.home) | copy-start | bytes 3076
  12.8 7.4 %copy-start = (f32[20,32,512]{2,1,0:T(8,128)S(1)}, f32[20,32,512]{2,1,0:T(8,128)}, u32[]{:S(2)}) copy-start(f32[20,32,512]{2,1,0:T(8,128)} %temper.5) | copy-start | bytes 3932164
  12.8 7.5 %copy-start.1 = (f32[20,32,512]{2,1,0:T(8,128)S(1)}, f32[20,32,512]{2,1,0:T(8,128)}, u32[]{:S(2)}) copy-start(f32[20,32,512]{2,1,0:T(8,128)} %saline.5) | copy-start | bytes 3932164
  12.8 41.8 %all-to-all-start = ((f32[32,80,128]{2,1,0:T(8,128)}), f32[32,80,128]{2,1,0:T(8,128)}, u32[]{:S(2)}, u32[]{:S(2)}) async-start(f32[32,80,128]{2,1,0:T(8,128)} %bitcast.9), calls=%async_computation | async-start | bytes 2621440 | tf_op jit(solution)/shard_map/all_to_all | solution.py:706
  25.2 76.5 %collective-permute-start.4 = (f32[21,8,512]{2,1,0:T(8,128)}, f32[21,8,512]{2,1,0:T(8,128)S(1)}, u32[]{:S(2)}, u32[]{:S(2)}) collective-permute-start(f32[21,8,512]{2,1,0:T(8,128)} %get-tuple-element.25), channel_id=1, source_target_pairs={{7,31},{15,23},{23,15},{31,7}} | collective-permute-start | bytes 1032200 | tf_op jit(solution)/shard_map/ppermute | solution.py:626
  25.8 75.8 %collective-permute-start.3 = (f32[21,8,512]{2,1,0:T(8,128)}, f32[21,8,512]{2,1,0:T(8,128)S(1)}, u32[]{:S(2)}, u32[]{:S(2)}) collective-permute-start(f32[21,8,512]{2,1,0:T(8,128)} %get-tuple-element.25), channel_id=1, source_target_pairs={{0,1},{1,2},{2,3},{3,4},{4,5},{5,6},{6,7},{8,9},{9,10},{10,11},{11... | collective-permute-start | bytes 1032200 | tf_op jit(solution)/shard_map/ppermute | solution.py:624
  29.5 3.3 %collective-permute-start = (f32[2,32,128]{2,1,0:T(8,128)S(1)}, f32[2,32,128]{2,1,0:T(8,128)S(1)}, u32[]{:S(2)}, u32[]{:S(2)}) collective-permute-start(f32[2,32,128]{2,1,0:T(8,128)S(1)} %get-tuple-element.22), channel_id=1, source_target_pairs={{8,0},{16,8},{24,16},{0,24},{9,1},{17,9},{25,17},{1,25},{10,2},{18... | collective-permute-start | bytes 98312 | tf_op jit(solution)/shard_map/ppermute | solution.py:623
  30.5 4.5 %collective-permute-start.1 = (f32[2,32,128]{2,1,0:T(8,128)S(1)}, f32[2,32,128]{2,1,0:T(8,128)S(1)}, u32[]{:S(2)}, u32[]{:S(2)}) collective-permute-start(f32[2,32,128]{2,1,0:T(8,128)S(1)} %get-tuple-element.23), channel_id=1, source_target_pairs={{0,8},{8,16},{16,24},{24,0},{1,9},{9,17},{17,25},{25,1},{2,10},{10... | collective-permute-start | bytes 98312 | tf_op jit(solution)/shard_map/ppermute | solution.py:622
  30.5 66.0 %collective-permute-start.2 = (f32[21,8,512]{2,1,0:T(8,128)}, f32[21,8,512]{2,1,0:T(8,128)}, u32[]{:S(2)}, u32[]{:S(2)}) collective-permute-start(f32[21,8,512]{2,1,0:T(8,128)} %get-tuple-element.24), channel_id=1, source_target_pairs={{1,0},{2,1},{3,2},{4,3},{5,4},{6,5},{7,6},{9,8},{10,9},{11,10},{12... | collective-permute-start | bytes 1032200 | tf_op jit(solution)/shard_map/ppermute | solution.py:625
  56.3 29.1 %copy-start.26 = (pred[128]{0:T(512)(128)(4,1)S(1)}, pred[128]{0:T(512)(128)(4,1)}, u32[]{:S(2)}) copy-start(pred[128]{0:T(512)(128)(4,1)} %iota_compare_fusion) | copy-start | bytes 388
  79.7 15.5 %copy-start.22 = (f32[528,128]{1,0:T(8,128)}, f32[528,128]{1,0:T(8,128)S(1)}, u32[]{:S(2)}) copy-start(f32[528,128]{1,0:T(8,128)S(1)} %get-tuple-element.28.places) | copy-start | bytes 811012
  79.7 3.7 %collective-permute-start.9 = (f32[4,32,128]{2,1,0:T(8,128)S(1)}, f32[4,32,128]{2,1,0:T(8,128)S(1)}, u32[]{:S(2)}, u32[]{:S(2)}) collective-permute-start(f32[4,32,128]{2,1,0:T(8,128)S(1)} %get-tuple-element.37), channel_id=1, source_target_pairs={{0,8},{8,16},{16,24},{24,0},{1,9},{9,17},{17,25},{25,1},{2,10},{10... | collective-permute-start | bytes 196616 | tf_op jit(solution)/shard_map/ppermute | solution.py:644
  79.7 5.0 %collective-permute-start.8 = (f32[4,32,128]{2,1,0:T(8,128)S(1)}, f32[4,32,128]{2,1,0:T(8,128)S(1)}, u32[]{:S(2)}, u32[]{:S(2)}) collective-permute-start(f32[4,32,128]{2,1,0:T(8,128)S(1)} %get-tuple-element.38), channel_id=1, source_target_pairs={{8,0},{16,8},{24,16},{0,24},{9,1},{17,9},{25,17},{1,25},{10,2},{18... | collective-permute-start | bytes 196616 | tf_op jit(solution)/shard_map/ppermute | solution.py:647
  83.4 5.6 %collective-permute-start.5 = (f32[4,8,128]{2,1,0:T(8,128)S(1)}, f32[4,8,128]{2,1,0:T(8,128)S(1)}, u32[]{:S(2)}, u32[]{:S(2)}) collective-permute-start(f32[4,8,128]{2,1,0:T(8,128)S(1)} %pad_maximum_fusion.3), channel_id=1, source_target_pairs={{1,0},{2,1},{3,2},{4,3},{5,4},{6,5},{7,6},{9,8},{10,9},{11,10},{12... | collective-permute-start | bytes 49160 | tf_op jit(solution)/shard_map/ppermute | solution.py:635
  84.7 9.1 %collective-permute-start.7 = (f32[4,8,128]{2,1,0:T(8,128)}, f32[4,8,128]{2,1,0:T(8,128)S(1)}, u32[]{:S(2)}, u32[]{:S(2)}) collective-permute-start(f32[4,8,128]{2,1,0:T(8,128)} %pad_maximum_fusion.4), channel_id=1, source_target_pairs={{7,31},{15,23},{23,15},{31,7}} | collective-permute-start | bytes 49160 | tf_op jit(solution)/shard_map/ppermute | solution.py:637
  89.0 6.1 %collective-permute-start.6 = (f32[4,8,128]{2,1,0:T(8,128)}, f32[4,8,128]{2,1,0:T(8,128)S(1)}, u32[]{:S(2)}, u32[]{:S(2)}) collective-permute-start(f32[4,8,128]{2,1,0:T(8,128)} %pad_maximum_fusion.4), channel_id=1, source_target_pairs={{0,1},{1,2},{2,3},{3,4},{4,5},{5,6},{6,7},{8,9},{9,10},{10,11},{11... | collective-permute-start | bytes 49160 | tf_op jit(solution)/shard_map/ppermute | solution.py:636
  93.8 7.8 %collective-permute-start.10 = (f32[4,8,640]{2,1,0:T(8,128)}, f32[4,8,640]{2,1,0:T(8,128)}, u32[]{:S(2)}, u32[]{:S(2)}) collective-permute-start(f32[4,8,640]{2,1,0:T(8,128)} %pad_maximum_fusion), channel_id=1, source_target_pairs={{1,0},{2,1},{3,2},{4,3},{5,4},{6,5},{7,6},{9,8},{10,9},{11,10},{12... | collective-permute-start | bytes 245768 | tf_op jit(solution)/shard_map/ppermute | solution.py:655
  95.1 6.5 %collective-permute-start.12 = (f32[4,8,640]{2,1,0:T(8,128)}, f32[4,8,640]{2,1,0:T(8,128)}, u32[]{:S(2)}, u32[]{:S(2)}) collective-permute-start(f32[4,8,640]{2,1,0:T(8,128)} %pad_maximum_fusion.1), channel_id=1, source_target_pairs={{7,31},{15,23},{23,15},{31,7}} | collective-permute-start | bytes 245768 | tf_op jit(solution)/shard_map/ppermute | solution.py:656
  96.4 6.9 %collective-permute-start.11 = (f32[4,8,640]{2,1,0:T(8,128)}, f32[4,8,640]{2,1,0:T(8,128)}, u32[]{:S(2)}, u32[]{:S(2)}) collective-permute-start(f32[4,8,640]{2,1,0:T(8,128)} %pad_maximum_fusion.1), channel_id=1, source_target_pairs={{0,1},{1,2},{2,3},{3,4},{4,5},{5,6},{6,7},{8,9},{9,10},{10,11},{11... | collective-permute-start | bytes 245768 | tf_op jit(solution)/shard_map/ppermute | solution.py:654
  104.3 5.0 %copy-start.23 = (f32[528,128]{1,0:T(8,128)S(1)}, f32[528,128]{1,0:T(8,128)}, u32[]{:S(2)}) copy-start(f32[528,128]{1,0:T(8,128)} %copy-done.22) | copy-start | bytes 811012
  104.3 5.0 %copy-start.25 = (s32[529]{0:T(1024)S(1)}, s32[529]{0:T(1024)}, u32[]{:S(2)}) copy-start(s32[529]{0:T(1024)} %copy-done.24) | copy-start | bytes 6352
  129.9 39.5 %all-to-all-start.1 = ((f32[32,64,128]{2,1,0:T(8,128)}), f32[32,64,128]{2,1,0:T(8,128)}, u32[]{:S(2)}, u32[]{:S(2)}) async-start(f32[32,64,128]{2,1,0:T(8,128)} %bitcast.13), calls=%async_computation.1 | async-start | bytes 2097152 | tf_op jit(solution)/shard_map/all_to_all | solution.py:788
  145.0 24.4 %copy-start.15 = (s32[256]{0:T(256)S(1)}, s32[256]{0:T(256)}, u32[]{:S(2)}) copy-start(s32[256]{0:T(256)} %copy-done.14) | copy-start | bytes 3076
  (18 other events, 17.7 us)

commit v6 on v5

--- a/solution.py
+++ b/solution.py
@@ -78,7 +78,19 @@
 
 
 def send_kernel(
-    capacity, subdomain, table, element, profile, share, out, home, tally, split_table, numbers
+    half,
+    subdomain,
+    table,
+    element,
+    profile,
+    share,
+    early,
+    late,
+    home,
+    tally,
+    split_table,
+    numbers,
+    out,
 ):
     devices = tally.shape[0]
     blocks = element.shape[0]
@@ -116,16 +128,20 @@
                 tile = subdomain[base + b]
                 place = tally[tile]
                 tally[tile] = place + 1
-                home[base + b] = tile * (4 * capacity) + place
-                row = tile * (5 * capacity) + place
+                part = place // half
+                spot = (part * devices + tile) * half
+                home[base + b] = 4 * spot + place - part * half
+                row = 5 * spot + place - part * half
                 for field in range(4):
-                    out[pl.ds(row + field * capacity, 1), :] = (
+                    out[pl.ds(row + field * half, 1), :] = (
                         values[field][:, turn * LANES : (turn + 1) * LANES] * weight[b : b + 1]
                     )
-                out[pl.ds(row + 4 * capacity, 1), :] = address[b : b + 1]
+                out[pl.ds(row + 4 * half, 1), :] = address[b : b + 1]
         return carry
 
     lax.fori_loop(0, blocks // SEND_GROUP, group, 0)
+    early[...] = out[: early.shape[0]]
+    late[...] = out[early.shape[0] :]
 
 
 def gather_kernel_params(flops):
@@ -244,11 +260,13 @@
     out[...] = found_rows[: out.shape[0]]
 
 
-def back_kernel(capacity, home, returned, element, share, out, total, numbers):
+def back_kernel(half, home, early, late, element, share, out, total, numbers, returned):
     blocks = element.shape[0]
     high_rows = out.shape[0] // 4
     total[...] = jnp.zeros(total.shape, jnp.float32)
     number_rows(numbers)
+    returned[: early.shape[0]] = early[...]
+    returned[early.shape[0] :] = late[...]
 
     def group(g, carry):
         base = pl.multiple_of(g * BACK_GROUP, BACK_GROUP)
@@ -261,7 +279,7 @@
         for b in names:
             row = home[base + b]
             split = [
-                two_terms(returned[pl.ds(row + field * capacity, 1), :] * weight[b : b + 1])
+                two_terms(returned[pl.ds(row + field * half, 1), :] * weight[b : b + 1])
                 for field in range(4)
             ]
             terms = [split[field][term] for term in range(2) for field in range(4)]
@@ -274,8 +292,7 @@
         return carry
 
     lax.fori_loop(0, blocks // BACK_GROUP, group, 0)
-    half = 4 * high_rows
-    out[...] = total[:half] + total[half:]
+    out[...] = total[: 4 * high_rows] + total[4 * high_rows :]
 
 
 def next_column(x):
@@ -674,25 +691,29 @@
     atm_cells = air_forcing_quantities.shape[1]
     depth, parallels, meridians = thermal_deviation.shape
     capacity = max(2, 2 * blocks // devices)
-    slot_count = devices * capacity
-    spare = max(LAND_GROUP, PICK_GROUP, capacity)
+    half = -(-capacity // 2)
+    slot_count = devices * half
+    spare = max(LAND_GROUP, PICK_GROUP, half)
     f32 = jnp.float32
     air = air_forcing_quantities
     table = jnp.stack([air[0] + air[1] + air[2] + air[3], air[5] - air[4], air[6], air[7]])
     table = table.reshape(4 * atm_cells // LANES, LANES)
 
-    outgoing, home = pl.pallas_call(
-        functools.partial(send_kernel, capacity),
+    outgoing = jax.ShapeDtypeStruct((slot_count * 5, LANES), f32)
+    early, late, home = pl.pallas_call(
+        functools.partial(send_kernel, half),
         out_shape=(
-            jax.ShapeDtypeStruct((slot_count * 5, LANES), f32),
+            outgoing,
+            outgoing,
             jax.ShapeDtypeStruct((blocks,), jnp.int32),
         ),
         in_specs=[SMEM, VMEM, VMEM, VMEM, VMEM],
-        out_specs=(VMEM, SMEM),
+        out_specs=(VMEM, VMEM, SMEM),
         scratch_shapes=[
             pltpu.SMEM((devices,), jnp.int32),
             pltpu.VMEM((table.shape[0], 2 * LANES), jnp.bfloat16),
             pltpu.VMEM((LANES, LANES), jnp.bfloat16),
+            pltpu.VMEM((slot_count * 10, LANES), f32),
         ],
         **gather_kernel_params(10**9),
     )(
@@ -703,7 +724,10 @@
         overlay_fraction_share,
     )
 
-    arrived = lax.all_to_all(outgoing, ("gx", "gy"), split_axis=0, concat_axis=0, tiled=True)
+    arrivals = [
+        lax.all_to_all(x, ("gx", "gy"), split_axis=0, concat_axis=0, tiled=True)
+        for x in (early, late)
+    ]
     channels = 4 * depth + 1
     packed = jax.ShapeDtypeStruct((-(-channels // SIDE_CHANNELS), parallels, LANES), f32)
     stacked = jax.ShapeDtypeStruct((-(-channels // END_CHANNELS), 8, meridians), f32)
@@ -723,25 +747,30 @@
     )
     halo = edge_halo(*edges)
 
-    counts = jnp.sum(
-        (arrived.reshape(devices, 5, capacity, LANES)[:, 4, :, 0] >= 0).astype(jnp.int32), axis=1
-    )
-    remapped, places, slots = pl.pallas_call(
-        functools.partial(land_kernel, capacity, parallels, meridians),
-        out_shape=(
-            jax.ShapeDtypeStruct((4 * parallels, meridians), f32),
-            jax.ShapeDtypeStruct((slot_count + spare, LANES), f32),
-            jax.ShapeDtypeStruct((slot_count + spare + 1,), jnp.int32),
-        ),
-        in_specs=[SMEM, VMEM],
-        out_specs=(VMEM, VMEM, SMEM),
-        scratch_shapes=[
-            pltpu.VMEM((4, slot_count + spare, LANES), f32),
-            pltpu.VMEM((8 * parallels * (meridians // HALF), HALF), f32),
-            pltpu.VMEM((HALF, LANES), jnp.bfloat16),
-        ],
-        **gather_kernel_params(2 * 10**10),
-    )(counts, arrived)
+    landed = []
+    for arrived in arrivals:
+        counts = jnp.sum(
+            (arrived.reshape(devices, 5, half, LANES)[:, 4, :, 0] >= 0).astype(jnp.int32), axis=1
+        )
+        landed.append(
+            pl.pallas_call(
+                functools.partial(land_kernel, half, parallels, meridians),
+                out_shape=(
+                    jax.ShapeDtypeStruct((4 * parallels, meridians), f32),
+                    jax.ShapeDtypeStruct((slot_count + spare, LANES), f32),
+                    jax.ShapeDtypeStruct((slot_count + spare + 1,), jnp.int32),
+                ),
+                in_specs=[SMEM, VMEM],
+                out_specs=(VMEM, VMEM, SMEM),
+                scratch_shapes=[
+                    pltpu.VMEM((4, slot_count + spare, LANES), f32),
+                    pltpu.VMEM((8 * parallels * (meridians // HALF), HALF), f32),
+                    pltpu.VMEM((HALF, LANES), jnp.bfloat16),
+                ],
+                **gather_kernel_params(10**10),
+            )(counts, arrived)
+        )
+    remapped = landed[0][0] + landed[1][0]
     remapped = remapped.reshape(4, parallels, meridians)
     around = tile_halo(remapped)
 
@@ -772,20 +801,24 @@
         *around,
     )
 
-    picked = pl.pallas_call(
-        functools.partial(pick_kernel, capacity, parallels, meridians),
-        out_shape=jax.ShapeDtypeStruct((slot_count * 4, LANES), f32),
-        in_specs=[SMEM, VMEM, VMEM],
-        out_specs=VMEM,
-        scratch_shapes=[
-            pltpu.VMEM((8 * parallels * (meridians // HALF), HALF), jnp.bfloat16),
-            pltpu.VMEM((HALF, LANES), jnp.bfloat16),
-            pltpu.VMEM(((slot_count + capacity) * 4, LANES), f32),
-        ],
-        **gather_kernel_params(2 * 10**10),
-    )(slots, surface.reshape(4 * parallels, meridians), places)
-    picked, top = lax.optimization_barrier((picked, top))
-    returned = lax.all_to_all(picked, ("gx", "gy"), split_axis=0, concat_axis=0, tiled=True)
+    returns = []
+    for _, places, slots in landed:
+        picked = pl.pallas_call(
+            functools.partial(pick_kernel, half, parallels, meridians),
+            out_shape=jax.ShapeDtypeStruct((slot_count * 4, LANES), f32),
+            in_specs=[SMEM, VMEM, VMEM],
+            out_specs=VMEM,
+            scratch_shapes=[
+                pltpu.VMEM((8 * parallels * (meridians // HALF), HALF), jnp.bfloat16),
+                pltpu.VMEM((HALF, LANES), jnp.bfloat16),
+                pltpu.VMEM(((slot_count + half) * 4, LANES), f32),
+            ],
+            **gather_kernel_params(10**10),
+        )(slots, surface.reshape(4 * parallels, meridians), places)
+        picked, top = lax.optimization_barrier((picked, top))
+        returns.append(
+            lax.all_to_all(picked, ("gx", "gy"), split_axis=0, concat_axis=0, tiled=True)
+        )
     temper, saline = pl.pallas_call(
         deep_kernel,
         out_shape=(cube, cube),
@@ -805,16 +838,17 @@
         saline_near,
     )
     back_fields = pl.pallas_call(
-        functools.partial(back_kernel, capacity),
+        functools.partial(back_kernel, half),
         out_shape=jax.ShapeDtypeStruct((4 * atm_cells // LANES, LANES), f32),
-        in_specs=[SMEM, VMEM, VMEM, VMEM],
+        in_specs=[SMEM, VMEM, VMEM, VMEM, VMEM],
         out_specs=VMEM,
         scratch_shapes=[
             pltpu.VMEM((8 * atm_cells // LANES, LANES), f32),
             pltpu.VMEM((LANES, LANES), jnp.bfloat16),
+            pltpu.VMEM((slot_count * 8, LANES), f32),
         ],
         **gather_kernel_params(2 * 10**9),
-    )(home, returned, overlay_air_element, overlay_fraction_share)
+    )(home, *returns, overlay_air_element, overlay_fraction_share)
     return temper, saline, back_fields.reshape(4, atm_cells)
 
 

time: 180 us -> 194 us (1.078)
  blocking collectives: 0 us -> 26.4 us
  Pallas kernels: 77.6 us -> 63.7 us
  waiting for transfers between devices: 35.8 us -> 29.1 us
  starting transfers between devices: 41.5 us -> 45 us
    all_to_all x0 -> x1, blocking collectives: none -> 26.4 us  [body(): lax.all_to_all(x, ('gx', 'gy'), split_axis=0, concat_axis=0, tiled=True)]
    all_to_all x1, waiting for transfers between devices: 19 us -> 2.59 us  [body(): lax.all_to_all(x, ('gx', 'gy'), split_axis=0, concat_axis=0, tiled=True)]
    pallas_call x4 -> x6, Pallas kernels: 54.7 us -> 40.5 us  [the longest x2 14.3 us: body(): pl.pallas_call(functools.partial(land_kernel, half, parallels, meridians)...]
    all_to_all x1 -> x2, waiting for transfers between devices: 7.4 us -> 13.1 us  [body(): lax.all_to_all(picked, ('gx', 'gy'), split_axis=0, concat_axis=0, tiled=T...]
    ppermute x1, waiting for transfers between devices: 2.98 us -> 7.5 us  [edge_halo(): lax.ppermute(corner_low, 'gy', north_of)]
    all_to_all x1, starting transfers between devices: 7.41 us -> 3.34 us  [body(): lax.all_to_all(x, ('gx', 'gy'), split_axis=0, concat_axis=0, tiled=True)]
    ppermute x1, starting transfers between devices: 1.73 us -> 4.93 us  [tile_halo(): lax.ppermute(x[:, :, :LANES], 'gx', [((i + 1) % count_gx, i) for i in ran...]
    all_to_all x1 -> x2, starting transfers between devices: 11.9 us -> 15.1 us  [body(): lax.all_to_all(picked, ('gx', 'gy'), split_axis=0, concat_axis=0, tiled=T...]
  transfers between devices with their start and end apart: 15 -> 16, of which waited for: 7 -> 7; matrix products, arithmetic and copies ran while one was open for 2% -> 3% of each run, Pallas kernels for 24% -> 19%
where the time goes in v6:
time: 194 us; the launch traced here: 191 us
  Pallas kernels  63.7 us (33%)
  starting transfers between devices  45 us (23%)
  waiting for transfers between devices  29.1 us (15%)
  blocking collectives  26.4 us (14%)
  local copies, waits for them, and re-layouts  18.9 us (10%)
  other arithmetic  6.21 us (3%)
    all_to_all x1, blocking collectives, body(): lax.all_to_all(x, ('gx', 'gy'), split_axis=0, concat_axis=0, tiled=True)  26.4 us
    unnamed x78, local copies, waits for them, and re-layouts  17.4 us
    pallas_call x1, Pallas kernels, body(): pl.pallas_call(deep_kernel, out_shape=(cube, cube), in_specs=[SMEM] + [VM...  17.1 us
    all_to_all x2, starting transfers between devices, body(): lax.all_to_all(picked, ('gx', 'gy'), split_axis=0, concat_axis=0, tiled=T...  15.1 us
    pallas_call x2, Pallas kernels, body(): pl.pallas_call(functools.partial(land_kernel, half, parallels, meridians)...  14.3 us
    all_to_all x2, waiting for transfers between devices, body(): lax.all_to_all(picked, ('gx', 'gy'), split_axis=0, concat_axis=0, tiled=T...  13.1 us
    pallas_call x2, Pallas kernels, body(): pl.pallas_call(functools.partial(pick_kernel, half, parallels, meridians)...  12.7 us
    ppermute x1, waiting for transfers between devices, edge_halo(): lax.ppermute(corner_low, 'gy', north_of)  7.5 us
  transfers between devices with their start and end apart: 16, of which 7 were waited for; matrix products, arithmetic and copies ran while one was open for 3% of the time, Pallas kernels for 19%

profile of v6, /device:TPU:0, one launch (start us, length us, event | category | flops | bytes accessed | tf_op | source)
XLA Modules:
  0.0 190.5 jit_solution(9067428164688601503)
XLA Ops:
  6.1 7.0 %shard_map.121 = (f32[1280,128]{1,0:T(8,128)S(1)}, f32[1280,128]{1,0:T(8,128)}, s32[256]{0:T(256)S(1)}) custom-call(s32[256]{0:T(256)S(1)} %bitcast.23, f32[64,128]{1,0:T(8,128)S(1)} %reshape.50.table, s32[256,128]{1,0:T(8,128)S(1)} %copy-done.26, s32[256,128]{1,0:T(8,128)S(1)} %copy-done.25, f32[256,128]{1,0:T(8,128)S(1)} %copy-done.28), custom_call_target="tpu_custom_call" | custom-call | flops 1000000000 | bytes 4000000 | tf_op jit(solution)/shard_map/pallas_call | solution.py:703
  13.1 26.4 %all_to_all.44 = f32[32,40,128]{2,1,0:T(8,128)} all-to-all(f32[32,40,128]{2,1,0:T(8,128)S(1)} %bitcast.19), channel_id=1, replica_groups=mesh['gx'=4,'gy'=8] {'gx','gy'}, dimensions={0} | all-to-all | bytes 1310720 | tf_op jit(solution)/shard_map/all_to_all | solution.py:728
  39.4 3.3 %all-to-all-start = ((f32[32,40,128]{2,1,0:T(8,128)}), f32[32,40,128]{2,1,0:T(8,128)}, u32[]{:S(2)}, u32[]{:S(2)}) async-start(f32[32,40,128]{2,1,0:T(8,128)} %bitcast.1), calls=%async_computation | async-start | bytes 1310720 | tf_op jit(solution)/shard_map/all_to_all | solution.py:728
  45.5 2.3 %shard_map.123 = (f32[2,32,128]{2,1,0:T(8,128)S(1)}, f32[2,32,128]{2,1,0:T(8,128)S(1)}, f32[21,8,512]{2,1,0:T(8,128)}, f32[21,8,512]{2,1,0:T(8,128)}) custom-call(s32[256]{0:T(256)S(1)} %get-tuple-element.27.home, f32[20,32,512]{2,1,0:T(8,128)S(1)} %copy-done, f32[20,32,512]{2,1,0:T(8,128)S(1)} %copy-done.1, f32[20,32,512]{2,1,0:T(8,128)S(1)} %copy-done.2, ...), custom_call_target="tpu_custom_call" | custom-call | flops 10000000 | bytes 4000000 | tf_op jit(solution)/shard_map/pallas_call | solution.py:734
  48.4 4.2 %collective-permute-start.3 = (f32[21,8,512]{2,1,0:T(8,128)}, f32[21,8,512]{2,1,0:T(8,128)}, u32[]{:S(2)}, u32[]{:S(2)}) collective-permute-start(f32[21,8,512]{2,1,0:T(8,128)} %get-tuple-element.31), channel_id=1, source_target_pairs={{0,1},{1,2},{2,3},{3,4},{4,5},{5,6},{6,7},{8,9},{9,10},{10,11},{11... | collective-permute-start | bytes 1032200 | tf_op jit(solution)/shard_map/ppermute | solution.py:641
  57.8 1.6 convert_reduce_fusion.counts
  59.4 2.6 %all-to-all-done = f32[32,40,128]{2,1,0:T(8,128)} async-done(((f32[32,40,128]{2,1,0:T(8,128)}), f32[32,40,128]{2,1,0:T(8,128)}, u32[]{:S(2)}, u32[]{:S(2)}) %all-to-all-start) | async-done | bytes 655392 | tf_op jit(solution)/shard_map/all_to_all | solution.py:728
  61.9 1.6 convert_reduce_fusion.1.counts
  64.6 11.3 %shard_map.124 = (f32[128,512]{1,0:T(8,128)S(1)}, f32[272,128]{1,0:T(8,128)S(1)}, s32[273]{0:T(512)S(1)}) custom-call(s32[32]{0:T(128)S(1)} %convert_reduce_fusion.counts, f32[1280,128]{1,0:T(8,128)S(1)} %bitcast.18), custom_call_target="tpu_custom_call" | custom-call | flops 10000000000 | bytes 4000000 | tf_op jit(solution)/shard_map/pallas_call | solution.py:756
  75.9 3.0 %shard_map.122 = (f32[128,512]{1,0:T(8,128)S(1)}, f32[272,128]{1,0:T(8,128)S(1)}, s32[273]{0:T(512)S(1)}) custom-call(s32[32]{0:T(128)S(1)} %convert_reduce_fusion.1.counts, f32[1280,128]{1,0:T(8,128)} %bitcast.3.arrived), custom_call_target="tpu_custom_call" | custom-call | flops 10000000000 | bytes 4000000 | tf_op jit(solution)/shard_map/pallas_call | solution.py:756
  79.2 4.9 %collective-permute-start.8 = (f32[4,32,128]{2,1,0:T(8,128)S(1)}, f32[4,32,128]{2,1,0:T(8,128)S(1)}, u32[]{:S(2)}, u32[]{:S(2)}) collective-permute-start(f32[4,32,128]{2,1,0:T(8,128)S(1)} %get-tuple-element.50), channel_id=1, source_target_pairs={{8,0},{16,8},{24,16},{0,24},{9,1},{17,9},{25,17},{1,25},{10,2},{18... | collective-permute-start | bytes 196616 | tf_op jit(solution)/shard_map/ppermute | solution.py:664
  84.1 1.9 %collective-permute-done.9 = f32[4,32,128]{2,1,0:T(8,128)S(1)} collective-permute-done((f32[4,32,128]{2,1,0:T(8,128)S(1)}, f32[4,32,128]{2,1,0:T(8,128)S(1)}, u32[]{:S(2)}, u32[]{:S(2)}) %collective-permute-start.9) | collective-permute-done | bytes 65568 | tf_op jit(solution)/shard_map/ppermute | solution.py:661
  88.7 7.5 %collective-permute-done.5.corner_n = f32[4,8,128]{2,1,0:T(8,128)S(1)} collective-permute-done((f32[4,8,128]{2,1,0:T(8,128)S(1)}, f32[4,8,128]{2,1,0:T(8,128)S(1)}, u32[]{:S(2)}, u32[]{:S(2)}) %collective-permute-start.5) | collective-permute-done | bytes 16416 | tf_op jit(solution)/shard_map/ppermute | solution.py:652
  96.2 4.8 %collective-permute-start.6 = (f32[4,8,128]{2,1,0:T(8,128)}, f32[4,8,128]{2,1,0:T(8,128)S(1)}, u32[]{:S(2)}, u32[]{:S(2)}) collective-permute-start(f32[4,8,128]{2,1,0:T(8,128)} %pad_maximum_fusion.4), channel_id=1, source_target_pairs={{0,1},{1,2},{2,3},{3,4},{4,5},{5,6},{6,7},{8,9},{9,10},{10,11},{11... | collective-permute-start | bytes 49160 | tf_op jit(solution)/shard_map/ppermute | solution.py:653
  104.2 5.2 %collective-permute-start.11 = (f32[4,8,640]{2,1,0:T(8,128)}, f32[4,8,640]{2,1,0:T(8,128)}, u32[]{:S(2)}, u32[]{:S(2)}) collective-permute-start(f32[4,8,640]{2,1,0:T(8,128)} %pad_maximum_fusion.1), channel_id=1, source_target_pairs={{0,1},{1,2},{2,3},{3,4},{4,5},{5,6},{6,7},{8,9},{9,10},{10,11},{11... | collective-permute-start | bytes 245768 | tf_op jit(solution)/shard_map/ppermute | solution.py:671
  109.4 1.7 collective-permute-done.11.from_south
  111.2 3.8 %shard_map.125 = (f32[2,32,512]{2,1,0:T(8,128)S(1)}, f32[2,32,512]{2,1,0:T(8,128)S(1)}, f32[4,32,512]{2,1,0:T(8,128)S(1)}) custom-call(s32[1]{0:T(128)} %bitcast.4.top, f32[20,32,512]{2,1,0:T(8,128)S(1)} %copy-done, f32[20,32,512]{2,1,0:T(8,128)S(1)} %copy-done.1, f32[20,32,512]{2,1,0:T(8,128)} %east.5, f32[20,32,512]{2,1,0:T(8,128)} %north.5, ...), custom_call_target="tpu_custom_call" | custom-call | flops 100000000 | bytes 4000000 | tf_op jit(solution)/shard_map/pallas_call | solution.py:783
  115.1 10.5 %shard_map.127 = f32[1024,128]{1,0:T(8,128)} custom-call(s32[273]{0:T(512)S(1)} %copy-done.38, f32[128,512]{1,0:T(8,128)S(1)} %bitcast.21, f32[272,128]{1,0:T(8,128)S(1)} %copy-done.34), custom_call_target="tpu_custom_call" | custom-call | flops 10000000000 | bytes 4000000 | tf_op jit(solution)/shard_map/pallas_call | solution.py:806
  125.5 12.3 %all-to-all-start.2 = ((f32[32,32,128]{2,1,0:T(8,128)}), f32[32,32,128]{2,1,0:T(8,128)}, u32[]{:S(2)}, u32[]{:S(2)}) async-start(f32[32,32,128]{2,1,0:T(8,128)} %bitcast.10), calls=%async_computation.2 | async-start | bytes 1048576 | tf_op jit(solution)/shard_map/all_to_all | solution.py:820
  138.8 2.2 %shard_map.126 = f32[1024,128]{1,0:T(8,128)} custom-call(s32[273]{0:T(512)S(1)} %copy-done.36, f32[128,512]{1,0:T(8,128)S(1)} %bitcast.22, f32[272,128]{1,0:T(8,128)S(1)} %copy-done.32), custom_call_target="tpu_custom_call" | custom-call | flops 10000000000 | bytes 4000000 | tf_op jit(solution)/shard_map/pallas_call | solution.py:806
  141.0 13.1 %all-to-all-done.2 = f32[32,32,128]{2,1,0:T(8,128)} async-done(((f32[32,32,128]{2,1,0:T(8,128)}), f32[32,32,128]{2,1,0:T(8,128)}, u32[]{:S(2)}, u32[]{:S(2)}) %all-to-all-start.2) | async-done | bytes 524320 | tf_op jit(solution)/shard_map/all_to_all | solution.py:820
  154.2 2.8 %all-to-all-start.3 = ((f32[32,32,128]{2,1,0:T(8,128)}), f32[32,32,128]{2,1,0:T(8,128)S(1)}, u32[]{:S(2)}, u32[]{:S(2)}) async-start(f32[32,32,128]{2,1,0:T(8,128)} %bitcast.12), calls=%async_computation.3 | async-start | bytes 1048576 | tf_op jit(solution)/shard_map/all_to_all | solution.py:820
  163.8 17.1 %shard_map.128 = (f32[20,32,512]{2,1,0:T(8,128)}, f32[20,32,512]{2,1,0:T(8,128)}) custom-call(s32[1]{0:T(128)} %bitcast.4.top, f32[20,32,512]{2,1,0:T(8,128)S(1)} %copy-done, f32[20,32,512]{2,1,0:T(8,128)S(1)} %copy-done.1, f32[20,32,512]{2,1,0:T(8,128)S(1)} %copy-done.3, f32[20,32,512]{2,1,0:T(8,128)} %north.5, s32[32,512]{1,0:T(8,128)S(1)} %copy-done.6, ...), custom_call_target="tpu_custom_call" | custom-call | flops 1000000000 | bytes 4000000 | tf_op jit(solution)/shard_map/pallas_call | solution.py:822
  183.4 6.5 %shard_map.129 = f32[64,128]{1,0:T(8,128)S(1)} custom-call(s32[256]{0:T(256)S(1)} %copy-done.22, f32[1024,128]{1,0:T(8,128)} %bitcast.11.early, f32[1024,128]{1,0:T(8,128)S(1)} %bitcast.20, s32[256,128]{1,0:T(8,128)S(1)} %copy-done.27, f32[256,128]{1,0:T(8,128)S(1)} %copy-done.29), custom_call_target="tpu_custom_call" | custom-call | flops 2000000000 | bytes 4000000 | tf_op jit(solution)/shard_map/pallas_call | solution.py:840
  (115 shorter events, 31.8 us)
Async XLA Ops:
  6.1 36.7 %copy-start.6 = (s32[32,512]{1,0:T(8,128)S(1)}, s32[32,512]{1,0:T(8,128)}, u32[]{:S(2)}) copy-start(s32[32,512]{1,0:T(8,128)} %ocean_mask.5) | copy-start | bytes 196612
  13.0 29.8 %copy-start.21 = (s32[256]{0:T(256)}, s32[256]{0:T(256)S(1)}, u32[]{:S(2)}) copy-start(s32[256]{0:T(256)S(1)} %get-tuple-element.27.home) | copy-start | bytes 3076
  13.0 29.8 %copy-start = (f32[20,32,512]{2,1,0:T(8,128)S(1)}, f32[20,32,512]{2,1,0:T(8,128)}, u32[]{:S(2)}) copy-start(f32[20,32,512]{2,1,0:T(8,128)} %temper.5) | copy-start | bytes 3932164
  13.1 29.8 %copy-start.1 = (f32[20,32,512]{2,1,0:T(8,128)S(1)}, f32[20,32,512]{2,1,0:T(8,128)}, u32[]{:S(2)}) copy-start(f32[20,32,512]{2,1,0:T(8,128)} %saline.5) | copy-start | bytes 3932164
  39.4 22.5 %all-to-all-start = ((f32[32,40,128]{2,1,0:T(8,128)}), f32[32,40,128]{2,1,0:T(8,128)}, u32[]{:S(2)}, u32[]{:S(2)}) async-start(f32[32,40,128]{2,1,0:T(8,128)} %bitcast.1), calls=%async_computation | async-start | bytes 1310720 | tf_op jit(solution)/shard_map/all_to_all | solution.py:728
  47.7 61.7 %collective-permute-start.4 = (f32[21,8,512]{2,1,0:T(8,128)}, f32[21,8,512]{2,1,0:T(8,128)S(1)}, u32[]{:S(2)}, u32[]{:S(2)}) collective-permute-start(f32[21,8,512]{2,1,0:T(8,128)} %get-tuple-element.31), channel_id=1, source_target_pairs={{7,31},{15,23},{23,15},{31,7}} | collective-permute-start | bytes 1032200 | tf_op jit(solution)/shard_map/ppermute | solution.py:643
  48.4 61.0 %collective-permute-start.3 = (f32[21,8,512]{2,1,0:T(8,128)}, f32[21,8,512]{2,1,0:T(8,128)}, u32[]{:S(2)}, u32[]{:S(2)}) collective-permute-start(f32[21,8,512]{2,1,0:T(8,128)} %get-tuple-element.31), channel_id=1, source_target_pairs={{0,1},{1,2},{2,3},{3,4},{4,5},{5,6},{6,7},{8,9},{9,10},{10,11},{11... | collective-permute-start | bytes 1032200 | tf_op jit(solution)/shard_map/ppermute | solution.py:641
  52.6 3.0 %collective-permute-start = (f32[2,32,128]{2,1,0:T(8,128)S(1)}, f32[2,32,128]{2,1,0:T(8,128)S(1)}, u32[]{:S(2)}, u32[]{:S(2)}) collective-permute-start(f32[2,32,128]{2,1,0:T(8,128)S(1)} %get-tuple-element.28), channel_id=1, source_target_pairs={{8,0},{16,8},{24,16},{0,24},{9,1},{17,9},{25,17},{1,25},{10,2},{18... | collective-permute-start | bytes 98312 | tf_op jit(solution)/shard_map/ppermute | solution.py:640
  53.6 3.6 %collective-permute-start.1 = (f32[2,32,128]{2,1,0:T(8,128)S(1)}, f32[2,32,128]{2,1,0:T(8,128)S(1)}, u32[]{:S(2)}, u32[]{:S(2)}) collective-permute-start(f32[2,32,128]{2,1,0:T(8,128)S(1)} %get-tuple-element.29), channel_id=1, source_target_pairs={{0,8},{8,16},{16,24},{24,0},{1,9},{9,17},{17,25},{25,1},{2,10},{10... | collective-permute-start | bytes 98312 | tf_op jit(solution)/shard_map/ppermute | solution.py:639
  53.6 50.6 %collective-permute-start.2 = (f32[21,8,512]{2,1,0:T(8,128)}, f32[21,8,512]{2,1,0:T(8,128)}, u32[]{:S(2)}, u32[]{:S(2)}) collective-permute-start(f32[21,8,512]{2,1,0:T(8,128)} %get-tuple-element.30), channel_id=1, source_target_pairs={{1,0},{2,1},{3,2},{4,3},{5,4},{6,5},{7,6},{9,8},{10,9},{11,10},{12... | collective-permute-start | bytes 1032200 | tf_op jit(solution)/shard_map/ppermute | solution.py:642
  55.7 55.5 %copy-start.7 = (f32[2,32,128]{2,1,0:T(8,128)}, f32[2,32,128]{2,1,0:T(8,128)S(1)}, u32[]{:S(2)}) copy-start(f32[2,32,128]{2,1,0:T(8,128)S(1)} %collective-permute-done.from_east) | copy-start | bytes 98308
  57.2 54.0 %copy-start.9 = (f32[2,32,128]{2,1,0:T(8,128)}, f32[2,32,128]{2,1,0:T(8,128)S(1)}, u32[]{:S(2)}) copy-start(f32[2,32,128]{2,1,0:T(8,128)S(1)} %collective-permute-done.1.from_west) | copy-start | bytes 98308
  79.0 23.9 %copy-start.31 = (f32[272,128]{1,0:T(8,128)}, f32[272,128]{1,0:T(8,128)S(1)}, u32[]{:S(2)}) copy-start(f32[272,128]{1,0:T(8,128)S(1)} %get-tuple-element.36.places) | copy-start | bytes 417796
  79.0 25.2 %copy-start.35 = (s32[273]{0:T(512)}, s32[273]{0:T(512)S(1)}, u32[]{:S(2)}) copy-start(s32[273]{0:T(512)S(1)} %get-tuple-element.26.slots) | copy-start | bytes 3280
  79.1 6.9 %collective-permute-start.9 = (f32[4,32,128]{2,1,0:T(8,128)S(1)}, f32[4,32,128]{2,1,0:T(8,128)S(1)}, u32[]{:S(2)}, u32[]{:S(2)}) collective-permute-start(f32[4,32,128]{2,1,0:T(8,128)S(1)} %get-tuple-element.49), channel_id=1, source_target_pairs={{0,8},{8,16},{16,24},{24,0},{1,9},{9,17},{17,25},{25,1},{2,10},{10... | collective-permute-start | bytes 196616 | tf_op jit(solution)/shard_map/ppermute | solution.py:661
  79.2 8.2 %collective-permute-start.8 = (f32[4,32,128]{2,1,0:T(8,128)S(1)}, f32[4,32,128]{2,1,0:T(8,128)S(1)}, u32[]{:S(2)}, u32[]{:S(2)}) collective-permute-start(f32[4,32,128]{2,1,0:T(8,128)S(1)} %get-tuple-element.50), channel_id=1, source_target_pairs={{8,0},{16,8},{24,16},{0,24},{9,1},{17,9},{25,17},{1,25},{10,2},{18... | collective-permute-start | bytes 196616 | tf_op jit(solution)/shard_map/ppermute | solution.py:664
  86.0 10.1 %collective-permute-start.5 = (f32[4,8,128]{2,1,0:T(8,128)S(1)}, f32[4,8,128]{2,1,0:T(8,128)S(1)}, u32[]{:S(2)}, u32[]{:S(2)}) collective-permute-start(f32[4,8,128]{2,1,0:T(8,128)S(1)} %pad_maximum_fusion.3), channel_id=1, source_target_pairs={{1,0},{2,1},{3,2},{4,3},{5,4},{6,5},{7,6},{9,8},{10,9},{11,10},{12... | collective-permute-start | bytes 49160 | tf_op jit(solution)/shard_map/ppermute | solution.py:652
  87.3 14.3 %collective-permute-start.7 = (f32[4,8,128]{2,1,0:T(8,128)}, f32[4,8,128]{2,1,0:T(8,128)S(1)}, u32[]{:S(2)}, u32[]{:S(2)}) collective-permute-start(f32[4,8,128]{2,1,0:T(8,128)} %pad_maximum_fusion.4), channel_id=1, source_target_pairs={{7,31},{15,23},{23,15},{31,7}} | collective-permute-start | bytes 49160 | tf_op jit(solution)/shard_map/ppermute | solution.py:654
  96.2 6.8 %collective-permute-start.6 = (f32[4,8,128]{2,1,0:T(8,128)}, f32[4,8,128]{2,1,0:T(8,128)S(1)}, u32[]{:S(2)}, u32[]{:S(2)}) collective-permute-start(f32[4,8,128]{2,1,0:T(8,128)} %pad_maximum_fusion.4), channel_id=1, source_target_pairs={{0,1},{1,2},{2,3},{3,4},{4,5},{5,6},{6,7},{8,9},{9,10},{10,11},{11... | collective-permute-start | bytes 49160 | tf_op jit(solution)/shard_map/ppermute | solution.py:653
  101.6 7.8 %collective-permute-start.10 = (f32[4,8,640]{2,1,0:T(8,128)}, f32[4,8,640]{2,1,0:T(8,128)S(1)}, u32[]{:S(2)}, u32[]{:S(2)}) collective-permute-start(f32[4,8,640]{2,1,0:T(8,128)} %pad_maximum_fusion), channel_id=1, source_target_pairs={{1,0},{2,1},{3,2},{4,3},{5,4},{6,5},{7,6},{9,8},{10,9},{11,10},{12... | collective-permute-start | bytes 245768 | tf_op jit(solution)/shard_map/ppermute | solution.py:672
  102.9 6.5 %collective-permute-start.12 = (f32[4,8,640]{2,1,0:T(8,128)}, f32[4,8,640]{2,1,0:T(8,128)}, u32[]{:S(2)}, u32[]{:S(2)}) collective-permute-start(f32[4,8,640]{2,1,0:T(8,128)} %pad_maximum_fusion.1), channel_id=1, source_target_pairs={{7,31},{15,23},{23,15},{31,7}} | collective-permute-start | bytes 245768 | tf_op jit(solution)/shard_map/ppermute | solution.py:673
  104.2 6.9 %collective-permute-start.11 = (f32[4,8,640]{2,1,0:T(8,128)}, f32[4,8,640]{2,1,0:T(8,128)}, u32[]{:S(2)}, u32[]{:S(2)}) collective-permute-start(f32[4,8,640]{2,1,0:T(8,128)} %pad_maximum_fusion.1), channel_id=1, source_target_pairs={{0,1},{1,2},{2,3},{3,4},{4,5},{5,6},{6,7},{8,9},{9,10},{10,11},{11... | collective-permute-start | bytes 245768 | tf_op jit(solution)/shard_map/ppermute | solution.py:671
  125.5 28.6 %all-to-all-start.2 = ((f32[32,32,128]{2,1,0:T(8,128)}), f32[32,32,128]{2,1,0:T(8,128)}, u32[]{:S(2)}, u32[]{:S(2)}) async-start(f32[32,32,128]{2,1,0:T(8,128)} %bitcast.10), calls=%async_computation.2 | async-start | bytes 1048576 | tf_op jit(solution)/shard_map/all_to_all | solution.py:820
  154.2 26.7 %all-to-all-start.3 = ((f32[32,32,128]{2,1,0:T(8,128)}), f32[32,32,128]{2,1,0:T(8,128)S(1)}, u32[]{:S(2)}, u32[]{:S(2)}) async-start(f32[32,32,128]{2,1,0:T(8,128)} %bitcast.12), calls=%async_computation.3 | async-start | bytes 1048576 | tf_op jit(solution)/shard_map/all_to_all | solution.py:820
  (31 other events, 152.7 us)

commit v7 on v5

--- a/solution.py
+++ b/solution.py
@@ -16,8 +16,8 @@
 
 LANES = 128
 SEND_GROUP = 32
-LAND_GROUP = 16
-PICK_GROUP = 16
+LAND_GROUP = 32
+PICK_GROUP = 32
 BACK_GROUP = 32
 HALF = 256
 PAIR = 2

time: 180 us -> 172 us (0.956)
  Pallas kernels: 77.6 us -> 55 us
  starting transfers between devices: 41.5 us -> 57.6 us
    all_to_all x1, starting transfers between devices: 11.9 us -> 24.7 us  [body(): lax.all_to_all(picked, ('gx', 'gy'), split_axis=0, concat_axis=0, tiled=T...]
    pallas_call x1, Pallas kernels: 22.8 us -> 11.1 us  [body(): pl.pallas_call(functools.partial(land_kernel, capacity, parallels, meridi...]
    pallas_call x1, Pallas kernels: 19.6 us -> 8.58 us  [body(): pl.pallas_call(functools.partial(pick_kernel, capacity, parallels, meridi...]
    ppermute x1, starting transfers between devices: 1.73 us -> 6.49 us  [tile_halo(): lax.ppermute(x[:, :, :LANES], 'gx', [((i + 1) % count_gx, i) for i in ran...]
    ppermute x1, starting transfers between devices: 4.14 us -> 1.62 us  [edge_halo(): lax.ppermute(corner_high, 'gy', south_of)]
  transfers between devices with their start and end apart: 15 -> 15, of which waited for: 7 -> 7; matrix products, arithmetic and copies ran while one was open for 2% -> 2% of each run, Pallas kernels for 24% -> 18%
where the time goes in v7:
time: 172 us
  starting transfers between devices  57.6 us (33%)
  Pallas kernels  55 us (32%)
  waiting for transfers between devices  35.8 us (21%)
  local copies, waits for them, and re-layouts  17.4 us (10%)
  other arithmetic  5.21 us (3%)
    all_to_all x1, starting transfers between devices, body(): lax.all_to_all(picked, ('gx', 'gy'), split_axis=0, concat_axis=0, tiled=T...  24.7 us
    all_to_all x1, waiting for transfers between devices, body(): lax.all_to_all(outgoing, ('gx', 'gy'), split_axis=0, concat_axis=0, tiled...  19 us
    pallas_call x1, Pallas kernels, body(): pl.pallas_call(deep_kernel, out_shape=(cube, cube), in_specs=[SMEM] + [VM...  17 us
    unnamed x54, local copies, waits for them, and re-layouts  15.8 us
    pallas_call x1, Pallas kernels, body(): pl.pallas_call(functools.partial(land_kernel, capacity, parallels, meridi...  11.1 us
    pallas_call x1, Pallas kernels, body(): pl.pallas_call(functools.partial(pick_kernel, capacity, parallels, meridi...  8.58 us
    all_to_all x1, starting transfers between devices, body(): lax.all_to_all(outgoing, ('gx', 'gy'), split_axis=0, concat_axis=0, tiled...  7.41 us
    all_to_all x1, waiting for transfers between devices, body(): lax.all_to_all(picked, ('gx', 'gy'), split_axis=0, concat_axis=0, tiled=T...  7.4 us
  transfers between devices with their start and end apart: 15, of which 7 were waited for; matrix products, arithmetic and copies ran while one was open for 2% of the time, Pallas kernels for 18%

profile of v7, /device:TPU:0, one launch (start us, length us, event | category | flops | bytes accessed | tf_op | source)
XLA Modules:
  0.0 171.9 jit_solution(8821686422445492109)
XLA Ops:
  6.1 5.7 %shard_map.121 = (f32[2560,128]{1,0:T(8,128)S(1)}, s32[256]{0:T(256)S(1)}) custom-call(s32[256]{0:T(256)S(1)} %bitcast.15, f32[64,128]{1,0:T(8,128)S(1)} %reshape.38.table, s32[256,128]{1,0:T(8,128)S(1)} %copy-done.17, s32[256,128]{1,0:T(8,128)S(1)} %copy-done.16, f32[256,128]{1,0:T(8,128)S(1)} %copy-done.19), custom_call_target="tpu_custom_call" | custom-call | flops 1000000000 | bytes 4000000 | tf_op jit(solution)/shard_map/pallas_call | solution.py:684
  12.8 7.4 %all-to-all-start = ((f32[32,80,128]{2,1,0:T(8,128)}), f32[32,80,128]{2,1,0:T(8,128)}, u32[]{:S(2)}, u32[]{:S(2)}) async-start(f32[32,80,128]{2,1,0:T(8,128)} %bitcast.9), calls=%async_computation | async-start | bytes 2621440 | tf_op jit(solution)/shard_map/all_to_all | solution.py:706
  20.3 1.3 copy-done.2
  21.6 1.3 copy-done.4
  22.9 2.2 %shard_map.123 = (f32[2,32,128]{2,1,0:T(8,128)S(1)}, f32[2,32,128]{2,1,0:T(8,128)S(1)}, f32[21,8,512]{2,1,0:T(8,128)}, f32[21,8,512]{2,1,0:T(8,128)}) custom-call(s32[256]{0:T(256)S(1)} %get-tuple-element.21.home, f32[20,32,512]{2,1,0:T(8,128)S(1)} %copy-done, f32[20,32,512]{2,1,0:T(8,128)S(1)} %copy-done.1, f32[20,32,512]{2,1,0:T(8,128)S(1)} %copy-done.2, ...), custom_call_target="tpu_custom_call" | custom-call | flops 10000000 | bytes 4000000 | tf_op jit(solution)/shard_map/pallas_call | solution.py:710
  25.8 3.6 %collective-permute-start.3 = (f32[21,8,512]{2,1,0:T(8,128)}, f32[21,8,512]{2,1,0:T(8,128)S(1)}, u32[]{:S(2)}, u32[]{:S(2)}) collective-permute-start(f32[21,8,512]{2,1,0:T(8,128)} %get-tuple-element.25), channel_id=1, source_target_pairs={{0,1},{1,2},{2,3},{3,4},{4,5},{5,6},{6,7},{8,9},{9,10},{10,11},{11... | collective-permute-start | bytes 1032200 | tf_op jit(solution)/shard_map/ppermute | solution.py:624
  32.7 2.3 %collective-permute-done.1.from_west = f32[2,32,128]{2,1,0:T(8,128)S(1)} collective-permute-done((f32[2,32,128]{2,1,0:T(8,128)S(1)}, f32[2,32,128]{2,1,0:T(8,128)S(1)}, u32[]{:S(2)}, u32[]{:S(2)}) %collective-permute-start.1) | collective-permute-done | bytes 32800 | tf_op jit(solution)/shard_map/ppermute | solution.py:622
  35.6 19.0 %all-to-all-done = f32[32,80,128]{2,1,0:T(8,128)} async-done(((f32[32,80,128]{2,1,0:T(8,128)}), f32[32,80,128]{2,1,0:T(8,128)}, u32[]{:S(2)}, u32[]{:S(2)}) %all-to-all-start) | async-done | bytes 1310752 | tf_op jit(solution)/shard_map/all_to_all | solution.py:706
  54.6 1.6 convert_reduce_fusion.counts
  56.3 11.1 %shard_map.122 = (f32[128,512]{1,0:T(8,128)S(1)}, f32[544,128]{1,0:T(8,128)S(1)}, s32[545]{0:T(1024)S(1)}) custom-call(s32[32]{0:T(128)S(1)} %convert_reduce_fusion.counts, f32[2560,128]{1,0:T(8,128)} %bitcast.3.arrived), custom_call_target="tpu_custom_call" | custom-call | flops 20000000000 | bytes 4000000 | tf_op jit(solution)/shard_map/pallas_call | solution.py:729
  69.2 6.5 %collective-permute-start.8 = (f32[4,32,128]{2,1,0:T(8,128)S(1)}, f32[4,32,128]{2,1,0:T(8,128)S(1)}, u32[]{:S(2)}, u32[]{:S(2)}) collective-permute-start(f32[4,32,128]{2,1,0:T(8,128)S(1)} %get-tuple-element.38), channel_id=1, source_target_pairs={{8,0},{16,8},{24,16},{0,24},{9,1},{17,9},{25,17},{1,25},{10,2},{18... | collective-permute-start | bytes 196616 | tf_op jit(solution)/shard_map/ppermute | solution.py:647
  75.7 1.9 %collective-permute-done.9 = f32[4,32,128]{2,1,0:T(8,128)S(1)} collective-permute-done((f32[4,32,128]{2,1,0:T(8,128)S(1)}, f32[4,32,128]{2,1,0:T(8,128)S(1)}, u32[]{:S(2)}, u32[]{:S(2)}) %collective-permute-start.9) | collective-permute-done | bytes 65568 | tf_op jit(solution)/shard_map/ppermute | solution.py:644
  80.2 3.0 %collective-permute-done.5.corner_n = f32[4,8,128]{2,1,0:T(8,128)S(1)} collective-permute-done((f32[4,8,128]{2,1,0:T(8,128)S(1)}, f32[4,8,128]{2,1,0:T(8,128)S(1)}, u32[]{:S(2)}, u32[]{:S(2)}) %collective-permute-start.5) | collective-permute-done | bytes 16416 | tf_op jit(solution)/shard_map/ppermute | solution.py:635
  83.2 1.6 collective-permute-start.6
  86.8 1.3 collective-permute-start.12
  88.1 5.2 %collective-permute-start.11 = (f32[4,8,640]{2,1,0:T(8,128)}, f32[4,8,640]{2,1,0:T(8,128)}, u32[]{:S(2)}, u32[]{:S(2)}) collective-permute-start(f32[4,8,640]{2,1,0:T(8,128)} %pad_maximum_fusion.1), channel_id=1, source_target_pairs={{0,1},{1,2},{2,3},{3,4},{4,5},{5,6},{6,7},{8,9},{9,10},{10,11},{11... | collective-permute-start | bytes 245768 | tf_op jit(solution)/shard_map/ppermute | solution.py:654
  93.3 1.7 collective-permute-done.11.from_south
  95.9 3.7 %shard_map.124 = (f32[2,32,512]{2,1,0:T(8,128)S(1)}, f32[2,32,512]{2,1,0:T(8,128)S(1)}, f32[4,32,512]{2,1,0:T(8,128)S(1)}) custom-call(s32[1]{0:T(128)} %bitcast.4.top, f32[20,32,512]{2,1,0:T(8,128)S(1)} %copy-done, f32[20,32,512]{2,1,0:T(8,128)S(1)} %copy-done.1, f32[20,32,512]{2,1,0:T(8,128)} %east.5, f32[20,32,512]{2,1,0:T(8,128)} %north.5, ...), custom_call_target="tpu_custom_call" | custom-call | flops 100000000 | bytes 4000000 | tf_op jit(solution)/shard_map/pallas_call | solution.py:754
  101.0 8.6 %shard_map.125 = f32[2048,128]{1,0:T(8,128)S(1)} custom-call(s32[545]{0:T(1024)S(1)} %copy-done.25, f32[128,512]{1,0:T(8,128)S(1)} %bitcast.14, f32[544,128]{1,0:T(8,128)S(1)} %copy-done.23), custom_call_target="tpu_custom_call" | custom-call | flops 20000000000 | bytes 4000000 | tf_op jit(solution)/shard_map/pallas_call | solution.py:775
  110.5 24.7 %all-to-all-start.1 = ((f32[32,64,128]{2,1,0:T(8,128)}), f32[32,64,128]{2,1,0:T(8,128)}, u32[]{:S(2)}, u32[]{:S(2)}) async-start(f32[32,64,128]{2,1,0:T(8,128)} %bitcast.13), calls=%async_computation.1 | async-start | bytes 2097152 | tf_op jit(solution)/shard_map/all_to_all | solution.py:788
  135.2 1.3 copy-done.3
  138.3 17.0 %shard_map.126 = (f32[20,32,512]{2,1,0:T(8,128)}, f32[20,32,512]{2,1,0:T(8,128)}) custom-call(s32[1]{0:T(128)} %bitcast.4.top, f32[20,32,512]{2,1,0:T(8,128)S(1)} %copy-done, f32[20,32,512]{2,1,0:T(8,128)S(1)} %copy-done.1, f32[20,32,512]{2,1,0:T(8,128)S(1)} %copy-done.3, f32[20,32,512]{2,1,0:T(8,128)} %north.5, s32[32,512]{1,0:T(8,128)S(1)} %copy-done.9, ...), custom_call_target="tpu_custom_call" | custom-call | flops 1000000000 | bytes 4000000 | tf_op jit(solution)/shard_map/pallas_call | solution.py:789
  155.4 7.4 %all-to-all-done.1 = f32[32,64,128]{2,1,0:T(8,128)} async-done(((f32[32,64,128]{2,1,0:T(8,128)}), f32[32,64,128]{2,1,0:T(8,128)}, u32[]{:S(2)}, u32[]{:S(2)}) %all-to-all-start.1) | async-done | bytes 1048608 | tf_op jit(solution)/shard_map/all_to_all | solution.py:788
  164.6 6.6 %shard_map.127 = f32[64,128]{1,0:T(8,128)S(1)} custom-call(s32[256]{0:T(256)S(1)} %copy-done.15, f32[2048,128]{1,0:T(8,128)} %bitcast.8.returned, s32[256,128]{1,0:T(8,128)S(1)} %copy-done.18, f32[256,128]{1,0:T(8,128)S(1)} %copy-done.20), custom_call_target="tpu_custom_call" | custom-call | flops 2000000000 | bytes 4000000 | tf_op jit(solution)/shard_map/pallas_call | solution.py:807
  (84 shorter events, 24.7 us)
Async XLA Ops:
  6.1 14.2 %copy-start.9 = (s32[32,512]{1,0:T(8,128)S(1)}, s32[32,512]{1,0:T(8,128)}, u32[]{:S(2)}) copy-start(s32[32,512]{1,0:T(8,128)} %ocean_mask.5) | copy-start | bytes 196612
  12.8 7.4 %copy-start.14 = (s32[256]{0:T(256)}, s32[256]{0:T(256)S(1)}, u32[]{:S(2)}) copy-start(s32[256]{0:T(256)S(1)} %get-tuple-element.21.home) | copy-start | bytes 3076
  12.8 7.4 %copy-start = (f32[20,32,512]{2,1,0:T(8,128)S(1)}, f32[20,32,512]{2,1,0:T(8,128)}, u32[]{:S(2)}) copy-start(f32[20,32,512]{2,1,0:T(8,128)} %temper.5) | copy-start | bytes 3932164
  12.8 7.5 %copy-start.1 = (f32[20,32,512]{2,1,0:T(8,128)S(1)}, f32[20,32,512]{2,1,0:T(8,128)}, u32[]{:S(2)}) copy-start(f32[20,32,512]{2,1,0:T(8,128)} %saline.5) | copy-start | bytes 3932164
  12.8 41.8 %all-to-all-start = ((f32[32,80,128]{2,1,0:T(8,128)}), f32[32,80,128]{2,1,0:T(8,128)}, u32[]{:S(2)}, u32[]{:S(2)}) async-start(f32[32,80,128]{2,1,0:T(8,128)} %bitcast.9), calls=%async_computation | async-start | bytes 2621440 | tf_op jit(solution)/shard_map/all_to_all | solution.py:706
  25.2 68.1 %collective-permute-start.4 = (f32[21,8,512]{2,1,0:T(8,128)}, f32[21,8,512]{2,1,0:T(8,128)S(1)}, u32[]{:S(2)}, u32[]{:S(2)}) collective-permute-start(f32[21,8,512]{2,1,0:T(8,128)} %get-tuple-element.25), channel_id=1, source_target_pairs={{7,31},{15,23},{23,15},{31,7}} | collective-permute-start | bytes 1032200 | tf_op jit(solution)/shard_map/ppermute | solution.py:626
  25.8 67.4 %collective-permute-start.3 = (f32[21,8,512]{2,1,0:T(8,128)}, f32[21,8,512]{2,1,0:T(8,128)S(1)}, u32[]{:S(2)}, u32[]{:S(2)}) collective-permute-start(f32[21,8,512]{2,1,0:T(8,128)} %get-tuple-element.25), channel_id=1, source_target_pairs={{0,1},{1,2},{2,3},{3,4},{4,5},{5,6},{6,7},{8,9},{9,10},{10,11},{11... | collective-permute-start | bytes 1032200 | tf_op jit(solution)/shard_map/ppermute | solution.py:624
  29.5 3.3 %collective-permute-start = (f32[2,32,128]{2,1,0:T(8,128)S(1)}, f32[2,32,128]{2,1,0:T(8,128)S(1)}, u32[]{:S(2)}, u32[]{:S(2)}) collective-permute-start(f32[2,32,128]{2,1,0:T(8,128)S(1)} %get-tuple-element.22), channel_id=1, source_target_pairs={{8,0},{16,8},{24,16},{0,24},{9,1},{17,9},{25,17},{1,25},{10,2},{18... | collective-permute-start | bytes 98312 | tf_op jit(solution)/shard_map/ppermute | solution.py:623
  30.5 4.5 %collective-permute-start.1 = (f32[2,32,128]{2,1,0:T(8,128)S(1)}, f32[2,32,128]{2,1,0:T(8,128)S(1)}, u32[]{:S(2)}, u32[]{:S(2)}) collective-permute-start(f32[2,32,128]{2,1,0:T(8,128)S(1)} %get-tuple-element.23), channel_id=1, source_target_pairs={{0,8},{8,16},{16,24},{24,0},{1,9},{9,17},{17,25},{25,1},{2,10},{10... | collective-permute-start | bytes 98312 | tf_op jit(solution)/shard_map/ppermute | solution.py:622
  30.5 57.6 %collective-permute-start.2 = (f32[21,8,512]{2,1,0:T(8,128)}, f32[21,8,512]{2,1,0:T(8,128)}, u32[]{:S(2)}, u32[]{:S(2)}) collective-permute-start(f32[21,8,512]{2,1,0:T(8,128)} %get-tuple-element.24), channel_id=1, source_target_pairs={{1,0},{2,1},{3,2},{4,3},{5,4},{6,5},{7,6},{9,8},{10,9},{11,10},{12... | collective-permute-start | bytes 1032200 | tf_op jit(solution)/shard_map/ppermute | solution.py:625
  56.3 23.3 %copy-start.26 = (pred[128]{0:T(512)(128)(4,1)S(1)}, pred[128]{0:T(512)(128)(4,1)}, u32[]{:S(2)}) copy-start(pred[128]{0:T(512)(128)(4,1)} %iota_compare_fusion) | copy-start | bytes 388
  68.0 7.6 %copy-start.6 = (f32[128,512]{1,0:T(8,128)}, f32[128,512]{1,0:T(8,128)S(1)}, u32[]{:S(2)}) copy-start(f32[128,512]{1,0:T(8,128)S(1)} %get-tuple-element.26) | copy-start | bytes 786436
  68.0 18.8 %copy-start.22 = (f32[544,128]{1,0:T(8,128)}, f32[544,128]{1,0:T(8,128)S(1)}, u32[]{:S(2)}) copy-start(f32[544,128]{1,0:T(8,128)S(1)} %get-tuple-element.28.places) | copy-start | bytes 835588
  68.0 9.6 %collective-permute-start.9 = (f32[4,32,128]{2,1,0:T(8,128)S(1)}, f32[4,32,128]{2,1,0:T(8,128)S(1)}, u32[]{:S(2)}, u32[]{:S(2)}) collective-permute-start(f32[4,32,128]{2,1,0:T(8,128)S(1)} %get-tuple-element.37), channel_id=1, source_target_pairs={{0,8},{8,16},{16,24},{24,0},{1,9},{9,17},{17,25},{25,1},{2,10},{10... | collective-permute-start | bytes 196616 | tf_op jit(solution)/shard_map/ppermute | solution.py:644
  69.2 9.7 %collective-permute-start.8 = (f32[4,32,128]{2,1,0:T(8,128)S(1)}, f32[4,32,128]{2,1,0:T(8,128)S(1)}, u32[]{:S(2)}, u32[]{:S(2)}) collective-permute-start(f32[4,32,128]{2,1,0:T(8,128)S(1)} %get-tuple-element.38), channel_id=1, source_target_pairs={{8,0},{16,8},{24,16},{0,24},{9,1},{17,9},{25,17},{1,25},{10,2},{18... | collective-permute-start | bytes 196616 | tf_op jit(solution)/shard_map/ppermute | solution.py:647
  77.6 5.6 %collective-permute-start.5 = (f32[4,8,128]{2,1,0:T(8,128)S(1)}, f32[4,8,128]{2,1,0:T(8,128)S(1)}, u32[]{:S(2)}, u32[]{:S(2)}) collective-permute-start(f32[4,8,128]{2,1,0:T(8,128)S(1)} %pad_maximum_fusion.3), channel_id=1, source_target_pairs={{1,0},{2,1},{3,2},{4,3},{5,4},{6,5},{7,6},{9,8},{10,9},{11,10},{12... | collective-permute-start | bytes 49160 | tf_op jit(solution)/shard_map/ppermute | solution.py:635
  78.9 6.6 %collective-permute-start.7 = (f32[4,8,128]{2,1,0:T(8,128)}, f32[4,8,128]{2,1,0:T(8,128)S(1)}, u32[]{:S(2)}, u32[]{:S(2)}) collective-permute-start(f32[4,8,128]{2,1,0:T(8,128)} %pad_maximum_fusion.4), channel_id=1, source_target_pairs={{7,31},{15,23},{23,15},{31,7}} | collective-permute-start | bytes 49160 | tf_op jit(solution)/shard_map/ppermute | solution.py:637
  83.2 3.6 %collective-permute-start.6 = (f32[4,8,128]{2,1,0:T(8,128)}, f32[4,8,128]{2,1,0:T(8,128)S(1)}, u32[]{:S(2)}, u32[]{:S(2)}) collective-permute-start(f32[4,8,128]{2,1,0:T(8,128)} %pad_maximum_fusion.4), channel_id=1, source_target_pairs={{0,1},{1,2},{2,3},{3,4},{4,5},{5,6},{6,7},{8,9},{9,10},{10,11},{11... | collective-permute-start | bytes 49160 | tf_op jit(solution)/shard_map/ppermute | solution.py:636
  85.5 7.8 %collective-permute-start.10 = (f32[4,8,640]{2,1,0:T(8,128)}, f32[4,8,640]{2,1,0:T(8,128)}, u32[]{:S(2)}, u32[]{:S(2)}) collective-permute-start(f32[4,8,640]{2,1,0:T(8,128)} %pad_maximum_fusion), channel_id=1, source_target_pairs={{1,0},{2,1},{3,2},{4,3},{5,4},{6,5},{7,6},{9,8},{10,9},{11,10},{12... | collective-permute-start | bytes 245768 | tf_op jit(solution)/shard_map/ppermute | solution.py:655
  86.8 6.5 %collective-permute-start.12 = (f32[4,8,640]{2,1,0:T(8,128)}, f32[4,8,640]{2,1,0:T(8,128)}, u32[]{:S(2)}, u32[]{:S(2)}) collective-permute-start(f32[4,8,640]{2,1,0:T(8,128)} %pad_maximum_fusion.1), channel_id=1, source_target_pairs={{7,31},{15,23},{23,15},{31,7}} | collective-permute-start | bytes 245768 | tf_op jit(solution)/shard_map/ppermute | solution.py:656
  88.1 6.9 %collective-permute-start.11 = (f32[4,8,640]{2,1,0:T(8,128)}, f32[4,8,640]{2,1,0:T(8,128)}, u32[]{:S(2)}, u32[]{:S(2)}) collective-permute-start(f32[4,8,640]{2,1,0:T(8,128)} %pad_maximum_fusion.1), channel_id=1, source_target_pairs={{0,1},{1,2},{2,3},{3,4},{4,5},{5,6},{6,7},{8,9},{9,10},{10,11},{11... | collective-permute-start | bytes 245768 | tf_op jit(solution)/shard_map/ppermute | solution.py:654
  95.9 5.0 %copy-start.25 = (s32[545]{0:T(1024)S(1)}, s32[545]{0:T(1024)}, u32[]{:S(2)}) copy-start(s32[545]{0:T(1024)} %copy-done.24) | copy-start | bytes 6544
  110.5 52.2 %all-to-all-start.1 = ((f32[32,64,128]{2,1,0:T(8,128)}), f32[32,64,128]{2,1,0:T(8,128)}, u32[]{:S(2)}, u32[]{:S(2)}) async-start(f32[32,64,128]{2,1,0:T(8,128)} %bitcast.13), calls=%async_computation.1 | async-start | bytes 2097152 | tf_op jit(solution)/shard_map/all_to_all | solution.py:788
  138.3 24.4 %copy-start.15 = (s32[256]{0:T(256)S(1)}, s32[256]{0:T(256)}, u32[]{:S(2)}) copy-start(s32[256]{0:T(256)} %copy-done.14) | copy-start | bytes 3076
  (18 other events, 20.9 us)
